TPU v7x, 256 devices: a whole 4x4x8 slice. The times are simulated.
256 devices in a mesh: tok: 16 (over y, x), code: 16 (over z, core).
Axes of the slice: x: 4, y: 4, z: 8, core: 2. Of those that a mesh axis runs over, the one named last changes fastest.
Arguments:
- tokens: bfloat16 [4096, 512], P('tok'), may hold values from -128 to 128
- codebook: bfloat16 [65536, 512], P('code'), may hold values from -1 to 1
Outputs:
- targets: bfloat16 [4096, 65536], P('tok', 'code')
- updated_codebook: float32 [65536, 512], P(('code', 'tok'))
All inputs are finite; a program needn't handle non-finite values.
Results may differ from a plain program's by a relative error of at most 0.011.
Values may be sent and summed in bfloat16 or wider, within the bound.
No kernel may reach another device: no remote copies, remote signals or barrier semaphores. Data moves between devices by JAX's collectives and lax.ppermute only.
A program may use at most 64 MiB of HBM per device.

v0:
```python
import math

import jax
import jax.numpy as jnp
from jax import lax
from jax.sharding import PartitionSpec as P

ITERS = 3


sharpness_factor = 2.5
rms_epsilon = 1e-06


def per_device(tokens, codebook):
    tok_rows = tokens.shape[0]
    code_rows = codebook.shape[0]
    total_tokens = tok_rows * lax.axis_size("tok")
    total_codes = code_rows * lax.axis_size("code")

    def score_panel():
        return jnp.dot(tokens, codebook.T, preferred_element_type=jnp.float32) * sharpness_factor

    token_potential = jnp.zeros((tok_rows,), jnp.float32)
    for step in range(ITERS):
        column_values = score_panel() + token_potential[:, None]
        column_top = lax.pmax(jnp.max(column_values, axis=0), "tok")
        column_total = lax.psum(
            jnp.sum(jnp.exp(column_values - column_top[None, :]), axis=0), "tok"
        )
        code_potential = -math.log(total_codes) - (column_top + jnp.log(column_total))
        values = score_panel() + code_potential[None, :]
        top = lax.pmax(jnp.max(values, axis=1), "code")
        total = lax.psum(jnp.sum(jnp.exp(values - top[:, None]), axis=1), "code")
        token_potential = -math.log(total_tokens) - (top + jnp.log(total))
    targets = (
        total_tokens * jnp.exp(score_panel() + token_potential[:, None] + code_potential[None, :])
    ).astype(jnp.bfloat16)
    share = code_rows // lax.axis_size("tok")
    offset = lax.axis_index("tok") * share
    own_codes = lax.dynamic_slice_in_dim(codebook, offset, share, 0)
    summed = lax.psum_scatter(
        lax.dot_general(
            targets, tokens, (((0,), (0,)), ((), ())), preferred_element_type=jnp.float32
        ).astype(jnp.bfloat16),
        "tok",
        scatter_dimension=0,
        tiled=True,
    ).astype(jnp.float32)
    mixed = own_codes.astype(jnp.float32) + summed
    updated_codebook = mixed * lax.rsqrt(
        jnp.mean(mixed * mixed, axis=1, keepdims=True) + rms_epsilon
    )
    return (targets, updated_codebook)


def solution(mesh):
    return jax.shard_map(
        per_device,
        mesh=mesh,
        in_specs=(P("tok", None), P("code", None)),
        out_specs=(P("tok", "code"), P(("code", "tok"), None)),
        check_vma=False,
    )
```

profile of v0, /device:TPU:1, one launch (start us, length us, event | category | flops | bytes accessed | tf_op | source)
XLA Modules:
  0.0 704.0 jit_solution(13124708392009150387)
XLA Ops:
  7.2 0.0 reduce-scatter.2.cloned.1.call-start
  7.2 0.9 copy-done
  8.1 5.4 fusion.1
  13.5 61.2 %pmax.42 = f32[4096]{0:T(1024)S(1)} all-reduce(f32[4096]{0:T(1024)S(1)} %get-tuple-element.2), channel_id=1, replica_groups=mesh['tok'=16,'code'=16] {'tok'}, use_global_device_ids=true, to_apply=%region_1.0 | all-reduce | flops 4096 | bytes 32768 | tf_op jit(solution)/shard_map/pmax | solution.py:27
  74.8 2.8 exponential_reduce_fusion.5
  77.5 55.9 %psum.42 = f32[4096]{0:T(1024)S(1)} all-reduce(f32[4096]{0:T(1024)S(1)} %exponential_reduce_fusion.5), channel_id=1, replica_groups=mesh['tok'=16,'code'=16] {'tok'}, use_global_device_ids=true, to_apply=%region_3.0 | all-reduce | flops 4096 | bytes 32768 | tf_op jit(solution)/shard_map/psum | solution.py:28
  133.4 2.6 add_reduce_fusion.4
  136.0 54.5 %pmax.43 = f32[256]{0:T(256)S(1)} all-reduce(f32[256]{0:T(256)S(1)} %add_reduce_fusion.4), channel_id=1, replica_groups=mesh['tok'=16,'code'=16] {'code'}, use_global_device_ids=true, to_apply=%region_5.0 | all-reduce | flops 256 | bytes 2048 | tf_op jit(solution)/shard_map/pmax | solution.py:33
  190.4 3.0 exponential_reduce_fusion.4
  193.4 23.1 %psum.43 = f32[256]{0:T(256)S(1)} all-reduce(f32[256]{0:T(256)S(1)} %exponential_reduce_fusion.4), channel_id=1, replica_groups=mesh['tok'=16,'code'=16] {'code'}, use_global_device_ids=true, to_apply=%region_7.0 | all-reduce | flops 256 | bytes 2048 | tf_op jit(solution)/shard_map/psum | solution.py:34
  216.5 2.7 add_reduce_fusion.3
  219.2 55.7 %pmax.44 = f32[4096]{0:T(1024)S(1)} all-reduce(f32[4096]{0:T(1024)S(1)} %add_reduce_fusion.3), channel_id=1, replica_groups=mesh['tok'=16,'code'=16] {'tok'}, use_global_device_ids=true, to_apply=%region_9.0 | all-reduce | flops 4096 | bytes 32768 | tf_op jit(solution)/shard_map/pmax | solution.py:27
  274.9 3.0 exponential_reduce_fusion.3
  277.9 55.8 %psum.44 = f32[4096]{0:T(1024)S(1)} all-reduce(f32[4096]{0:T(1024)S(1)} %exponential_reduce_fusion.3), channel_id=1, replica_groups=mesh['tok'=16,'code'=16] {'tok'}, use_global_device_ids=true, to_apply=%region_11.0 | all-reduce | flops 4096 | bytes 32768 | tf_op jit(solution)/shard_map/psum | solution.py:28
  333.7 2.6 add_reduce_fusion.2
  336.2 51.4 %pmax.45 = f32[256]{0:T(256)S(1)} all-reduce(f32[256]{0:T(256)S(1)} %add_reduce_fusion.2), channel_id=1, replica_groups=mesh['tok'=16,'code'=16] {'code'}, use_global_device_ids=true, to_apply=%region_13.0 | all-reduce | flops 256 | bytes 2048 | tf_op jit(solution)/shard_map/pmax | solution.py:33
  387.7 3.0 exponential_reduce_fusion.2
  390.7 23.5 %psum.45 = f32[256]{0:T(256)S(1)} all-reduce(f32[256]{0:T(256)S(1)} %exponential_reduce_fusion.2), channel_id=1, replica_groups=mesh['tok'=16,'code'=16] {'code'}, use_global_device_ids=true, to_apply=%region_15.0 | all-reduce | flops 256 | bytes 2048 | tf_op jit(solution)/shard_map/psum | solution.py:34
  414.2 2.7 add_reduce_fusion.1
  416.9 56.3 %pmax.46 = f32[4096]{0:T(1024)S(1)} all-reduce(f32[4096]{0:T(1024)S(1)} %add_reduce_fusion.1), channel_id=1, replica_groups=mesh['tok'=16,'code'=16] {'tok'}, use_global_device_ids=true, to_apply=%region_17.0 | all-reduce | flops 4096 | bytes 32768 | tf_op jit(solution)/shard_map/pmax | solution.py:27
  473.2 3.0 exponential_reduce_fusion.1
  476.1 55.8 %psum.46 = f32[4096]{0:T(1024)S(1)} all-reduce(f32[4096]{0:T(1024)S(1)} %exponential_reduce_fusion.1), channel_id=1, replica_groups=mesh['tok'=16,'code'=16] {'tok'}, use_global_device_ids=true, to_apply=%region_19.0 | all-reduce | flops 4096 | bytes 32768 | tf_op jit(solution)/shard_map/psum | solution.py:28
  531.9 2.6 add_reduce_fusion
  534.5 50.6 %pmax.47 = f32[256]{0:T(256)S(1)} all-reduce(f32[256]{0:T(256)S(1)} %add_reduce_fusion), channel_id=1, replica_groups=mesh['tok'=16,'code'=16] {'code'}, use_global_device_ids=true, to_apply=%region_21.0 | all-reduce | flops 256 | bytes 2048 | tf_op jit(solution)/shard_map/pmax | solution.py:33
  585.1 3.0 exponential_reduce_fusion
  588.1 23.5 %psum.47 = f32[256]{0:T(256)S(1)} all-reduce(f32[256]{0:T(256)S(1)} %exponential_reduce_fusion), channel_id=1, replica_groups=mesh['tok'=16,'code'=16] {'code'}, use_global_device_ids=true, to_apply=%region_23.0 | all-reduce | flops 256 | bytes 2048 | tf_op jit(solution)/shard_map/psum | solution.py:34
  611.6 3.0 multiply_convert_fusion
  614.7 3.2 convolution_convert_fusion
  617.9 0.0 reduce-scatter.2.cloned.1.call-update
  617.9 76.2 %reduce-scatter.2.cloned.1.call-done = bf16[256,512]{1,0:T(8,128)(2,1)} async-done(((bf16[4096,512]{1,0:T(8,128)(2,1)}), bf16[256,512]{1,0:T(8,128)(2,1)}) %reduce-scatter.2.cloned.1.call-update) | async-done | bytes 262160 | tf_op jit(solution)/shard_map/reduce_scatter | solution.py:42
  694.1 1.2 multiply_reduce_fusion
  695.3 1.9 fusion
  (10 shorter events, 0.1 us)
Async XLA Ops:
  7.2 1.0 copy-start
  7.2 686.9 %reduce-scatter.2.cloned.1.call-start = ((), (), s32[]{:S(2)}) async-start(), calls=%async_computation.1 | async-start | bytes 4456448 | tf_op jit(solution)/shard_map/reduce_scatter | solution.py:42
  614.6 3.2 copy-start.1
Sparse Core Ops, SparseCore 0:
  618.0 75.9 reduce-scatter.1
where the time goes:
time: 705 us; the launch traced here: 704 us
  blocking collectives  567 us (80%)
  waiting for transfers between devices  76.2 us (11%)
  other arithmetic  37 us (5%)
  between operations  14.1 us (2%)
  matrix products  8.62 us (1%)
    pmax x3, blocking collectives, per_device(): column_top = lax.pmax(jnp.max(column_values, axis=0), 'tok')  173 us
    psum x3, blocking collectives, per_device(): lax.psum(jnp.sum(jnp.exp(column_values - column_top[None, :]), axis=0), '...  167 us
    pmax x3, blocking collectives, per_device(): top = lax.pmax(jnp.max(values, axis=1), 'code')  156 us
    reduce_scatter x1, waiting for transfers between devices, per_device(): lax.psum_scatter(lax.dot_general(targets, tokens, (((0,), (0,)), ((), ())...  76.2 us
    psum x3, blocking collectives, per_device(): total = lax.psum(jnp.sum(jnp.exp(values - top[:, None]), axis=1), 'code')  70.1 us
  transfers between devices with their start and end apart: 1, of which 1 were waited for; matrix products, arithmetic and copies ran while one was open for 0% of the time, Pallas kernels for 0%

commit v1 on v0

v1 whole, which is shorter than its diff:
```python
import functools
import math

import jax
import jax.numpy as jnp
from jax import lax
from jax.experimental import pallas as pl
from jax.experimental.pallas import tpu as pltpu
from jax.sharding import PartitionSpec as P

ITERS = 3


sharpness_factor = 2.5
rms_epsilon = 1e-06

LANES = 128
CHUNK = 512
MIB = 1 << 20

score_scale = sharpness_factor * math.log2(math.e)


def lse2(values, axis):
    top = jnp.max(values, axis=axis, keepdims=True)
    total = jnp.sum(jnp.exp2(values - top), axis=axis)
    return jnp.squeeze(top, axis) + jnp.log2(total)


def as_column(row):
    return jnp.broadcast_to(row, (LANES, LANES)).T


def tile(k):
    return pl.ds(pl.multiple_of(k * LANES, LANES), LANES)


def column_lse(scores, potential, k):
    values = scores[:, tile(k)]
    if potential is not None:
        values = values + potential[...]
    values = values.reshape(values.shape[0] // 8, 8, LANES)
    top = jnp.max(values, axis=0)
    total = jnp.sum(jnp.exp2(values - top[None]), axis=0)
    most = jnp.max(top, axis=0, keepdims=True)
    total = jnp.sum(total * jnp.exp2(top - most), axis=0, keepdims=True)
    return most + jnp.log2(total)


def send_copies(local, out):
    for d in range(out.shape[0]):
        out[d] = local[...]


def scores_kernel(tokens, codebook, scores, out, held, local, sems):
    chunks = codebook.shape[0] // CHUNK
    copies = [
        pltpu.make_async_copy(
            codebook.at[pl.ds(k * CHUNK, CHUNK)], held.at[pl.ds(k * CHUNK, CHUNK)], sems.at[k]
        )
        for k in range(chunks)
    ]
    for copy in copies:
        copy.start()
    for k in range(chunks):
        copies[k].wait()
        scores[:, pl.ds(k * CHUNK, CHUNK)] = (
            lax.dot_general(
                tokens[...],
                held[pl.ds(k * CHUNK, CHUNK), :],
                (((1,), (1,)), ((), ())),
                preferred_element_type=jnp.float32,
            )
            * score_scale
        )
        for j in range(k * CHUNK // LANES, (k + 1) * CHUNK // LANES):
            local[pl.ds(j, 1), :] = column_lse(scores, None, j)
    send_copies(local, out)


def columns_kernel(shift, received, scores, out, column, local):
    potential = -shift - lse2(received[...], 0)
    for h in range(potential.shape[0]):
        column[pl.ds(h * LANES, LANES), :] = as_column(potential[h : h + 1, :])

    def step(k, carry):
        local[pl.ds(k, 1), :] = column_lse(scores, column, k)
        return carry

    lax.fori_loop(0, local.shape[0], step, 0, unroll=4)
    send_copies(local, out)


def rows_kernel(shift, received, scores, out, potential, local):
    potential[...] = -shift - lse2(received[...], 0)
    tiles = potential.shape[0]
    for h in range(local.shape[0]):
        rows = pl.ds(h * LANES, LANES)

        def values(k):
            return scores[rows, tile(k)] + potential[pl.ds(k, 1), :]

        top = lax.fori_loop(
            0, tiles, lambda k, top: jnp.maximum(top, values(k)), values(0), unroll=4
        )
        total = lax.fori_loop(
            0,
            tiles,
            lambda k, total: total + jnp.exp2(values(k) - top),
            jnp.zeros((LANES, LANES), jnp.float32),
            unroll=4,
        )
        top = top.T
        most = jnp.max(top, axis=0, keepdims=True)
        total = jnp.sum(total.T * jnp.exp2(top - most), axis=0, keepdims=True)
        local[pl.ds(h, 1), :] = most + jnp.log2(total)
    send_copies(local, out)


def token_potential_kernel(shift, received, out):
    potential = -shift - lse2(received[...], 0)
    for d in range(out.shape[0]):
        out[d] = potential


def targets_kernel(scale, token_potential, code_potential, scores, out, column, held, sems):
    for h in range(token_potential.shape[0]):
        column[pl.ds(h * LANES, LANES), :] = as_column(token_potential[h : h + 1, :]) + scale
    copies = []
    for k in range(scores.shape[1] // CHUNK):
        for j in range(k * CHUNK // LANES, (k + 1) * CHUNK // LANES):
            held[:, tile(j)] = jnp.exp2(
                scores[:, tile(j)] + column[...] + code_potential[pl.ds(j, 1), :]
            ).astype(held.dtype)
        part = (slice(None), pl.ds(k * CHUNK, CHUNK))
        copies.append(pltpu.make_async_copy(held.at[part], out.at[part], sems.at[k]))
        copies[k].start()
    for copy in copies:
        copy.wait()


def own_scores_kernel(scale, codes, potential, tokens, scores, held, column, sems):
    chunks = tokens.shape[0] // CHUNK
    copies = [
        pltpu.make_async_copy(
            tokens.at[pl.ds(k * CHUNK, CHUNK)], held.at[pl.ds(k * CHUNK, CHUNK)], sems.at[k]
        )
        for k in range(chunks)
    ]
    for copy in copies:
        copy.start()
    for h in range(potential.shape[0]):
        column[pl.ds(h * LANES, LANES), :] = as_column(potential[h : h + 1, :]) + scale
    for k in range(chunks):
        copies[k].wait()
        values = lax.dot_general(
            codes[...],
            held[pl.ds(k * CHUNK, CHUNK), :],
            (((1,), (1,)), ((), ())),
            preferred_element_type=jnp.float32,
        )
        for j in range(CHUNK // LANES):
            scores[:, pl.ds(k * CHUNK + j * LANES, LANES)] = (
                values[:, j * LANES : (j + 1) * LANES] * score_scale + column[...]
            )


def refresh_kernel(codes, potential, scores, tokens, out):
    halves = potential.shape[1]
    assigned = jnp.zeros(out.shape, jnp.float32)
    for k in range(tokens.shape[0] // CHUNK):
        parts = []
        for j in range(k * CHUNK // LANES, (k + 1) * CHUNK // LANES):
            row = potential[j // halves, pl.ds(j % halves, 1), :]
            parts.append(jnp.exp2(scores[:, tile(j)] + row).astype(tokens.dtype))
        assigned += jnp.dot(
            jnp.concatenate(parts, axis=1),
            tokens[pl.ds(k * CHUNK, CHUNK), :],
            preferred_element_type=jnp.float32,
        )
    mixed = codes[...].astype(jnp.float32) + assigned
    out[...] = mixed * lax.rsqrt(
        jnp.mean(mixed * mixed, axis=1, keepdims=True) + rms_epsilon
    )


def in_vmem(array):
    return pltpu.with_memory_space_constraint(array, pltpu.VMEM)


def call(kernel, out_shape, scratch=(), specs=None, out_specs=None, limit=24, elements=0, flops=0):
    vmem = pl.BlockSpec(memory_space=pltpu.VMEM)
    return pl.pallas_call(
        kernel,
        out_shape=out_shape,
        in_specs=specs,
        out_specs=out_specs if out_specs is not None else jax.tree.map(lambda _: vmem, out_shape),
        scratch_shapes=list(scratch),
        compiler_params=pltpu.CompilerParams(vmem_limit_bytes=limit * MIB),
        cost_estimate=pl.CostEstimate(
            flops=flops + 4 * elements, transcendentals=elements, bytes_accessed=4 * elements
        ),
    )


def per_device(tokens, codebook):
    tok_size, code_size = lax.axis_size("tok"), lax.axis_size("code")
    tok_rows, depth = tokens.shape
    code_rows = codebook.shape[0]
    total_tokens = tok_rows * tok_size
    total_codes = code_rows * code_size
    share = code_rows // tok_size
    row_tiles, code_tiles = tok_rows // LANES, code_rows // LANES
    elements = tok_rows * code_rows
    f32 = jnp.float32
    vmem = pl.BlockSpec(memory_space=pltpu.VMEM)
    hbm = pl.BlockSpec(memory_space=pl.ANY)
    resident = functools.partial(pltpu.VMEM, dtype=f32)
    to_tok = jax.ShapeDtypeStruct((tok_size, code_tiles, LANES), f32)
    to_code = jax.ShapeDtypeStruct((code_size, row_tiles, LANES), f32)
    column = pltpu.VMEM((tok_rows, LANES), f32)

    def exchange(copies, axis):
        return lax.all_to_all(copies, axis, 0, 0)

    all_tokens = lax.all_gather(tokens, "tok", axis=0, tiled=True)

    scores, copies = call(
        scores_kernel,
        (pltpu.VMEM((tok_rows, code_rows), f32), to_tok),
        [
            pltpu.VMEM((code_rows, depth), codebook.dtype),
            pltpu.VMEM((code_tiles, LANES), f32),
            pltpu.SemaphoreType.DMA((code_rows // CHUNK,)),
        ],
        specs=[vmem, hbm],
        elements=elements,
        flops=2 * elements * depth,
    )(tokens, codebook)
    for step in range(ITERS):
        received = exchange(copies, "tok")
        copies, code_potential = call(
            functools.partial(rows_kernel, math.log2(total_codes)),
            (to_code, jax.ShapeDtypeStruct((code_tiles, LANES), f32)),
            [pltpu.VMEM((row_tiles, LANES), f32)],
            specs=[vmem, vmem],
            elements=elements,
        )(received, in_vmem(scores))
        received = exchange(copies, "code")
        if step < ITERS - 1:
            copies = call(
                functools.partial(columns_kernel, math.log2(total_tokens)),
                to_tok,
                [column, pltpu.VMEM((code_tiles, LANES), f32)],
                specs=[vmem, vmem],
                elements=elements,
            )(received, in_vmem(scores))

    place = lax.axis_index("tok")
    own_codes = lax.dynamic_slice_in_dim(codebook, place * share, share, 0)
    share_tiles = share // LANES
    own_potential = lax.dynamic_slice_in_dim(code_potential, place * share_tiles, share_tiles, 0)
    own_scores, held_tokens = call(
        functools.partial(own_scores_kernel, math.log2(total_tokens)),
        (
            pltpu.VMEM((share, total_tokens), f32),
            pltpu.VMEM((total_tokens, depth), tokens.dtype),
        ),
        [
            pltpu.VMEM((share, LANES), f32),
            pltpu.SemaphoreType.DMA((total_tokens // CHUNK,)),
        ],
        specs=[vmem, vmem, hbm],
        elements=elements,
        flops=2 * elements * depth,
    )(own_codes, own_potential, all_tokens)

    copies = call(
        functools.partial(token_potential_kernel, math.log2(total_tokens)),
        jax.ShapeDtypeStruct((tok_size, row_tiles, LANES), f32),
        specs=[vmem],
    )(received)
    all_potential = exchange(copies, "tok")
    targets = call(
        functools.partial(targets_kernel, math.log2(total_tokens)),
        jax.ShapeDtypeStruct((tok_rows, code_rows), jnp.bfloat16),
        [
            column,
            pltpu.VMEM((tok_rows, code_rows), jnp.bfloat16),
            pltpu.SemaphoreType.DMA((code_rows // CHUNK,)),
        ],
        specs=[vmem, vmem, vmem],
        out_specs=hbm,
        elements=elements,
    )(copies[0], code_potential, in_vmem(scores))
    updated_codebook = call(
        refresh_kernel,
        jax.ShapeDtypeStruct((share, depth), f32),
        specs=[vmem, vmem, vmem, vmem],
        elements=elements,
        flops=2 * elements * depth,
    )(own_codes, all_potential, in_vmem(own_scores), in_vmem(held_tokens))
    return (targets, updated_codebook)


def solution(mesh):
    return jax.shard_map(
        per_device,
        mesh=mesh,
        in_specs=(P("tok", None), P("code", None)),
        out_specs=(P("tok", "code"), P(("code", "tok"), None)),
        check_vma=False,
    )
```

time: 705 us -> 142 us (0.20)
  blocking collectives: 567 us -> 58.4 us
  waiting for transfers between devices: 76.2 us -> 15.5 us
  other arithmetic: 37 us -> 0 us
  Pallas kernels: 0 us -> 22.4 us
  local copies, waits for them, and re-layouts: 0.91 us -> 19.7 us
  starting transfers between devices: 0.04 us -> 11.6 us
  matrix products: 8.62 us -> 0 us
    pmax x6 -> x0, blocking collectives: 330 us -> none  [the longest x3 173 us: per_device(): column_top = lax.pmax(jnp.max(column_values, axis=0), 'tok')]
    psum x6 -> x0, blocking collectives: 238 us -> none  [the longest x3 167 us: per_device(): lax.psum(jnp.sum(jnp.exp(column_values - column_top[None, :]), axis=0), '...]
    reduce_scatter x1 -> x0, waiting for transfers between devices: 76.2 us -> none  [per_device(): lax.psum_scatter(lax.dot_general(targets, tokens, (((0,), (0,)), ((), ())...]
    all_to_all x0 -> x4, blocking collectives: none -> 58.4 us  [exchange(): return lax.all_to_all(copies, axis, 0, 0)]
    pallas_call x0 -> x10, Pallas kernels: none -> 22.4 us  [the longest x3 7.07 us: per_device(): call(functools.partial(rows_kernel, math.log2(total_codes)), (to_code, ja...]
    reduce_sum x7 -> x0, other arithmetic: 18.9 us -> none  [the longest x3 9.03 us: per_device(): total = lax.psum(jnp.sum(jnp.exp(values - top[:, None]), axis=1), 'code')]
    unnamed x4 -> x20, local copies, waits for them, and re-layouts: 0.91 us -> 18 us
    all_to_all x0 -> x3, waiting for transfers between devices: none -> 14.8 us  [exchange(): return lax.all_to_all(copies, axis, 0, 0)]
  transfers between devices with their start and end apart: 1 -> 4, of which waited for: 1 -> 2; matrix products, arithmetic and copies ran while one was open for 0% -> 1% of each run, Pallas kernels for 0% -> 14%
where the time goes in v1:
time: 142 us
  blocking collectives  58.4 us (41%)
  Pallas kernels  22.4 us (16%)
  local copies, waits for them, and re-layouts  19.7 us (14%)
  waiting for transfers between devices  15.5 us (11%)
  between operations  14.1 us (10%)
  starting transfers between devices  11.6 us (8%)
    all_to_all x4, blocking collectives, exchange(): return lax.all_to_all(copies, axis, 0, 0)  58.4 us
    unnamed x20, local copies, waits for them, and re-layouts  18 us
    all_to_all x3, waiting for transfers between devices, exchange(): return lax.all_to_all(copies, axis, 0, 0)  14.8 us
    all_to_all x3, starting transfers between devices, exchange(): return lax.all_to_all(copies, axis, 0, 0)  11.5 us
    pallas_call x3, Pallas kernels, per_device(): call(functools.partial(rows_kernel, math.log2(total_codes)), (to_code, ja...  7.07 us
    pallas_call x1, Pallas kernels, per_device(): call(scores_kernel, (pltpu.VMEM((tok_rows, code_rows), f32), to_tok), [pl...  4.07 us
    pallas_call x2, Pallas kernels, per_device(): call(functools.partial(columns_kernel, math.log2(total_tokens)), to_tok,...  3.81 us
    pallas_call x1, Pallas kernels, per_device(): call(functools.partial(own_scores_kernel, math.log2(total_tokens)), (pltp...  3.14 us
  transfers between devices with their start and end apart: 4, of which 2 were waited for; matrix products, arithmetic and copies ran while one was open for 1% of the time, Pallas kernels for 14%

profile of v1, /device:TPU:1, one launch (start us, length us, event | category | flops | bytes accessed | tf_op | source)
XLA Modules:
  0.0 141.7 jit_solution(68632199662390596)
XLA Ops:
  7.2 0.0 all-gather.2.cloned.1.call-start
  7.2 0.7 all-gather.2.cloned.1.call-update
  7.9 2.2 %copy-done.3 = bf16[4096,512]{1,0:T(8,128)(2,1)S(1)} copy-done((bf16[4096,512]{1,0:T(8,128)(2,1)S(1)}, bf16[4096,512]{1,0:T(8,128)(2,1)}, u32[]{:S(2)}) %copy-start.3) | copy-done | bytes 4194328
  10.1 0.9 copy-done.9
  11.0 4.1 %shard_map.41 = (f32[256,4096]{1,0:T(8,128)S(1)}, f32[16,32,128]{2,1,0:T(8,128)S(1)}) custom-call(bf16[256,512]{1,0:T(8,128)(2,1)S(1)} %copy-done.9, bf16[4096,512]{1,0:T(8,128)(2,1)S(1)} %copy-done.3), custom_call_target="tpu_custom_call" | custom-call | flops 1077936128 | bytes 4194304 | tf_op jit(solution)/shard_map/pallas_call | solution.py:228
  15.1 14.9 %all_to_all.35.received = f32[16,32,128]{2,1,0:T(8,128)S(1)} all-to-all(f32[16,32,128]{2,1,0:T(8,128)S(1)} %get-tuple-element.10), channel_id=1, replica_groups=mesh['tok'=16,'code'=16] {'tok'}, dimensions={0} | all-to-all | bytes 524288 | tf_op jit(solution)/shard_map/all_to_all | solution.py:224
  30.1 2.3 %shard_map.42 = (f32[16,2,128]{2,1,0:T(2,128)S(1)}, f32[32,128]{1,0:T(8,128)}) custom-call(f32[16,32,128]{2,1,0:T(8,128)S(1)} %all_to_all.35.received, f32[256,4096]{1,0:T(8,128)S(1)} %get-tuple-element.11.scores), custom_call_target="tpu_custom_call" | custom-call | flops 4194304 | bytes 4194304 | tf_op jit(solution)/shard_map/pallas_call | solution.py:242
  32.4 18.1 %all_to_all.36.received = f32[16,2,128]{2,1,0:T(2,128)S(1)} all-to-all(f32[16,2,128]{2,1,0:T(2,128)S(1)} %get-tuple-element.12), channel_id=1, replica_groups=mesh['tok'=16,'code'=16] {'code'}, dimensions={0} | all-to-all | bytes 32768 | tf_op jit(solution)/shard_map/all_to_all | solution.py:224
  50.5 1.6 %shard_map.43 = f32[16,32,128]{2,1,0:T(8,128)S(1)} custom-call(f32[16,2,128]{2,1,0:T(2,128)S(1)} %all_to_all.36.received, f32[256,4096]{1,0:T(8,128)S(1)} %get-tuple-element.11.scores), custom_call_target="tpu_custom_call" | custom-call | flops 4194304 | bytes 4194304 | tf_op jit(solution)/shard_map/pallas_call | solution.py:251
  52.0 14.0 %all_to_all.37.received = f32[16,32,128]{2,1,0:T(8,128)S(1)} all-to-all(f32[16,32,128]{2,1,0:T(8,128)S(1)} %shard_map.43), channel_id=1, replica_groups=mesh['tok'=16,'code'=16] {'tok'}, dimensions={0} | all-to-all | bytes 524288 | tf_op jit(solution)/shard_map/all_to_all | solution.py:224
  66.1 2.3 %shard_map.44 = (f32[16,2,128]{2,1,0:T(2,128)S(1)}, f32[32,128]{1,0:T(8,128)}) custom-call(f32[16,32,128]{2,1,0:T(8,128)S(1)} %all_to_all.37.received, f32[256,4096]{1,0:T(8,128)S(1)} %get-tuple-element.11.scores), custom_call_target="tpu_custom_call" | custom-call | flops 4194304 | bytes 4194304 | tf_op jit(solution)/shard_map/pallas_call | solution.py:242
  68.4 11.3 %all_to_all.38.received = f32[16,2,128]{2,1,0:T(2,128)S(1)} all-to-all(f32[16,2,128]{2,1,0:T(2,128)S(1)} %get-tuple-element.13), channel_id=1, replica_groups=mesh['tok'=16,'code'=16] {'code'}, dimensions={0} | all-to-all | bytes 32768 | tf_op jit(solution)/shard_map/all_to_all | solution.py:224
  79.7 2.3 %shard_map.45 = f32[16,32,128]{2,1,0:T(8,128)} custom-call(f32[16,2,128]{2,1,0:T(2,128)S(1)} %all_to_all.38.received, f32[256,4096]{1,0:T(8,128)S(1)} %get-tuple-element.11.scores), custom_call_target="tpu_custom_call" | custom-call | flops 4194304 | bytes 4194304 | tf_op jit(solution)/shard_map/pallas_call | solution.py:251
  82.0 3.5 %all-to-all-start.4 = ((f32[16,32,128]{2,1,0:T(8,128)}), f32[16,32,128]{2,1,0:T(8,128)S(1)}, u32[]{:S(2)}, u32[]{:S(2)}) async-start(f32[16,32,128]{2,1,0:T(8,128)} %shard_map.45), calls=%async_computation.4 | async-start | bytes 524288 | tf_op jit(solution)/shard_map/all_to_all | solution.py:224
  85.5 1.0 constant_dynamic-slice_fusion.1.codes
  86.5 7.4 %all-to-all-done.4.received = f32[16,32,128]{2,1,0:T(8,128)S(1)} async-done(((f32[16,32,128]{2,1,0:T(8,128)}), f32[16,32,128]{2,1,0:T(8,128)S(1)}, u32[]{:S(2)}, u32[]{:S(2)}) %all-to-all-start.4) | async-done | bytes 262176 | tf_op jit(solution)/shard_map/all_to_all | solution.py:224
  93.9 2.2 %copy-done.1 = f32[256,4096]{1,0:T(8,128)S(1)} copy-done((f32[256,4096]{1,0:T(8,128)S(1)}, f32[256,4096]{1,0:T(8,128)}, u32[]{:S(2)}) %copy-start.1) | copy-done | bytes 4194328
  96.1 2.5 %shard_map.46 = (f32[16,2,128]{2,1,0:T(2,128)}, f32[32,128]{1,0:T(8,128)S(1)}) custom-call(f32[16,32,128]{2,1,0:T(8,128)S(1)} %all-to-all-done.4.received, f32[256,4096]{1,0:T(8,128)S(1)} %copy-done.1), custom_call_target="tpu_custom_call" | custom-call | flops 4194304 | bytes 4194304 | tf_op jit(solution)/shard_map/pallas_call | solution.py:242
  98.5 4.5 %all-to-all-start.5 = ((f32[16,2,128]{2,1,0:T(2,128)}), f32[16,2,128]{2,1,0:T(2,128)S(1)}, u32[]{:S(2)}, u32[]{:S(2)}) async-start(f32[16,2,128]{2,1,0:T(2,128)} %get-tuple-element.14), calls=%async_computation.5 | async-start | bytes 32768 | tf_op jit(solution)/shard_map/all_to_all | solution.py:224
  103.0 7.4 %all-to-all-done.5.received = f32[16,2,128]{2,1,0:T(2,128)S(1)} async-done(((f32[16,2,128]{2,1,0:T(2,128)}), f32[16,2,128]{2,1,0:T(2,128)S(1)}, u32[]{:S(2)}, u32[]{:S(2)}) %all-to-all-start.5) | async-done | bytes 16416 | tf_op jit(solution)/shard_map/all_to_all | solution.py:224
  110.4 0.7 shard_map.47
  111.1 3.5 %all-to-all-start.6 = ((f32[16,2,128]{2,1,0:T(2,128)}), f32[16,2,128]{2,1,0:T(2,128)S(1)}, u32[]{:S(2)}, u32[]{:S(2)}) async-start(f32[16,2,128]{2,1,0:T(2,128)} %shard_map.47), calls=%async_computation.6 | async-start | bytes 32768 | tf_op jit(solution)/shard_map/all_to_all | solution.py:224
  114.6 0.7 slice_bitcast_fusion.token_potential
  115.3 2.2 %copy-done.2 = f32[256,4096]{1,0:T(8,128)S(1)} copy-done((f32[256,4096]{1,0:T(8,128)S(1)}, f32[256,4096]{1,0:T(8,128)}, u32[]{:S(2)}) %copy-start.2) | copy-done | bytes 4194328
  117.5 1.5 %shard_map.48 = bf16[256,4096]{1,0:T(8,128)(2,1)} custom-call(f32[2,128]{1,0:T(2,128)S(1)} %slice_bitcast_fusion.token_potential, f32[32,128]{1,0:T(8,128)S(1)} %get-tuple-element.15.code_potential, f32[256,4096]{1,0:T(8,128)S(1)} %copy-done.2), custom_call_target="tpu_custom_call" | custom-call | flops 4194304 | bytes 4194304 | tf_op jit(solution)/shard_map/pallas_call | solution.py:284
  119.1 2.2 %copy-done.4 = bf16[4096,512]{1,0:T(8,128)(2,1)S(1)} copy-done((bf16[4096,512]{1,0:T(8,128)(2,1)S(1)}, bf16[4096,512]{1,0:T(8,128)(2,1)}, u32[]{:S(2)}) %copy-start.4) | copy-done | bytes 4194328
  121.2 3.1 %shard_map.49 = (f32[256,4096]{1,0:T(8,128)S(1)}, bf16[4096,512]{1,0:T(8,128)(2,1)S(1)}) custom-call(bf16[256,512]{1,0:T(8,128)(2,1)S(1)} %constant_dynamic-slice_fusion.1.codes, f32[2,128]{1,0:T(2,128)S(1)} %constant_dynamic-slice_fusion.potential, bf16[4096,512]{1,0:T(8,128)(2,1)S(1)} %copy-done.4), custom_call_target="tpu_custom_call" | custom-call | flops 1077936128 | bytes 4194304 | tf_op jit(solution)/shard_map/pallas_call | solution.py:263
  124.4 1.9 %copy-done.5 = f32[256,4096]{1,0:T(8,128)} copy-done((f32[256,4096]{1,0:T(8,128)}, f32[256,4096]{1,0:T(8,128)S(1)}, u32[]{:S(2)}) %copy-start.5) | copy-done | bytes 4194328
  126.3 2.0 %copy-done.7 = bf16[4096,512]{1,0:T(8,128)(2,1)} copy-done((bf16[4096,512]{1,0:T(8,128)(2,1)}, bf16[4096,512]{1,0:T(8,128)(2,1)S(1)}, u32[]{:S(2)}) %copy-start.7) | copy-done | bytes 4194328
  128.3 2.2 %copy-done.6 = f32[256,4096]{1,0:T(8,128)S(1)} copy-done((f32[256,4096]{1,0:T(8,128)S(1)}, f32[256,4096]{1,0:T(8,128)}, u32[]{:S(2)}) %copy-start.6) | copy-done | bytes 4194328
  130.5 2.2 %copy-done.8 = bf16[4096,512]{1,0:T(8,128)(2,1)S(1)} copy-done((bf16[4096,512]{1,0:T(8,128)(2,1)S(1)}, bf16[4096,512]{1,0:T(8,128)(2,1)}, u32[]{:S(2)}) %copy-start.8) | copy-done | bytes 4194328
  132.7 2.1 %shard_map.50 = f32[256,512]{1,0:T(8,128)} custom-call(bf16[256,512]{1,0:T(8,128)(2,1)S(1)} %constant_dynamic-slice_fusion.1.codes, f32[16,2,128]{2,1,0:T(2,128)S(1)} %all-to-all-done.6.potential, f32[256,4096]{1,0:T(8,128)S(1)} %copy-done.6, bf16[4096,512]{1,0:T(8,128)(2,1)S(1)} %copy-done.8), custom_call_target="tpu_custom_call" | custom-call | flops 1077936128 | bytes 4194304 | tf_op jit(solution)/shard_map/pallas_call | solution.py:296
  (14 shorter events, 0.1 us)
Async XLA Ops:
  7.2 111.9 %all-gather.2.cloned.1.call-start = ((), (), s32[]{:S(2)}) async-start(), calls=%async_computation.7 | async-start | bytes 4456448 | tf_op jit(solution)/shard_map/all_gather | solution.py:226
  7.9 2.2 %copy-start.3 = (bf16[4096,512]{1,0:T(8,128)(2,1)S(1)}, bf16[4096,512]{1,0:T(8,128)(2,1)}, u32[]{:S(2)}) copy-start(bf16[4096,512]{1,0:T(8,128)(2,1)} %codebook.1) | copy-start | bytes 12582916
  10.1 0.9 copy-start.9
  15.1 64.6 %copy-start = (f32[256,4096]{1,0:T(8,128)}, f32[256,4096]{1,0:T(8,128)S(1)}, u32[]{:S(2)}) copy-start(f32[256,4096]{1,0:T(8,128)S(1)} %get-tuple-element.11.scores) | copy-start | bytes 12582916
  82.0 11.9 %all-to-all-start.4 = ((f32[16,32,128]{2,1,0:T(8,128)}), f32[16,32,128]{2,1,0:T(8,128)S(1)}, u32[]{:S(2)}, u32[]{:S(2)}) async-start(f32[16,32,128]{2,1,0:T(8,128)} %shard_map.45), calls=%async_computation.4 | async-start | bytes 524288 | tf_op jit(solution)/shard_map/all_to_all | solution.py:224
  93.9 2.2 %copy-start.1 = (f32[256,4096]{1,0:T(8,128)S(1)}, f32[256,4096]{1,0:T(8,128)}, u32[]{:S(2)}) copy-start(f32[256,4096]{1,0:T(8,128)} %copy-done) | copy-start | bytes 12582916
  98.5 11.9 %all-to-all-start.5 = ((f32[16,2,128]{2,1,0:T(2,128)}), f32[16,2,128]{2,1,0:T(2,128)S(1)}, u32[]{:S(2)}, u32[]{:S(2)}) async-start(f32[16,2,128]{2,1,0:T(2,128)} %get-tuple-element.14), calls=%async_computation.5 | async-start | bytes 32768 | tf_op jit(solution)/shard_map/all_to_all | solution.py:224
  111.1 17.2 %all-to-all-start.6 = ((f32[16,2,128]{2,1,0:T(2,128)}), f32[16,2,128]{2,1,0:T(2,128)S(1)}, u32[]{:S(2)}, u32[]{:S(2)}) async-start(f32[16,2,128]{2,1,0:T(2,128)} %shard_map.47), calls=%async_computation.6 | async-start | bytes 32768 | tf_op jit(solution)/shard_map/all_to_all | solution.py:224
  115.3 2.2 %copy-start.2 = (f32[256,4096]{1,0:T(8,128)S(1)}, f32[256,4096]{1,0:T(8,128)}, u32[]{:S(2)}) copy-start(f32[256,4096]{1,0:T(8,128)} %copy-done) | copy-start | bytes 12582916
  119.1 2.2 %copy-start.4 = (bf16[4096,512]{1,0:T(8,128)(2,1)S(1)}, bf16[4096,512]{1,0:T(8,128)(2,1)}, u32[]{:S(2)}) copy-start(bf16[4096,512]{1,0:T(8,128)(2,1)} %all-gather.2.cloned.1.call-done.tokens) | copy-start | bytes 12582916
  124.4 1.9 %copy-start.5 = (f32[256,4096]{1,0:T(8,128)}, f32[256,4096]{1,0:T(8,128)S(1)}, u32[]{:S(2)}) copy-start(f32[256,4096]{1,0:T(8,128)S(1)} %get-tuple-element.16.scores) | copy-start | bytes 12582916
  126.3 2.0 %copy-start.7 = (bf16[4096,512]{1,0:T(8,128)(2,1)}, bf16[4096,512]{1,0:T(8,128)(2,1)S(1)}, u32[]{:S(2)}) copy-start(bf16[4096,512]{1,0:T(8,128)(2,1)S(1)} %get-tuple-element.17.tokens) | copy-start | bytes 12582916
  128.3 2.2 %copy-start.6 = (f32[256,4096]{1,0:T(8,128)S(1)}, f32[256,4096]{1,0:T(8,128)}, u32[]{:S(2)}) copy-start(f32[256,4096]{1,0:T(8,128)} %copy-done.5) | copy-start | bytes 12582916
  130.5 2.2 %copy-start.8 = (bf16[4096,512]{1,0:T(8,128)(2,1)S(1)}, bf16[4096,512]{1,0:T(8,128)(2,1)}, u32[]{:S(2)}) copy-start(bf16[4096,512]{1,0:T(8,128)(2,1)} %copy-done.7) | copy-start | bytes 12582916
Sparse Core Ops, SparseCore 0:
  10.4 63.3 all-gather.1

commit v2 on v1

--- a/solution.py
+++ b/solution.py
@@ -52,17 +52,19 @@
         out[d] = local[...]
 
 
+def chunk_copies(source, held, sems, axis=0):
+    copies = []
+    for k in range(source.shape[axis] // CHUNK):
+        part = (slice(None),) * axis + (pl.ds(k * CHUNK, CHUNK),)
+        copies.append(pltpu.make_async_copy(source.at[part], held.at[part], sems.at[k]))
+    return copies
+
+
 def scores_kernel(tokens, codebook, scores, out, held, local, sems):
-    chunks = codebook.shape[0] // CHUNK
-    copies = [
-        pltpu.make_async_copy(
-            codebook.at[pl.ds(k * CHUNK, CHUNK)], held.at[pl.ds(k * CHUNK, CHUNK)], sems.at[k]
-        )
-        for k in range(chunks)
-    ]
+    copies = chunk_copies(codebook, held, sems)
     for copy in copies:
         copy.start()
-    for k in range(chunks):
+    for k in range(len(copies)):
         copies[k].wait()
         scores[:, pl.ds(k * CHUNK, CHUNK)] = (
             lax.dot_general(
@@ -123,60 +125,59 @@
         out[d] = potential
 
 
-def targets_kernel(scale, token_potential, code_potential, scores, out, column, held, sems):
-    for h in range(token_potential.shape[0]):
-        column[pl.ds(h * LANES, LANES), :] = as_column(token_potential[h : h + 1, :]) + scale
-    copies = []
-    for k in range(scores.shape[1] // CHUNK):
+def targets_kernel(
+    scale, token_potential, code_potential, scores, out, column, panel, held, sems, out_sems
+):
+    copies = chunk_copies(scores, panel, sems, 1)
+    for copy in copies:
+        copy.start()
+    for h in range(token_potential.shape[1]):
+        column[pl.ds(h * LANES, LANES), :] = as_column(token_potential[0, pl.ds(h, 1), :]) + scale
+    out_copies = chunk_copies(held, out, out_sems, 1)
+    for k in range(len(copies)):
+        copies[k].wait()
         for j in range(k * CHUNK // LANES, (k + 1) * CHUNK // LANES):
             held[:, tile(j)] = jnp.exp2(
-                scores[:, tile(j)] + column[...] + code_potential[pl.ds(j, 1), :]
+                panel[:, tile(j)] + column[...] + code_potential[pl.ds(j, 1), :]
             ).astype(held.dtype)
-        part = (slice(None), pl.ds(k * CHUNK, CHUNK))
-        copies.append(pltpu.make_async_copy(held.at[part], out.at[part], sems.at[k]))
-        copies[k].start()
-    for copy in copies:
+        out_copies[k].start()
+    for copy in out_copies:
         copy.wait()
 
 
-def own_scores_kernel(scale, codes, potential, tokens, scores, held, column, sems):
-    chunks = tokens.shape[0] // CHUNK
-    copies = [
-        pltpu.make_async_copy(
-            tokens.at[pl.ds(k * CHUNK, CHUNK)], held.at[pl.ds(k * CHUNK, CHUNK)], sems.at[k]
-        )
-        for k in range(chunks)
-    ]
+def refresh_kernel(
+    scale, code_potential, potential, codebook, tokens, out, held, codes, column, sems, own_sem
+):
+    copies = chunk_copies(tokens, held, sems)
+    share, halves = codes.shape[0], potential.shape[1]
+    place = lax.axis_index("tok")
+    own_rows = pl.ds(pl.multiple_of(place * share, share), share)
+    own = pltpu.make_async_copy(codebook.at[own_rows], codes, own_sem)
+    own.start()
     for copy in copies:
         copy.start()
-    for h in range(potential.shape[0]):
-        column[pl.ds(h * LANES, LANES), :] = as_column(potential[h : h + 1, :]) + scale
-    for k in range(chunks):
+    for h in range(share // LANES):
+        row = code_potential[pl.ds(place * (share // LANES) + h, 1), :]
+        column[pl.ds(h * LANES, LANES), :] = as_column(row) + scale
+    own.wait()
+    assigned = jnp.zeros(out.shape, jnp.float32)
+    for k in range(len(copies)):
         copies[k].wait()
-        values = lax.dot_general(
-            codes[...],
-            held[pl.ds(k * CHUNK, CHUNK), :],
-            (((1,), (1,)), ((), ())),
-            preferred_element_type=jnp.float32,
-        )
+        part = held[pl.ds(k * CHUNK, CHUNK), :]
+        scores = (
+            lax.dot_general(
+                codes[...], part, (((1,), (1,)), ((), ())), preferred_element_type=jnp.float32
+            )
+            * score_scale
+        )
+        weights = []
         for j in range(CHUNK // LANES):
-            scores[:, pl.ds(k * CHUNK + j * LANES, LANES)] = (
-                values[:, j * LANES : (j + 1) * LANES] * score_scale + column[...]
-            )
-
-
-def refresh_kernel(codes, potential, scores, tokens, out):
-    halves = potential.shape[1]
-    assigned = jnp.zeros(out.shape, jnp.float32)
-    for k in range(tokens.shape[0] // CHUNK):
-        parts = []
-        for j in range(k * CHUNK // LANES, (k + 1) * CHUNK // LANES):
-            row = potential[j // halves, pl.ds(j % halves, 1), :]
-            parts.append(jnp.exp2(scores[:, tile(j)] + row).astype(tokens.dtype))
+            at = k * CHUNK // LANES + j
+            row = potential[at // halves, pl.ds(at % halves, 1), :]
+            values = scores[:, j * LANES : (j + 1) * LANES] + column[...] + row
+            weights.append(jnp.exp2(values).astype(part.dtype))
         assigned += jnp.dot(
-            jnp.concatenate(parts, axis=1),
-            tokens[pl.ds(k * CHUNK, CHUNK), :],
-            preferred_element_type=jnp.float32,
+            jnp.concatenate(weights, axis=1), part, preferred_element_type=jnp.float32
         )
     mixed = codes[...].astype(jnp.float32) + assigned
     out[...] = mixed * lax.rsqrt(
@@ -186,6 +187,10 @@
 
 def in_vmem(array):
     return pltpu.with_memory_space_constraint(array, pltpu.VMEM)
+
+
+def in_hbm(array):
+    return pltpu.with_memory_space_constraint(array, pltpu.HBM)
 
 
 def call(kernel, out_shape, scratch=(), specs=None, out_specs=None, limit=24, elements=0, flops=0):
@@ -214,7 +219,7 @@
     elements = tok_rows * code_rows
     f32 = jnp.float32
     vmem = pl.BlockSpec(memory_space=pltpu.VMEM)
-    hbm = pl.BlockSpec(memory_space=pl.ANY)
+    hbm = pl.BlockSpec(memory_space=pltpu.HBM)
     resident = functools.partial(pltpu.VMEM, dtype=f32)
     to_tok = jax.ShapeDtypeStruct((tok_size, code_tiles, LANES), f32)
     to_code = jax.ShapeDtypeStruct((code_size, row_tiles, LANES), f32)
@@ -236,18 +241,21 @@
         specs=[vmem, hbm],
         elements=elements,
         flops=2 * elements * depth,
-    )(tokens, codebook)
+    )(tokens, in_hbm(codebook))
     for step in range(ITERS):
+        last = step == ITERS - 1
         received = exchange(copies, "tok")
-        copies, code_potential = call(
+        potential = pltpu.VMEM((code_tiles, LANES), f32)
+        row_partials = pltpu.VMEM((row_tiles, LANES), f32)
+        copies, *code_potential = call(
             functools.partial(rows_kernel, math.log2(total_codes)),
-            (to_code, jax.ShapeDtypeStruct((code_tiles, LANES), f32)),
-            [pltpu.VMEM((row_tiles, LANES), f32)],
+            (to_code, potential) if last else (to_code,),
+            [row_partials] if last else [potential, row_partials],
             specs=[vmem, vmem],
             elements=elements,
         )(received, in_vmem(scores))
         received = exchange(copies, "code")
-        if step < ITERS - 1:
+        if not last:
             copies = call(
                 functools.partial(columns_kernel, math.log2(total_tokens)),
                 to_tok,
@@ -255,25 +263,7 @@
                 specs=[vmem, vmem],
                 elements=elements,
             )(received, in_vmem(scores))
-
-    place = lax.axis_index("tok")
-    own_codes = lax.dynamic_slice_in_dim(codebook, place * share, share, 0)
-    share_tiles = share // LANES
-    own_potential = lax.dynamic_slice_in_dim(code_potential, place * share_tiles, share_tiles, 0)
-    own_scores, held_tokens = call(
-        functools.partial(own_scores_kernel, math.log2(total_tokens)),
-        (
-            pltpu.VMEM((share, total_tokens), f32),
-            pltpu.VMEM((total_tokens, depth), tokens.dtype),
-        ),
-        [
-            pltpu.VMEM((share, LANES), f32),
-            pltpu.SemaphoreType.DMA((total_tokens // CHUNK,)),
-        ],
-        specs=[vmem, vmem, hbm],
-        elements=elements,
-        flops=2 * elements * depth,
-    )(own_codes, own_potential, all_tokens)
+    (code_potential,) = code_potential
 
     copies = call(
         functools.partial(token_potential_kernel, math.log2(total_tokens)),
@@ -281,25 +271,35 @@
         specs=[vmem],
     )(received)
     all_potential = exchange(copies, "tok")
+    code_sems = pltpu.SemaphoreType.DMA((code_rows // CHUNK,))
     targets = call(
         functools.partial(targets_kernel, math.log2(total_tokens)),
         jax.ShapeDtypeStruct((tok_rows, code_rows), jnp.bfloat16),
         [
             column,
+            pltpu.VMEM((tok_rows, code_rows), f32),
             pltpu.VMEM((tok_rows, code_rows), jnp.bfloat16),
-            pltpu.SemaphoreType.DMA((code_rows // CHUNK,)),
+            code_sems,
+            code_sems,
         ],
-        specs=[vmem, vmem, vmem],
+        specs=[vmem, vmem, hbm],
         out_specs=hbm,
         elements=elements,
-    )(copies[0], code_potential, in_vmem(scores))
+    )(copies, code_potential, in_hbm(scores))
     updated_codebook = call(
-        refresh_kernel,
+        functools.partial(refresh_kernel, math.log2(total_tokens)),
         jax.ShapeDtypeStruct((share, depth), f32),
-        specs=[vmem, vmem, vmem, vmem],
+        [
+            pltpu.VMEM((total_tokens, depth), tokens.dtype),
+            pltpu.VMEM((share, depth), codebook.dtype),
+            pltpu.VMEM((share, LANES), f32),
+            pltpu.SemaphoreType.DMA((total_tokens // CHUNK,)),
+            pltpu.SemaphoreType.DMA,
+        ],
+        specs=[vmem, vmem, hbm, hbm],
         elements=elements,
-        flops=2 * elements * depth,
-    )(own_codes, all_potential, in_vmem(own_scores), in_vmem(held_tokens))
+        flops=4 * elements * depth,
+    )(code_potential, all_potential, in_hbm(codebook), in_hbm(all_tokens))
     return (targets, updated_codebook)
 
 

time: 142 us -> 127 us (0.89)
  blocking collectives: 58.4 us -> 80.2 us
  local copies, waits for them, and re-layouts: 19.7 us -> 0.95 us
  waiting for transfers between devices: 15.5 us -> 3 us
  starting transfers between devices: 11.6 us -> 3.53 us
  Pallas kernels: 22.4 us -> 25 us
    all_to_all x4 -> x6, blocking collectives: 58.4 us -> 80.2 us  [exchange(): return lax.all_to_all(copies, axis, 0, 0)]
    unnamed x20 -> x4, local copies, waits for them, and re-layouts: 18 us -> 0.95 us
    all_to_all x3 -> x1, waiting for transfers between devices: 14.8 us -> 2.31 us  [exchange(): return lax.all_to_all(copies, axis, 0, 0)]
    all_to_all x3 -> x1, starting transfers between devices: 11.5 us -> 3.49 us  [exchange(): return lax.all_to_all(copies, axis, 0, 0)]
    pallas_call x1, Pallas kernels: 1.55 us -> 4.05 us  [per_device(): call(functools.partial(targets_kernel, math.log2(total_tokens)), jax.Shap...]
    pallas_call x5 -> x4, Pallas kernels: 12.4 us -> 12.4 us  [the longest x1 6.83 us: per_device(): call(functools.partial(refresh_kernel, math.log2(total_tokens)), jax.Shap...]
  transfers between devices with their start and end apart: 4 -> 2, of which waited for: 2 -> 1; matrix products, arithmetic and copies ran while one was open for 1% -> 0% of each run, Pallas kernels for 14% -> 14%
where the time goes in v2:
time: 127 us
  blocking collectives  80.2 us (63%)
  Pallas kernels  25 us (20%)
  between operations  14.1 us (11%)
  starting transfers between devices  3.53 us (3%)
  waiting for transfers between devices  3 us (2%)
    all_to_all x6, blocking collectives, exchange(): return lax.all_to_all(copies, axis, 0, 0)  80.2 us
    pallas_call x1, Pallas kernels, per_device(): call(functools.partial(refresh_kernel, math.log2(total_tokens)), jax.Shap...  6.83 us
    pallas_call x3, Pallas kernels, per_device(): call(functools.partial(rows_kernel, math.log2(total_codes)), (to_code, po...  5.57 us
    pallas_call x1, Pallas kernels, per_device(): call(scores_kernel, (pltpu.VMEM((tok_rows, code_rows), f32), to_tok), [pl...  4.83 us
    pallas_call x1, Pallas kernels, per_device(): call(functools.partial(targets_kernel, math.log2(total_tokens)), jax.Shap...  4.05 us
    all_to_all x1, starting transfers between devices, exchange(): return lax.all_to_all(copies, axis, 0, 0)  3.49 us
    pallas_call x2, Pallas kernels, per_device(): call(functools.partial(columns_kernel, math.log2(total_tokens)), to_tok,...  3.1 us
  transfers between devices with their start and end apart: 2, of which 1 were waited for; matrix products, arithmetic and copies ran while one was open for 0% of the time, Pallas kernels for 14%

profile of v2, /device:TPU:1, one launch (start us, length us, event | category | flops | bytes accessed | tf_op | source)
XLA Modules:
  0.0 126.8 jit_solution(10291757631888690184)
XLA Ops:
  7.2 0.0 all-gather.2.cloned.1.call-start
  7.2 0.7 all-gather.2.cloned.1.call-update
  7.9 0.0 copy-start.1
  7.9 0.9 copy-done.1
  8.8 4.8 %shard_map.41 = (f32[256,4096]{1,0:T(8,128)S(1)}, f32[16,32,128]{2,1,0:T(8,128)S(1)}) custom-call(bf16[256,512]{1,0:T(8,128)(2,1)S(1)} %copy-done.1, bf16[4096,512]{1,0:T(8,128)(2,1)} %codebook.3), custom_call_target="tpu_custom_call" | custom-call | flops 1077936128 | bytes 4194304 | tf_op jit(solution)/shard_map/pallas_call | solution.py:233
  13.7 0.0 copy-start
  13.7 14.9 %all_to_all.35.received = f32[16,32,128]{2,1,0:T(8,128)S(1)} all-to-all(f32[16,32,128]{2,1,0:T(8,128)S(1)} %get-tuple-element.6), channel_id=1, replica_groups=mesh['tok'=16,'code'=16] {'tok'}, dimensions={0} | all-to-all | bytes 524288 | tf_op jit(solution)/shard_map/all_to_all | solution.py:229
  28.6 1.9 %shard_map.42 = f32[16,2,128]{2,1,0:T(2,128)S(1)} custom-call(f32[16,32,128]{2,1,0:T(8,128)S(1)} %all_to_all.35.received, f32[256,4096]{1,0:T(8,128)S(1)} %get-tuple-element.7.scores), custom_call_target="tpu_custom_call" | custom-call | flops 4194304 | bytes 4194304 | tf_op jit(solution)/shard_map/pallas_call | solution.py:250
  30.5 17.7 %all_to_all.36.received = f32[16,2,128]{2,1,0:T(2,128)S(1)} all-to-all(f32[16,2,128]{2,1,0:T(2,128)S(1)} %shard_map.42), channel_id=1, replica_groups=mesh['tok'=16,'code'=16] {'code'}, dimensions={0} | all-to-all | bytes 32768 | tf_op jit(solution)/shard_map/all_to_all | solution.py:229
  48.2 1.6 %shard_map.43 = f32[16,32,128]{2,1,0:T(8,128)S(1)} custom-call(f32[16,2,128]{2,1,0:T(2,128)S(1)} %all_to_all.36.received, f32[256,4096]{1,0:T(8,128)S(1)} %get-tuple-element.7.scores), custom_call_target="tpu_custom_call" | custom-call | flops 4194304 | bytes 4194304 | tf_op jit(solution)/shard_map/pallas_call | solution.py:259
  49.8 14.0 %all_to_all.37.received = f32[16,32,128]{2,1,0:T(8,128)S(1)} all-to-all(f32[16,32,128]{2,1,0:T(8,128)S(1)} %shard_map.43), channel_id=1, replica_groups=mesh['tok'=16,'code'=16] {'tok'}, dimensions={0} | all-to-all | bytes 524288 | tf_op jit(solution)/shard_map/all_to_all | solution.py:229
  63.7 1.9 %shard_map.44 = f32[16,2,128]{2,1,0:T(2,128)S(1)} custom-call(f32[16,32,128]{2,1,0:T(8,128)S(1)} %all_to_all.37.received, f32[256,4096]{1,0:T(8,128)S(1)} %get-tuple-element.7.scores), custom_call_target="tpu_custom_call" | custom-call | flops 4194304 | bytes 4194304 | tf_op jit(solution)/shard_map/pallas_call | solution.py:250
  65.6 11.6 %all_to_all.38.received = f32[16,2,128]{2,1,0:T(2,128)S(1)} all-to-all(f32[16,2,128]{2,1,0:T(2,128)S(1)} %shard_map.44), channel_id=1, replica_groups=mesh['tok'=16,'code'=16] {'code'}, dimensions={0} | all-to-all | bytes 32768 | tf_op jit(solution)/shard_map/all_to_all | solution.py:229
  77.2 1.6 %shard_map.45 = f32[16,32,128]{2,1,0:T(8,128)S(1)} custom-call(f32[16,2,128]{2,1,0:T(2,128)S(1)} %all_to_all.38.received, f32[256,4096]{1,0:T(8,128)S(1)} %get-tuple-element.7.scores), custom_call_target="tpu_custom_call" | custom-call | flops 4194304 | bytes 4194304 | tf_op jit(solution)/shard_map/pallas_call | solution.py:259
  78.7 11.0 %all_to_all.39.received = f32[16,32,128]{2,1,0:T(8,128)S(1)} all-to-all(f32[16,32,128]{2,1,0:T(8,128)S(1)} %shard_map.45), channel_id=1, replica_groups=mesh['tok'=16,'code'=16] {'tok'}, dimensions={0} | all-to-all | bytes 524288 | tf_op jit(solution)/shard_map/all_to_all | solution.py:229
  89.7 0.0 copy-done
  89.7 1.9 %shard_map.46 = (f32[16,2,128]{2,1,0:T(2,128)S(1)}, f32[32,128]{1,0:T(8,128)S(1)}) custom-call(f32[16,32,128]{2,1,0:T(8,128)S(1)} %all_to_all.39.received, f32[256,4096]{1,0:T(8,128)S(1)} %get-tuple-element.7.scores), custom_call_target="tpu_custom_call" | custom-call | flops 4194304 | bytes 4194304 | tf_op jit(solution)/shard_map/pallas_call | solution.py:250
  91.5 11.1 %all_to_all.40.received = f32[16,2,128]{2,1,0:T(2,128)S(1)} all-to-all(f32[16,2,128]{2,1,0:T(2,128)S(1)} %get-tuple-element.8), channel_id=1, replica_groups=mesh['tok'=16,'code'=16] {'code'}, dimensions={0} | all-to-all | bytes 32768 | tf_op jit(solution)/shard_map/all_to_all | solution.py:229
  102.6 0.7 shard_map.47.token_potential
  103.3 3.5 %all-to-all-start.6 = ((f32[16,2,128]{2,1,0:T(2,128)}), f32[16,2,128]{2,1,0:T(2,128)S(1)}, u32[]{:S(2)}, u32[]{:S(2)}) async-start(f32[16,2,128]{2,1,0:T(2,128)} %shard_map.47.token_potential), calls=%async_computation.6 | async-start | bytes 32768 | tf_op jit(solution)/shard_map/all_to_all | solution.py:229
  106.8 4.1 %shard_map.48 = bf16[256,4096]{1,0:T(8,128)(2,1)} custom-call(f32[16,2,128]{2,1,0:T(2,128)} %shard_map.47.token_potential, f32[32,128]{1,0:T(8,128)S(1)} %get-tuple-element.9.code_potential, f32[256,4096]{1,0:T(8,128)} %copy-done), custom_call_target="tpu_custom_call" | custom-call | flops 4194304 | bytes 4194304 | tf_op jit(solution)/shard_map/pallas_call | solution.py:275
  110.8 2.3 %all-to-all-done.6.potential = f32[16,2,128]{2,1,0:T(2,128)S(1)} async-done(((f32[16,2,128]{2,1,0:T(2,128)}), f32[16,2,128]{2,1,0:T(2,128)S(1)}, u32[]{:S(2)}, u32[]{:S(2)}) %all-to-all-start.6) | async-done | bytes 16416 | tf_op jit(solution)/shard_map/all_to_all | solution.py:229
  113.2 0.0 all-gather.2.cloned.1.call-done.tokens
  113.2 6.8 %shard_map.49 = f32[256,512]{1,0:T(8,128)} custom-call(f32[32,128]{1,0:T(8,128)S(1)} %get-tuple-element.9.code_potential, f32[16,2,128]{2,1,0:T(2,128)S(1)} %all-to-all-done.6.potential, bf16[4096,512]{1,0:T(8,128)(2,1)} %codebook.3, bf16[4096,512]{1,0:T(8,128)(2,1)} %all-gather.2.cloned.1.call-done.tokens), custom_call_target="tpu_custom_call" | custom-call | flops 2151677952 | bytes 4194304 | tf_op jit(solution)/shard_map/pallas_call | solution.py:289
Async XLA Ops:
  7.2 106.0 %all-gather.2.cloned.1.call-start = ((), (), s32[]{:S(2)}) async-start(), calls=%async_computation.7 | async-start | bytes 4456448 | tf_op jit(solution)/shard_map/all_gather | solution.py:231
  7.9 1.0 copy-start.1
  13.7 76.0 %copy-start = (f32[256,4096]{1,0:T(8,128)}, f32[256,4096]{1,0:T(8,128)S(1)}, u32[]{:S(2)}) copy-start(f32[256,4096]{1,0:T(8,128)S(1)} %get-tuple-element.7.scores) | copy-start | bytes 12582916
  103.3 9.9 %all-to-all-start.6 = ((f32[16,2,128]{2,1,0:T(2,128)}), f32[16,2,128]{2,1,0:T(2,128)S(1)}, u32[]{:S(2)}, u32[]{:S(2)}) async-start(f32[16,2,128]{2,1,0:T(2,128)} %shard_map.47.token_potential), calls=%async_computation.6 | async-start | bytes 32768 | tf_op jit(solution)/shard_map/all_to_all | solution.py:229
Sparse Core Ops, SparseCore 0:
  10.4 63.1 all-gather.1

commit v3 on v2

--- a/solution.py
+++ b/solution.py
@@ -16,6 +16,7 @@
 
 LANES = 128
 CHUNK = 512
+AHEAD = 3
 MIB = 1 << 20
 
 score_scale = sharpness_factor * math.log2(math.e)
@@ -52,6 +53,11 @@
         out[d] = local[...]
 
 
+def send_copies(local, out):
+    for d in range(out.shape[0]):
+        out[d] = local[...]
+
+
 def chunk_copies(source, held, sems, axis=0):
     copies = []
     for k in range(source.shape[axis] // CHUNK):
@@ -60,23 +66,30 @@
     return copies
 
 
-def scores_kernel(tokens, codebook, scores, out, held, local, sems):
+def scores_kernel(tokens, codebook, scores, out, held, rows, local, sems, rows_sem):
     copies = chunk_copies(codebook, held, sems)
-    for copy in copies:
+    rows_copy = pltpu.make_async_copy(tokens, rows, rows_sem)
+    rows_copy.start()
+    for copy in copies[:AHEAD]:
         copy.start()
-    for k in range(len(copies)):
-        copies[k].wait()
-        scores[:, pl.ds(k * CHUNK, CHUNK)] = (
-            lax.dot_general(
-                tokens[...],
-                held[pl.ds(k * CHUNK, CHUNK), :],
-                (((1,), (1,)), ((), ())),
-                preferred_element_type=jnp.float32,
+    rows_copy.wait()
+    for k in range(len(copies) + 1):
+        if k < len(copies):
+            copies[k].wait()
+            if k + AHEAD < len(copies):
+                copies[k + AHEAD].start()
+            scores[:, pl.ds(k * CHUNK, CHUNK)] = (
+                lax.dot_general(
+                    rows[...],
+                    held[pl.ds(k * CHUNK, CHUNK), :],
+                    (((1,), (1,)), ((), ())),
+                    preferred_element_type=jnp.float32,
+                )
+                * score_scale
             )
-            * score_scale
-        )
-        for j in range(k * CHUNK // LANES, (k + 1) * CHUNK // LANES):
-            local[pl.ds(j, 1), :] = column_lse(scores, None, j)
+        if k > 0:
+            for j in range((k - 1) * CHUNK // LANES, k * CHUNK // LANES):
+                local[pl.ds(j, 1), :] = column_lse(scores, None, j)
     send_copies(local, out)
 
 
@@ -89,34 +102,38 @@
         local[pl.ds(k, 1), :] = column_lse(scores, column, k)
         return carry
 
-    lax.fori_loop(0, local.shape[0], step, 0, unroll=4)
+    lax.fori_loop(0, local.shape[0], step, 0, unroll=8)
     send_copies(local, out)
 
 
-def rows_kernel(shift, received, scores, out, potential, local):
+def rows_kernel(shift, received, scores, out, potential):
     potential[...] = -shift - lse2(received[...], 0)
     tiles = potential.shape[0]
-    for h in range(local.shape[0]):
+    partials = []
+    for h in range(out.shape[1]):
         rows = pl.ds(h * LANES, LANES)
 
         def values(k):
             return scores[rows, tile(k)] + potential[pl.ds(k, 1), :]
 
         top = lax.fori_loop(
-            0, tiles, lambda k, top: jnp.maximum(top, values(k)), values(0), unroll=4
+            0, tiles, lambda k, top: jnp.maximum(top, values(k)), values(0), unroll=8
         )
         total = lax.fori_loop(
             0,
             tiles,
             lambda k, total: total + jnp.exp2(values(k) - top),
             jnp.zeros((LANES, LANES), jnp.float32),
-            unroll=4,
+            unroll=8,
         )
+        partials.append((top, total))
+    for h, (top, total) in enumerate(partials):
         top = top.T
         most = jnp.max(top, axis=0, keepdims=True)
         total = jnp.sum(total.T * jnp.exp2(top - most), axis=0, keepdims=True)
-        local[pl.ds(h, 1), :] = most + jnp.log2(total)
-    send_copies(local, out)
+        local = most + jnp.log2(total)
+        for d in range(out.shape[0]):
+            out[d, pl.ds(h, 1), :] = local
 
 
 def token_potential_kernel(shift, received, out):
@@ -145,40 +162,51 @@
         copy.wait()
 
 
+def own_code_copy(codebook, codes, sem):
+    share = codes.shape[0]
+    start = pl.multiple_of(lax.axis_index("tok") * share, share)
+    return pltpu.make_async_copy(codebook.at[pl.ds(start, share)], codes, sem)
+
+
 def refresh_kernel(
     scale, code_potential, potential, codebook, tokens, out, held, codes, column, sems, own_sem
 ):
+    own = own_code_copy(codebook, codes, own_sem)
     copies = chunk_copies(tokens, held, sems)
-    share, halves = codes.shape[0], potential.shape[1]
-    place = lax.axis_index("tok")
-    own_rows = pl.ds(pl.multiple_of(place * share, share), share)
-    own = pltpu.make_async_copy(codebook.at[own_rows], codes, own_sem)
     own.start()
-    for copy in copies:
+    for copy in copies[:AHEAD]:
         copy.start()
-    for h in range(share // LANES):
-        row = code_potential[pl.ds(place * (share // LANES) + h, 1), :]
+    halves, tiles = potential.shape[1], codes.shape[0] // LANES
+    for h in range(tiles):
+        row = code_potential[pl.ds(lax.axis_index("tok") * tiles + h, 1), :]
         column[pl.ds(h * LANES, LANES), :] = as_column(row) + scale
     own.wait()
+
+    def part(k):
+        return held[pl.ds(k * CHUNK, CHUNK), :]
+
+    def chunk_scores(k):
+        copies[k].wait()
+        if k + AHEAD < len(copies):
+            copies[k + AHEAD].start()
+        return lax.dot_general(
+            codes[...], part(k), (((1,), (1,)), ((), ())), preferred_element_type=jnp.float32
+        )
+
     assigned = jnp.zeros(out.shape, jnp.float32)
+    scores = chunk_scores(0)
     for k in range(len(copies)):
-        copies[k].wait()
-        part = held[pl.ds(k * CHUNK, CHUNK), :]
-        scores = (
-            lax.dot_general(
-                codes[...], part, (((1,), (1,)), ((), ())), preferred_element_type=jnp.float32
-            )
-            * score_scale
-        )
+        ahead = chunk_scores(k + 1) if k + 1 < len(copies) else None
         weights = []
         for j in range(CHUNK // LANES):
             at = k * CHUNK // LANES + j
             row = potential[at // halves, pl.ds(at % halves, 1), :]
-            values = scores[:, j * LANES : (j + 1) * LANES] + column[...] + row
-            weights.append(jnp.exp2(values).astype(part.dtype))
+            values = scores[:, j * LANES : (j + 1) * LANES] * score_scale + column[...] + row
+            weights.append(jnp.exp2(values).astype(held.dtype))
         assigned += jnp.dot(
-            jnp.concatenate(weights, axis=1), part, preferred_element_type=jnp.float32
+            jnp.concatenate(weights, axis=1), part(k), preferred_element_type=jnp.float32
         )
+        scores = ahead
     mixed = codes[...].astype(jnp.float32) + assigned
     out[...] = mixed * lax.rsqrt(
         jnp.mean(mixed * mixed, axis=1, keepdims=True) + rms_epsilon
@@ -220,7 +248,6 @@
     f32 = jnp.float32
     vmem = pl.BlockSpec(memory_space=pltpu.VMEM)
     hbm = pl.BlockSpec(memory_space=pltpu.HBM)
-    resident = functools.partial(pltpu.VMEM, dtype=f32)
     to_tok = jax.ShapeDtypeStruct((tok_size, code_tiles, LANES), f32)
     to_code = jax.ShapeDtypeStruct((code_size, row_tiles, LANES), f32)
     column = pltpu.VMEM((tok_rows, LANES), f32)
@@ -235,31 +262,31 @@
         (pltpu.VMEM((tok_rows, code_rows), f32), to_tok),
         [
             pltpu.VMEM((code_rows, depth), codebook.dtype),
+            pltpu.VMEM((tok_rows, depth), tokens.dtype),
             pltpu.VMEM((code_tiles, LANES), f32),
             pltpu.SemaphoreType.DMA((code_rows // CHUNK,)),
+            pltpu.SemaphoreType.DMA,
         ],
-        specs=[vmem, hbm],
+        specs=[hbm, hbm],
         elements=elements,
         flops=2 * elements * depth,
-    )(tokens, in_hbm(codebook))
+    )(in_hbm(tokens), in_hbm(codebook))
     for step in range(ITERS):
         last = step == ITERS - 1
-        received = exchange(copies, "tok")
         potential = pltpu.VMEM((code_tiles, LANES), f32)
-        row_partials = pltpu.VMEM((row_tiles, LANES), f32)
         copies, *code_potential = call(
             functools.partial(rows_kernel, math.log2(total_codes)),
             (to_code, potential) if last else (to_code,),
-            [row_partials] if last else [potential, row_partials],
+            [] if last else [potential],
             specs=[vmem, vmem],
             elements=elements,
-        )(received, in_vmem(scores))
+        )(exchange(copies, "tok"), in_vmem(scores))
         received = exchange(copies, "code")
         if not last:
             copies = call(
                 functools.partial(columns_kernel, math.log2(total_tokens)),
                 to_tok,
-                [column, pltpu.VMEM((code_tiles, LANES), f32)],
+                [column, potential],
                 specs=[vmem, vmem],
                 elements=elements,
             )(received, in_vmem(scores))

time: 127 us -> 124 us (0.976)
  Pallas kernels: 25 us -> 22.7 us
where the time goes in v3:
time: 124 us; the launch traced here: 123 us
  blocking collectives  80.2 us (65%)
  Pallas kernels  22.7 us (18%)
  between operations  14.1 us (11%)
  starting transfers between devices  3.53 us (3%)
  waiting for transfers between devices  3 us (2%)
    all_to_all x6, blocking collectives, exchange(): return lax.all_to_all(copies, axis, 0, 0)  80.2 us
    pallas_call x1, Pallas kernels, per_device(): call(functools.partial(refresh_kernel, math.log2(total_tokens)), jax.Shap...  5.59 us
    pallas_call x3, Pallas kernels, per_device(): call(functools.partial(rows_kernel, math.log2(total_codes)), (to_code, po...  5.19 us
    pallas_call x1, Pallas kernels, per_device(): call(scores_kernel, (pltpu.VMEM((tok_rows, code_rows), f32), to_tok), [pl...  4.46 us
    pallas_call x1, Pallas kernels, per_device(): call(functools.partial(targets_kernel, math.log2(total_tokens)), jax.Shap...  4.05 us
    all_to_all x1, starting transfers between devices, exchange(): return lax.all_to_all(copies, axis, 0, 0)  3.49 us
    pallas_call x2, Pallas kernels, per_device(): call(functools.partial(columns_kernel, math.log2(total_tokens)), to_tok,...  2.73 us
  transfers between devices with their start and end apart: 2, of which 1 were waited for; matrix products, arithmetic and copies ran while one was open for 0% of the time, Pallas kernels for 14%

profile of v3, /device:TPU:1, one launch (start us, length us, event | category | flops | bytes accessed | tf_op | source)
XLA Modules:
  0.0 123.5 jit_solution(10946919518205657325)
XLA Ops:
  7.2 0.0 all-gather.2.cloned.1.call-start
  7.2 0.7 all-gather.2.cloned.1.call-update
  7.9 4.5 %shard_map.41 = (f32[256,4096]{1,0:T(8,128)S(1)}, f32[16,32,128]{2,1,0:T(8,128)S(1)}) custom-call(bf16[256,512]{1,0:T(8,128)(2,1)} %tokens.1, bf16[4096,512]{1,0:T(8,128)(2,1)} %codebook.3), custom_call_target="tpu_custom_call" | custom-call | flops 1077936128 | bytes 4194304 | tf_op jit(solution)/shard_map/pallas_call | solution.py:260
  12.4 0.0 copy-start
  12.4 14.9 %all_to_all.35.received = f32[16,32,128]{2,1,0:T(8,128)S(1)} all-to-all(f32[16,32,128]{2,1,0:T(8,128)S(1)} %get-tuple-element.6), channel_id=1, replica_groups=mesh['tok'=16,'code'=16] {'tok'}, dimensions={0} | all-to-all | bytes 524288 | tf_op jit(solution)/shard_map/all_to_all | solution.py:256
  27.3 1.7 %shard_map.42 = f32[16,2,128]{2,1,0:T(2,128)S(1)} custom-call(f32[16,32,128]{2,1,0:T(8,128)S(1)} %all_to_all.35.received, f32[256,4096]{1,0:T(8,128)S(1)} %get-tuple-element.7.scores), custom_call_target="tpu_custom_call" | custom-call | flops 4194304 | bytes 4194304 | tf_op jit(solution)/shard_map/pallas_call | solution.py:277
  29.0 17.7 %all_to_all.36.received = f32[16,2,128]{2,1,0:T(2,128)S(1)} all-to-all(f32[16,2,128]{2,1,0:T(2,128)S(1)} %shard_map.42), channel_id=1, replica_groups=mesh['tok'=16,'code'=16] {'code'}, dimensions={0} | all-to-all | bytes 32768 | tf_op jit(solution)/shard_map/all_to_all | solution.py:256
  46.7 1.4 %shard_map.43 = f32[16,32,128]{2,1,0:T(8,128)S(1)} custom-call(f32[16,2,128]{2,1,0:T(2,128)S(1)} %all_to_all.36.received, f32[256,4096]{1,0:T(8,128)S(1)} %get-tuple-element.7.scores), custom_call_target="tpu_custom_call" | custom-call | flops 4194304 | bytes 4194304 | tf_op jit(solution)/shard_map/pallas_call | solution.py:286
  48.1 13.6 %all_to_all.37.received = f32[16,32,128]{2,1,0:T(8,128)S(1)} all-to-all(f32[16,32,128]{2,1,0:T(8,128)S(1)} %shard_map.43), channel_id=1, replica_groups=mesh['tok'=16,'code'=16] {'tok'}, dimensions={0} | all-to-all | bytes 524288 | tf_op jit(solution)/shard_map/all_to_all | solution.py:256
  61.7 1.7 %shard_map.44 = f32[16,2,128]{2,1,0:T(2,128)S(1)} custom-call(f32[16,32,128]{2,1,0:T(8,128)S(1)} %all_to_all.37.received, f32[256,4096]{1,0:T(8,128)S(1)} %get-tuple-element.7.scores), custom_call_target="tpu_custom_call" | custom-call | flops 4194304 | bytes 4194304 | tf_op jit(solution)/shard_map/pallas_call | solution.py:277
  63.5 11.9 %all_to_all.38.received = f32[16,2,128]{2,1,0:T(2,128)S(1)} all-to-all(f32[16,2,128]{2,1,0:T(2,128)S(1)} %shard_map.44), channel_id=1, replica_groups=mesh['tok'=16,'code'=16] {'code'}, dimensions={0} | all-to-all | bytes 32768 | tf_op jit(solution)/shard_map/all_to_all | solution.py:256
  75.4 1.4 %shard_map.45 = f32[16,32,128]{2,1,0:T(8,128)S(1)} custom-call(f32[16,2,128]{2,1,0:T(2,128)S(1)} %all_to_all.38.received, f32[256,4096]{1,0:T(8,128)S(1)} %get-tuple-element.7.scores), custom_call_target="tpu_custom_call" | custom-call | flops 4194304 | bytes 4194304 | tf_op jit(solution)/shard_map/pallas_call | solution.py:286
  76.7 11.0 %all_to_all.39.received = f32[16,32,128]{2,1,0:T(8,128)S(1)} all-to-all(f32[16,32,128]{2,1,0:T(8,128)S(1)} %shard_map.45), channel_id=1, replica_groups=mesh['tok'=16,'code'=16] {'tok'}, dimensions={0} | all-to-all | bytes 524288 | tf_op jit(solution)/shard_map/all_to_all | solution.py:256
  87.7 0.0 copy-done
  87.7 1.7 %shard_map.46 = (f32[16,2,128]{2,1,0:T(2,128)S(1)}, f32[32,128]{1,0:T(8,128)S(1)}) custom-call(f32[16,32,128]{2,1,0:T(8,128)S(1)} %all_to_all.39.received, f32[256,4096]{1,0:T(8,128)S(1)} %get-tuple-element.7.scores), custom_call_target="tpu_custom_call" | custom-call | flops 4194304 | bytes 4194304 | tf_op jit(solution)/shard_map/pallas_call | solution.py:277
  89.4 11.1 %all_to_all.40.received = f32[16,2,128]{2,1,0:T(2,128)S(1)} all-to-all(f32[16,2,128]{2,1,0:T(2,128)S(1)} %get-tuple-element.8), channel_id=1, replica_groups=mesh['tok'=16,'code'=16] {'code'}, dimensions={0} | all-to-all | bytes 32768 | tf_op jit(solution)/shard_map/all_to_all | solution.py:256
  100.5 0.7 shard_map.47.token_potential
  101.1 3.5 %all-to-all-start.6 = ((f32[16,2,128]{2,1,0:T(2,128)}), f32[16,2,128]{2,1,0:T(2,128)S(1)}, u32[]{:S(2)}, u32[]{:S(2)}) async-start(f32[16,2,128]{2,1,0:T(2,128)} %shard_map.47.token_potential), calls=%async_computation.6 | async-start | bytes 32768 | tf_op jit(solution)/shard_map/all_to_all | solution.py:256
  104.6 4.1 %shard_map.48 = bf16[256,4096]{1,0:T(8,128)(2,1)} custom-call(f32[16,2,128]{2,1,0:T(2,128)} %shard_map.47.token_potential, f32[32,128]{1,0:T(8,128)S(1)} %get-tuple-element.9.code_potential, f32[256,4096]{1,0:T(8,128)} %copy-done), custom_call_target="tpu_custom_call" | custom-call | flops 4194304 | bytes 4194304 | tf_op jit(solution)/shard_map/pallas_call | solution.py:302
  108.7 2.3 %all-to-all-done.6.potential = f32[16,2,128]{2,1,0:T(2,128)S(1)} async-done(((f32[16,2,128]{2,1,0:T(2,128)}), f32[16,2,128]{2,1,0:T(2,128)S(1)}, u32[]{:S(2)}, u32[]{:S(2)}) %all-to-all-start.6) | async-done | bytes 16416 | tf_op jit(solution)/shard_map/all_to_all | solution.py:256
  111.0 0.0 all-gather.2.cloned.1.call-done.tokens
  111.0 5.6 %shard_map.49 = f32[256,512]{1,0:T(8,128)} custom-call(f32[32,128]{1,0:T(8,128)S(1)} %get-tuple-element.9.code_potential, f32[16,2,128]{2,1,0:T(2,128)S(1)} %all-to-all-done.6.potential, bf16[4096,512]{1,0:T(8,128)(2,1)} %codebook.3, bf16[4096,512]{1,0:T(8,128)(2,1)} %all-gather.2.cloned.1.call-done.tokens), custom_call_target="tpu_custom_call" | custom-call | flops 2151677952 | bytes 4194304 | tf_op jit(solution)/shard_map/pallas_call | solution.py:316
Async XLA Ops:
  7.2 103.9 %all-gather.2.cloned.1.call-start = ((), (), s32[]{:S(2)}) async-start(), calls=%async_computation.7 | async-start | bytes 4456448 | tf_op jit(solution)/shard_map/all_gather | solution.py:258
  12.4 75.3 %copy-start = (f32[256,4096]{1,0:T(8,128)}, f32[256,4096]{1,0:T(8,128)S(1)}, u32[]{:S(2)}) copy-start(f32[256,4096]{1,0:T(8,128)S(1)} %get-tuple-element.7.scores) | copy-start | bytes 12582916
  101.1 9.9 %all-to-all-start.6 = ((f32[16,2,128]{2,1,0:T(2,128)}), f32[16,2,128]{2,1,0:T(2,128)S(1)}, u32[]{:S(2)}, u32[]{:S(2)}) async-start(f32[16,2,128]{2,1,0:T(2,128)} %shard_map.47.token_potential), calls=%async_computation.6 | async-start | bytes 32768 | tf_op jit(solution)/shard_map/all_to_all | solution.py:256
Sparse Core Ops, SparseCore 0:
  10.4 63.1 all-gather.1

commit v4 on v3

--- a/solution.py
+++ b/solution.py
@@ -15,8 +15,8 @@
 rms_epsilon = 1e-06
 
 LANES = 128
-CHUNK = 512
-AHEAD = 3
+CHUNK = 1024
+AHEAD = 2
 MIB = 1 << 20
 
 score_scale = sharpness_factor * math.log2(math.e)
@@ -136,30 +136,13 @@
             out[d, pl.ds(h, 1), :] = local
 
 
-def token_potential_kernel(shift, received, out):
-    potential = -shift - lse2(received[...], 0)
-    for d in range(out.shape[0]):
-        out[d] = potential
-
-
-def targets_kernel(
-    scale, token_potential, code_potential, scores, out, column, panel, held, sems, out_sems
-):
-    copies = chunk_copies(scores, panel, sems, 1)
-    for copy in copies:
-        copy.start()
-    for h in range(token_potential.shape[1]):
-        column[pl.ds(h * LANES, LANES), :] = as_column(token_potential[0, pl.ds(h, 1), :]) + scale
-    out_copies = chunk_copies(held, out, out_sems, 1)
-    for k in range(len(copies)):
-        copies[k].wait()
-        for j in range(k * CHUNK // LANES, (k + 1) * CHUNK // LANES):
-            held[:, tile(j)] = jnp.exp2(
-                panel[:, tile(j)] + column[...] + code_potential[pl.ds(j, 1), :]
-            ).astype(held.dtype)
-        out_copies[k].start()
-    for copy in out_copies:
-        copy.wait()
+def last_rows_kernel(shift, received, scores, tokens, out, potential, first_tokens, sem):
+    copy = pltpu.make_async_copy(
+        tokens.at[pl.ds(0, first_tokens.shape[0])], first_tokens, sem
+    )
+    copy.start()
+    rows_kernel(shift, received, scores, out, potential)
+    copy.wait()
 
 
 def own_code_copy(codebook, codes, sem):
@@ -168,45 +151,69 @@
     return pltpu.make_async_copy(codebook.at[pl.ds(start, share)], codes, sem)
 
 
-def refresh_kernel(
-    scale, code_potential, potential, codebook, tokens, out, held, codes, column, sems, own_sem
+def targets_kernel(
+    scale, received, code_potential, scores, codebook, tokens, first_tokens,
+    out, targets, own_scores, last_tokens,
+    panel, column, own_column, codes, own_sem, sems, out_sems,
 ):
     own = own_code_copy(codebook, codes, own_sem)
-    copies = chunk_copies(tokens, held, sems)
     own.start()
-    for copy in copies[:AHEAD]:
+    first = first_tokens.shape[0]
+    copies = chunk_copies(tokens.at[pl.ds(first, last_tokens.shape[0])], last_tokens, sems)
+    for copy in copies:
         copy.start()
-    halves, tiles = potential.shape[1], codes.shape[0] // LANES
+    potential = -scale - lse2(received[...], 0)
+    for d in range(out.shape[0]):
+        out[d] = potential
+    tiles = codes.shape[0] // LANES
     for h in range(tiles):
         row = code_potential[pl.ds(lax.axis_index("tok") * tiles + h, 1), :]
-        column[pl.ds(h * LANES, LANES), :] = as_column(row) + scale
+        own_column[pl.ds(h * LANES, LANES), :] = as_column(row) + scale
+    for h in range(potential.shape[0]):
+        column[pl.ds(h * LANES, LANES), :] = as_column(potential[h : h + 1, :]) + scale
     own.wait()
-
-    def part(k):
-        return held[pl.ds(k * CHUNK, CHUNK), :]
-
-    def chunk_scores(k):
-        copies[k].wait()
-        if k + AHEAD < len(copies):
-            copies[k + AHEAD].start()
-        return lax.dot_general(
-            codes[...], part(k), (((1,), (1,)), ((), ())), preferred_element_type=jnp.float32
+    out_copies = chunk_copies(panel, targets, out_sems, 1)
+    for k in range(len(out_copies)):
+        if k * CHUNK < first:
+            part = first_tokens[pl.ds(k * CHUNK, CHUNK), :]
+        else:
+            copies[k - first // CHUNK].wait()
+            part = last_tokens[pl.ds(k * CHUNK - first, CHUNK), :]
+        values = lax.dot_general(
+            codes[...], part, (((1,), (1,)), ((), ())), preferred_element_type=jnp.float32
         )
-
-    assigned = jnp.zeros(out.shape, jnp.float32)
-    scores = chunk_scores(0)
-    for k in range(len(copies)):
-        ahead = chunk_scores(k + 1) if k + 1 < len(copies) else None
-        weights = []
         for j in range(CHUNK // LANES):
             at = k * CHUNK // LANES + j
-            row = potential[at // halves, pl.ds(at % halves, 1), :]
-            values = scores[:, j * LANES : (j + 1) * LANES] * score_scale + column[...] + row
-            weights.append(jnp.exp2(values).astype(held.dtype))
-        assigned += jnp.dot(
-            jnp.concatenate(weights, axis=1), part(k), preferred_element_type=jnp.float32
-        )
-        scores = ahead
+            panel[:, tile(at)] = jnp.exp2(
+                scores[:, tile(at)] + column[...] + code_potential[pl.ds(at, 1), :]
+            ).astype(panel.dtype)
+            own_scores[:, tile(at)] = (
+                values[:, j * LANES : (j + 1) * LANES] * score_scale + own_column[...]
+            )
+        out_copies[k].start()
+    for copy in out_copies:
+        copy.wait()
+
+
+def refresh_kernel(potential, codebook, scores, first_tokens, last_tokens, out, codes, own_sem):
+    own = own_code_copy(codebook, codes, own_sem)
+    own.start()
+    halves = potential.shape[1]
+    assigned = jnp.zeros(out.shape, jnp.float32)
+    at = 0
+    for tokens in (first_tokens, last_tokens):
+        for k in range(tokens.shape[0] // CHUNK):
+            weights = []
+            for j in range(CHUNK // LANES):
+                row = potential[at // halves, pl.ds(at % halves, 1), :]
+                weights.append(jnp.exp2(scores[:, tile(at)] + row).astype(tokens.dtype))
+                at += 1
+            assigned += jnp.dot(
+                jnp.concatenate(weights, axis=1),
+                tokens[pl.ds(k * CHUNK, CHUNK), :],
+                preferred_element_type=jnp.float32,
+            )
+    own.wait()
     mixed = codes[...].astype(jnp.float32) + assigned
     out[...] = mixed * lax.rsqrt(
         jnp.mean(mixed * mixed, axis=1, keepdims=True) + rms_epsilon
@@ -271,18 +278,19 @@
         elements=elements,
         flops=2 * elements * depth,
     )(in_hbm(tokens), in_hbm(codebook))
+    potential = pltpu.VMEM((code_tiles, LANES), f32)
+    half_tokens = pltpu.VMEM((total_tokens // 2, depth), tokens.dtype)
     for step in range(ITERS):
-        last = step == ITERS - 1
-        potential = pltpu.VMEM((code_tiles, LANES), f32)
-        copies, *code_potential = call(
-            functools.partial(rows_kernel, math.log2(total_codes)),
-            (to_code, potential) if last else (to_code,),
-            [] if last else [potential],
-            specs=[vmem, vmem],
-            elements=elements,
-        )(exchange(copies, "tok"), in_vmem(scores))
-        received = exchange(copies, "code")
-        if not last:
+        received = exchange(copies, "tok")
+        if step < ITERS - 1:
+            copies = call(
+                functools.partial(rows_kernel, math.log2(total_codes)),
+                to_code,
+                [potential],
+                specs=[vmem, vmem],
+                elements=elements,
+            )(received, in_vmem(scores))
+            received = exchange(copies, "code")
             copies = call(
                 functools.partial(columns_kernel, math.log2(total_tokens)),
                 to_tok,
@@ -290,43 +298,61 @@
                 specs=[vmem, vmem],
                 elements=elements,
             )(received, in_vmem(scores))
-    (code_potential,) = code_potential
-
-    copies = call(
-        functools.partial(token_potential_kernel, math.log2(total_tokens)),
-        jax.ShapeDtypeStruct((tok_size, row_tiles, LANES), f32),
-        specs=[vmem],
-    )(received)
+        else:
+            copies, code_potential, first_tokens = call(
+                functools.partial(last_rows_kernel, math.log2(total_codes)),
+                (to_code, potential, half_tokens),
+                [pltpu.SemaphoreType.DMA],
+                specs=[vmem, vmem, hbm],
+                elements=elements,
+            )(received, in_vmem(scores), in_hbm(all_tokens))
+            received = exchange(copies, "code")
+
+    held_codes = pltpu.VMEM((share, depth), codebook.dtype)
+    copies, targets, own_scores, last_tokens = call(
+        functools.partial(targets_kernel, math.log2(total_tokens)),
+        (
+            jax.ShapeDtypeStruct((tok_size, row_tiles, LANES), f32),
+            jax.ShapeDtypeStruct((tok_rows, code_rows), jnp.bfloat16),
+            pltpu.VMEM((share, total_tokens), f32),
+            half_tokens,
+        ),
+        [
+            pltpu.VMEM((tok_rows, code_rows), jnp.bfloat16),
+            column,
+            pltpu.VMEM((share, LANES), f32),
+            held_codes,
+            pltpu.SemaphoreType.DMA,
+            pltpu.SemaphoreType.DMA((total_tokens // 2 // CHUNK,)),
+            pltpu.SemaphoreType.DMA((code_rows // CHUNK,)),
+        ],
+        specs=[vmem, vmem, vmem, hbm, hbm, vmem],
+        out_specs=(vmem, hbm, vmem, vmem),
+        elements=2 * elements,
+        flops=2 * elements * depth,
+    )(
+        received,
+        in_vmem(code_potential),
+        in_vmem(scores),
+        in_hbm(codebook),
+        in_hbm(all_tokens),
+        in_vmem(first_tokens),
+    )
     all_potential = exchange(copies, "tok")
-    code_sems = pltpu.SemaphoreType.DMA((code_rows // CHUNK,))
-    targets = call(
-        functools.partial(targets_kernel, math.log2(total_tokens)),
-        jax.ShapeDtypeStruct((tok_rows, code_rows), jnp.bfloat16),
-        [
-            column,
-            pltpu.VMEM((tok_rows, code_rows), f32),
-            pltpu.VMEM((tok_rows, code_rows), jnp.bfloat16),
-            code_sems,
-            code_sems,
-        ],
-        specs=[vmem, vmem, hbm],
-        out_specs=hbm,
+    updated_codebook = call(
+        refresh_kernel,
+        jax.ShapeDtypeStruct((share, depth), f32),
+        [held_codes, pltpu.SemaphoreType.DMA],
+        specs=[vmem, hbm, vmem, vmem, vmem],
         elements=elements,
-    )(copies, code_potential, in_hbm(scores))
-    updated_codebook = call(
-        functools.partial(refresh_kernel, math.log2(total_tokens)),
-        jax.ShapeDtypeStruct((share, depth), f32),
-        [
-            pltpu.VMEM((total_tokens, depth), tokens.dtype),
-            pltpu.VMEM((share, depth), codebook.dtype),
-            pltpu.VMEM((share, LANES), f32),
-            pltpu.SemaphoreType.DMA((total_tokens // CHUNK,)),
-            pltpu.SemaphoreType.DMA,
-        ],
-        specs=[vmem, vmem, hbm, hbm],
-        elements=elements,
-        flops=4 * elements * depth,
-    )(code_potential, all_potential, in_hbm(codebook), in_hbm(all_tokens))
+        flops=2 * elements * depth,
+    )(
+        all_potential,
+        in_hbm(codebook),
+        in_vmem(own_scores),
+        in_vmem(first_tokens),
+        in_vmem(last_tokens),
+    )
     return (targets, updated_codebook)
 
 

time: 124 us -> 126 us (1.016)
  blocking collectives: 80.2 us -> 89.1 us
  Pallas kernels: 22.7 us -> 19.2 us
  starting transfers between devices: 3.53 us -> 0.04 us
  waiting for transfers between devices: 3 us -> 0.68 us
  local copies, waits for them, and re-layouts: 0.01 us -> 2.19 us
    all_to_all x6 -> x7, blocking collectives: 80.2 us -> 89.1 us  [exchange(): return lax.all_to_all(copies, axis, 0, 0)]
    all_to_all x1 -> x0, starting transfers between devices: 3.49 us -> none  [exchange(): return lax.all_to_all(copies, axis, 0, 0)]
    pallas_call x6 -> x5, Pallas kernels: 15.5 us -> 12.7 us  [the longest x1 4.5 us: per_device(): call(functools.partial(targets_kernel, math.log2(total_tokens)), (jax.Sha...]
    all_to_all x1 -> x0, waiting for transfers between devices: 2.31 us -> none  [exchange(): return lax.all_to_all(copies, axis, 0, 0)]
    unnamed x2 -> x4, local copies, waits for them, and re-layouts: 0.01 us -> 2.19 us
  transfers between devices with their start and end apart: 2 -> 1, of which waited for: 1 -> 0; matrix products, arithmetic and copies ran while one was open for 0% -> 0% of each run, Pallas kernels for 14% -> 8%
where the time goes in v4:
time: 126 us; the launch traced here: 125 us
  blocking collectives  89.1 us (71%)
  Pallas kernels  19.2 us (15%)
  between operations  14.1 us (11%)
  local copies, waits for them, and re-layouts  2.19 us (2%)
    all_to_all x7, blocking collectives, exchange(): return lax.all_to_all(copies, axis, 0, 0)  89.1 us
    pallas_call x1, Pallas kernels, per_device(): call(functools.partial(targets_kernel, math.log2(total_tokens)), (jax.Sha...  4.5 us
    pallas_call x1, Pallas kernels, per_device(): call(scores_kernel, (pltpu.VMEM((tok_rows, code_rows), f32), to_tok), [pl...  3.78 us
    pallas_call x2, Pallas kernels, per_device(): call(functools.partial(rows_kernel, math.log2(total_codes)), to_code, [po...  3.45 us
    pallas_call x1, Pallas kernels, per_device(): call(refresh_kernel, jax.ShapeDtypeStruct((share, depth), f32), [held_cod...  3.03 us
    pallas_call x2, Pallas kernels, per_device(): call(functools.partial(columns_kernel, math.log2(total_tokens)), to_tok,...  2.73 us
  transfers between devices with their start and end apart: 1, of which 0 were waited for; matrix products, arithmetic and copies ran while one was open for 0% of the time, Pallas kernels for 8%

profile of v4, /device:TPU:1, one launch (start us, length us, event | category | flops | bytes accessed | tf_op | source)
XLA Modules:
  0.0 125.3 jit_solution(11245109964474429753)
XLA Ops:
  7.2 0.0 all-gather.2.cloned.1.call-start
  7.2 0.7 all-gather.2.cloned.1.call-update
  7.9 3.8 %shard_map.41 = (f32[256,4096]{1,0:T(8,128)S(1)}, f32[16,32,128]{2,1,0:T(8,128)S(1)}) custom-call(bf16[256,512]{1,0:T(8,128)(2,1)} %tokens.1, bf16[4096,512]{1,0:T(8,128)(2,1)} %codebook.5), custom_call_target="tpu_custom_call" | custom-call | flops 1077936128 | bytes 4194304 | tf_op jit(solution)/shard_map/pallas_call | solution.py:267
  11.7 0.0 copy-start
  11.7 14.9 %all_to_all.35.received = f32[16,32,128]{2,1,0:T(8,128)S(1)} all-to-all(f32[16,32,128]{2,1,0:T(8,128)S(1)} %get-tuple-element.11), channel_id=1, replica_groups=mesh['tok'=16,'code'=16] {'tok'}, dimensions={0} | all-to-all | bytes 524288 | tf_op jit(solution)/shard_map/all_to_all | solution.py:263
  26.6 1.7 %shard_map.42 = f32[16,2,128]{2,1,0:T(2,128)S(1)} custom-call(f32[16,32,128]{2,1,0:T(8,128)S(1)} %all_to_all.35.received, f32[256,4096]{1,0:T(8,128)S(1)} %get-tuple-element.12.scores), custom_call_target="tpu_custom_call" | custom-call | flops 4194304 | bytes 4194304 | tf_op jit(solution)/shard_map/pallas_call | solution.py:286
  28.4 17.7 %all_to_all.36.received = f32[16,2,128]{2,1,0:T(2,128)S(1)} all-to-all(f32[16,2,128]{2,1,0:T(2,128)S(1)} %shard_map.42), channel_id=1, replica_groups=mesh['tok'=16,'code'=16] {'code'}, dimensions={0} | all-to-all | bytes 32768 | tf_op jit(solution)/shard_map/all_to_all | solution.py:263
  46.1 1.4 %shard_map.43 = f32[16,32,128]{2,1,0:T(8,128)S(1)} custom-call(f32[16,2,128]{2,1,0:T(2,128)S(1)} %all_to_all.36.received, f32[256,4096]{1,0:T(8,128)S(1)} %get-tuple-element.12.scores), custom_call_target="tpu_custom_call" | custom-call | flops 4194304 | bytes 4194304 | tf_op jit(solution)/shard_map/pallas_call | solution.py:294
  47.4 13.8 %all_to_all.37.received = f32[16,32,128]{2,1,0:T(8,128)S(1)} all-to-all(f32[16,32,128]{2,1,0:T(8,128)S(1)} %shard_map.43), channel_id=1, replica_groups=mesh['tok'=16,'code'=16] {'tok'}, dimensions={0} | all-to-all | bytes 524288 | tf_op jit(solution)/shard_map/all_to_all | solution.py:263
  61.3 1.7 %shard_map.44 = f32[16,2,128]{2,1,0:T(2,128)S(1)} custom-call(f32[16,32,128]{2,1,0:T(8,128)S(1)} %all_to_all.37.received, f32[256,4096]{1,0:T(8,128)S(1)} %get-tuple-element.12.scores), custom_call_target="tpu_custom_call" | custom-call | flops 4194304 | bytes 4194304 | tf_op jit(solution)/shard_map/pallas_call | solution.py:286
  63.0 11.5 %all_to_all.38.received = f32[16,2,128]{2,1,0:T(2,128)S(1)} all-to-all(f32[16,2,128]{2,1,0:T(2,128)S(1)} %shard_map.44), channel_id=1, replica_groups=mesh['tok'=16,'code'=16] {'code'}, dimensions={0} | all-to-all | bytes 32768 | tf_op jit(solution)/shard_map/all_to_all | solution.py:263
  74.5 0.0 copy-done
  74.5 1.4 %shard_map.45 = f32[16,32,128]{2,1,0:T(8,128)S(1)} custom-call(f32[16,2,128]{2,1,0:T(2,128)S(1)} %all_to_all.38.received, f32[256,4096]{1,0:T(8,128)S(1)} %get-tuple-element.12.scores), custom_call_target="tpu_custom_call" | custom-call | flops 4194304 | bytes 4194304 | tf_op jit(solution)/shard_map/pallas_call | solution.py:294
  75.9 11.0 %all_to_all.39.received = f32[16,32,128]{2,1,0:T(8,128)S(1)} all-to-all(f32[16,32,128]{2,1,0:T(8,128)S(1)} %shard_map.45), channel_id=1, replica_groups=mesh['tok'=16,'code'=16] {'tok'}, dimensions={0} | all-to-all | bytes 524288 | tf_op jit(solution)/shard_map/all_to_all | solution.py:263
  86.9 0.0 all-gather.2.cloned.1.call-done.tokens
  86.9 0.0 copy-start.1
  86.9 2.2 %copy-done.1 = f32[256,4096]{1,0:T(8,128)S(1)} copy-done((f32[256,4096]{1,0:T(8,128)S(1)}, f32[256,4096]{1,0:T(8,128)}, u32[]{:S(2)}) %copy-start.1) | copy-done | bytes 4194328
  89.1 1.7 %shard_map.46 = (f32[16,2,128]{2,1,0:T(2,128)S(1)}, f32[32,128]{1,0:T(8,128)S(1)}, bf16[2048,512]{1,0:T(8,128)(2,1)S(1)}) custom-call(f32[16,32,128]{2,1,0:T(8,128)S(1)} %all_to_all.39.received, f32[256,4096]{1,0:T(8,128)S(1)} %copy-done.1, bf16[4096,512]{1,0:T(8,128)(2,1)} %all-gather.2.cloned.1.call-done.tokens), custom_call_target="tpu_custom_call" | custom-call | flops 4194304 | bytes 4194304 | tf_op jit(solution)/shard_map/pallas_call | solution.py:302
  90.8 11.1 %all_to_all.40.received = f32[16,2,128]{2,1,0:T(2,128)S(1)} all-to-all(f32[16,2,128]{2,1,0:T(2,128)S(1)} %get-tuple-element.13), channel_id=1, replica_groups=mesh['tok'=16,'code'=16] {'code'}, dimensions={0} | all-to-all | bytes 32768 | tf_op jit(solution)/shard_map/all_to_all | solution.py:263
  101.9 4.5 %shard_map.47 = (f32[16,2,128]{2,1,0:T(2,128)S(1)}, bf16[256,4096]{1,0:T(8,128)(2,1)}, f32[256,4096]{1,0:T(8,128)S(1)}, bf16[2048,512]{1,0:T(8,128)(2,1)S(1)}) custom-call(f32[16,2,128]{2,1,0:T(2,128)S(1)} %all_to_all.40.received, f32[32,128]{1,0:T(8,128)S(1)} %get-tuple-element.14.code_potential, f32[256,4096]{1,0:T(8,128)S(1)} %copy-done.1, ...), custom_call_target="tpu_custom_call" | custom-call | flops 1082130432 | bytes 8388608 | tf_op jit(solution)/shard_map/pallas_call | solution.py:312
  106.4 9.1 %all_to_all.41.potential = f32[16,2,128]{2,1,0:T(2,128)S(1)} all-to-all(f32[16,2,128]{2,1,0:T(2,128)S(1)} %get-tuple-element.17), channel_id=1, replica_groups=mesh['tok'=16,'code'=16] {'tok'}, dimensions={0} | all-to-all | bytes 32768 | tf_op jit(solution)/shard_map/all_to_all | solution.py:263
  115.5 3.0 %shard_map.48 = f32[256,512]{1,0:T(8,128)} custom-call(f32[16,2,128]{2,1,0:T(2,128)S(1)} %all_to_all.41.potential, bf16[4096,512]{1,0:T(8,128)(2,1)} %codebook.5, f32[256,4096]{1,0:T(8,128)S(1)} %get-tuple-element.18.scores, bf16[2048,512]{1,0:T(8,128)(2,1)S(1)} %get-tuple-element.15.first_tokens, bf16[2048,512]{1,0:T(8,128)(2,1)S(1)} %get-tuple-element.19.last_tokens), custom_call_target="tpu_custom_call" | custom-call | flops 1077936128 | bytes 4194304 | tf_op jit(solution)/shard_map/pallas_call | solution.py:342
Async XLA Ops:
  7.2 79.7 %all-gather.2.cloned.1.call-start = ((), (), s32[]{:S(2)}) async-start(), calls=%async_computation.7 | async-start | bytes 4456448 | tf_op jit(solution)/shard_map/all_gather | solution.py:265
  11.7 62.9 %copy-start = (f32[256,4096]{1,0:T(8,128)}, f32[256,4096]{1,0:T(8,128)S(1)}, u32[]{:S(2)}) copy-start(f32[256,4096]{1,0:T(8,128)S(1)} %get-tuple-element.12.scores) | copy-start | bytes 12582916
  86.9 2.2 %copy-start.1 = (f32[256,4096]{1,0:T(8,128)S(1)}, f32[256,4096]{1,0:T(8,128)}, u32[]{:S(2)}) copy-start(f32[256,4096]{1,0:T(8,128)} %copy-done) | copy-start | bytes 12582916
Sparse Core Ops, SparseCore 0:
  10.4 63.1 all-gather.1

commit v5 on v3

--- a/solution.py
+++ b/solution.py
@@ -17,6 +17,8 @@
 LANES = 128
 CHUNK = 512
 AHEAD = 3
+CODE_CHUNK = 1024
+CODE_AHEAD = 2
 MIB = 1 << 20
 
 score_scale = sharpness_factor * math.log2(math.e)
@@ -58,37 +60,37 @@
         out[d] = local[...]
 
 
-def chunk_copies(source, held, sems, axis=0):
+def chunk_copies(source, held, sems, axis=0, size=CHUNK):
     copies = []
-    for k in range(source.shape[axis] // CHUNK):
-        part = (slice(None),) * axis + (pl.ds(k * CHUNK, CHUNK),)
+    for k in range(source.shape[axis] // size):
+        part = (slice(None),) * axis + (pl.ds(k * size, size),)
         copies.append(pltpu.make_async_copy(source.at[part], held.at[part], sems.at[k]))
     return copies
 
 
+def scores_of(left, right):
+    return lax.dot_general(
+        left, right, (((1,), (1,)), ((), ())), preferred_element_type=jnp.float32
+    ).T
+
+
 def scores_kernel(tokens, codebook, scores, out, held, rows, local, sems, rows_sem):
-    copies = chunk_copies(codebook, held, sems)
+    size = CODE_CHUNK
+    copies = chunk_copies(codebook, held, sems, 0, size)
     rows_copy = pltpu.make_async_copy(tokens, rows, rows_sem)
     rows_copy.start()
-    for copy in copies[:AHEAD]:
+    for copy in copies[:CODE_AHEAD]:
         copy.start()
     rows_copy.wait()
     for k in range(len(copies) + 1):
         if k < len(copies):
             copies[k].wait()
-            if k + AHEAD < len(copies):
-                copies[k + AHEAD].start()
-            scores[:, pl.ds(k * CHUNK, CHUNK)] = (
-                lax.dot_general(
-                    rows[...],
-                    held[pl.ds(k * CHUNK, CHUNK), :],
-                    (((1,), (1,)), ((), ())),
-                    preferred_element_type=jnp.float32,
-                )
-                * score_scale
-            )
+            if k + CODE_AHEAD < len(copies):
+                copies[k + CODE_AHEAD].start()
+            part = pl.ds(k * size, size)
+            scores[:, part] = scores_of(held[part, :], rows[...]) * score_scale
         if k > 0:
-            for j in range((k - 1) * CHUNK // LANES, k * CHUNK // LANES):
+            for j in range((k - 1) * size // LANES, k * size // LANES):
                 local[pl.ds(j, 1), :] = column_lse(scores, None, j)
     send_copies(local, out)
 
@@ -189,9 +191,7 @@
         copies[k].wait()
         if k + AHEAD < len(copies):
             copies[k + AHEAD].start()
-        return lax.dot_general(
-            codes[...], part(k), (((1,), (1,)), ((), ())), preferred_element_type=jnp.float32
-        )
+        return scores_of(part(k), codes[...])
 
     assigned = jnp.zeros(out.shape, jnp.float32)
     scores = chunk_scores(0)
@@ -264,7 +264,7 @@
             pltpu.VMEM((code_rows, depth), codebook.dtype),
             pltpu.VMEM((tok_rows, depth), tokens.dtype),
             pltpu.VMEM((code_tiles, LANES), f32),
-            pltpu.SemaphoreType.DMA((code_rows // CHUNK,)),
+            pltpu.SemaphoreType.DMA((code_rows // CODE_CHUNK,)),
             pltpu.SemaphoreType.DMA,
         ],
         specs=[hbm, hbm],

time: 124 us -> 125 us (level)
  Pallas kernels: 22.7 us -> 24.1 us
    pallas_call x1, Pallas kernels: 5.59 us -> 6.85 us  [per_device(): call(functools.partial(refresh_kernel, math.log2(total_tokens)), jax.Shap...]
where the time goes in v5:
time: 125 us
  blocking collectives  80.2 us (64%)
  Pallas kernels  24.1 us (19%)
  between operations  14.1 us (11%)
  starting transfers between devices  3.53 us (3%)
  waiting for transfers between devices  3 us (2%)
    all_to_all x6, blocking collectives, exchange(): return lax.all_to_all(copies, axis, 0, 0)  80.2 us
    pallas_call x1, Pallas kernels, per_device(): call(functools.partial(refresh_kernel, math.log2(total_tokens)), jax.Shap...  6.85 us
    pallas_call x3, Pallas kernels, per_device(): call(functools.partial(rows_kernel, math.log2(total_codes)), (to_code, po...  5.19 us
    pallas_call x1, Pallas kernels, per_device(): call(scores_kernel, (pltpu.VMEM((tok_rows, code_rows), f32), to_tok), [pl...  4.67 us
    pallas_call x1, Pallas kernels, per_device(): call(functools.partial(targets_kernel, math.log2(total_tokens)), jax.Shap...  4.05 us
    all_to_all x1, starting transfers between devices, exchange(): return lax.all_to_all(copies, axis, 0, 0)  3.49 us
    pallas_call x2, Pallas kernels, per_device(): call(functools.partial(columns_kernel, math.log2(total_tokens)), to_tok,...  2.73 us
  transfers between devices with their start and end apart: 2, of which 1 were waited for; matrix products, arithmetic and copies ran while one was open for 0% of the time, Pallas kernels for 14%

profile of v5, /device:TPU:1, one launch (start us, length us, event | category | flops | bytes accessed | tf_op | source)
XLA Modules:
  0.0 125.0 jit_solution(14236893870556262194)
XLA Ops:
  7.2 0.0 all-gather.2.cloned.1.call-start
  7.2 0.7 all-gather.2.cloned.1.call-update
  7.9 4.7 %shard_map.41 = (f32[256,4096]{1,0:T(8,128)S(1)}, f32[16,32,128]{2,1,0:T(8,128)S(1)}) custom-call(bf16[256,512]{1,0:T(8,128)(2,1)} %tokens.1, bf16[4096,512]{1,0:T(8,128)(2,1)} %codebook.3), custom_call_target="tpu_custom_call" | custom-call | flops 1077936128 | bytes 4194304 | tf_op jit(solution)/shard_map/pallas_call | solution.py:260
  12.6 0.0 copy-start
  12.6 14.9 %all_to_all.35.received = f32[16,32,128]{2,1,0:T(8,128)S(1)} all-to-all(f32[16,32,128]{2,1,0:T(8,128)S(1)} %get-tuple-element.6), channel_id=1, replica_groups=mesh['tok'=16,'code'=16] {'tok'}, dimensions={0} | all-to-all | bytes 524288 | tf_op jit(solution)/shard_map/all_to_all | solution.py:256
  27.5 1.7 %shard_map.42 = f32[16,2,128]{2,1,0:T(2,128)S(1)} custom-call(f32[16,32,128]{2,1,0:T(8,128)S(1)} %all_to_all.35.received, f32[256,4096]{1,0:T(8,128)S(1)} %get-tuple-element.7.scores), custom_call_target="tpu_custom_call" | custom-call | flops 4194304 | bytes 4194304 | tf_op jit(solution)/shard_map/pallas_call | solution.py:277
  29.3 17.7 %all_to_all.36.received = f32[16,2,128]{2,1,0:T(2,128)S(1)} all-to-all(f32[16,2,128]{2,1,0:T(2,128)S(1)} %shard_map.42), channel_id=1, replica_groups=mesh['tok'=16,'code'=16] {'code'}, dimensions={0} | all-to-all | bytes 32768 | tf_op jit(solution)/shard_map/all_to_all | solution.py:256
  47.0 1.4 %shard_map.43 = f32[16,32,128]{2,1,0:T(8,128)S(1)} custom-call(f32[16,2,128]{2,1,0:T(2,128)S(1)} %all_to_all.36.received, f32[256,4096]{1,0:T(8,128)S(1)} %get-tuple-element.7.scores), custom_call_target="tpu_custom_call" | custom-call | flops 4194304 | bytes 4194304 | tf_op jit(solution)/shard_map/pallas_call | solution.py:286
  48.3 13.7 %all_to_all.37.received = f32[16,32,128]{2,1,0:T(8,128)S(1)} all-to-all(f32[16,32,128]{2,1,0:T(8,128)S(1)} %shard_map.43), channel_id=1, replica_groups=mesh['tok'=16,'code'=16] {'tok'}, dimensions={0} | all-to-all | bytes 524288 | tf_op jit(solution)/shard_map/all_to_all | solution.py:256
  62.0 1.7 %shard_map.44 = f32[16,2,128]{2,1,0:T(2,128)S(1)} custom-call(f32[16,32,128]{2,1,0:T(8,128)S(1)} %all_to_all.37.received, f32[256,4096]{1,0:T(8,128)S(1)} %get-tuple-element.7.scores), custom_call_target="tpu_custom_call" | custom-call | flops 4194304 | bytes 4194304 | tf_op jit(solution)/shard_map/pallas_call | solution.py:277
  63.8 11.8 %all_to_all.38.received = f32[16,2,128]{2,1,0:T(2,128)S(1)} all-to-all(f32[16,2,128]{2,1,0:T(2,128)S(1)} %shard_map.44), channel_id=1, replica_groups=mesh['tok'=16,'code'=16] {'code'}, dimensions={0} | all-to-all | bytes 32768 | tf_op jit(solution)/shard_map/all_to_all | solution.py:256
  75.6 1.4 %shard_map.45 = f32[16,32,128]{2,1,0:T(8,128)S(1)} custom-call(f32[16,2,128]{2,1,0:T(2,128)S(1)} %all_to_all.38.received, f32[256,4096]{1,0:T(8,128)S(1)} %get-tuple-element.7.scores), custom_call_target="tpu_custom_call" | custom-call | flops 4194304 | bytes 4194304 | tf_op jit(solution)/shard_map/pallas_call | solution.py:286
  77.0 11.0 %all_to_all.39.received = f32[16,32,128]{2,1,0:T(8,128)S(1)} all-to-all(f32[16,32,128]{2,1,0:T(8,128)S(1)} %shard_map.45), channel_id=1, replica_groups=mesh['tok'=16,'code'=16] {'tok'}, dimensions={0} | all-to-all | bytes 524288 | tf_op jit(solution)/shard_map/all_to_all | solution.py:256
  87.9 0.0 copy-done
  87.9 1.7 %shard_map.46 = (f32[16,2,128]{2,1,0:T(2,128)S(1)}, f32[32,128]{1,0:T(8,128)S(1)}) custom-call(f32[16,32,128]{2,1,0:T(8,128)S(1)} %all_to_all.39.received, f32[256,4096]{1,0:T(8,128)S(1)} %get-tuple-element.7.scores), custom_call_target="tpu_custom_call" | custom-call | flops 4194304 | bytes 4194304 | tf_op jit(solution)/shard_map/pallas_call | solution.py:277
  89.7 11.1 %all_to_all.40.received = f32[16,2,128]{2,1,0:T(2,128)S(1)} all-to-all(f32[16,2,128]{2,1,0:T(2,128)S(1)} %get-tuple-element.8), channel_id=1, replica_groups=mesh['tok'=16,'code'=16] {'code'}, dimensions={0} | all-to-all | bytes 32768 | tf_op jit(solution)/shard_map/all_to_all | solution.py:256
  100.7 0.7 shard_map.47.token_potential
  101.4 3.5 %all-to-all-start.6 = ((f32[16,2,128]{2,1,0:T(2,128)}), f32[16,2,128]{2,1,0:T(2,128)S(1)}, u32[]{:S(2)}, u32[]{:S(2)}) async-start(f32[16,2,128]{2,1,0:T(2,128)} %shard_map.47.token_potential), calls=%async_computation.6 | async-start | bytes 32768 | tf_op jit(solution)/shard_map/all_to_all | solution.py:256
  104.9 4.1 %shard_map.48 = bf16[256,4096]{1,0:T(8,128)(2,1)} custom-call(f32[16,2,128]{2,1,0:T(2,128)} %shard_map.47.token_potential, f32[32,128]{1,0:T(8,128)S(1)} %get-tuple-element.9.code_potential, f32[256,4096]{1,0:T(8,128)} %copy-done), custom_call_target="tpu_custom_call" | custom-call | flops 4194304 | bytes 4194304 | tf_op jit(solution)/shard_map/pallas_call | solution.py:302
  108.9 2.3 %all-to-all-done.6.potential = f32[16,2,128]{2,1,0:T(2,128)S(1)} async-done(((f32[16,2,128]{2,1,0:T(2,128)}), f32[16,2,128]{2,1,0:T(2,128)S(1)}, u32[]{:S(2)}, u32[]{:S(2)}) %all-to-all-start.6) | async-done | bytes 16416 | tf_op jit(solution)/shard_map/all_to_all | solution.py:256
  111.3 0.0 all-gather.2.cloned.1.call-done.tokens
  111.3 6.8 %shard_map.49 = f32[256,512]{1,0:T(8,128)} custom-call(f32[32,128]{1,0:T(8,128)S(1)} %get-tuple-element.9.code_potential, f32[16,2,128]{2,1,0:T(2,128)S(1)} %all-to-all-done.6.potential, bf16[4096,512]{1,0:T(8,128)(2,1)} %codebook.3, bf16[4096,512]{1,0:T(8,128)(2,1)} %all-gather.2.cloned.1.call-done.tokens), custom_call_target="tpu_custom_call" | custom-call | flops 2151677952 | bytes 4194304 | tf_op jit(solution)/shard_map/pallas_call | solution.py:316
Async XLA Ops:
  7.2 104.1 %all-gather.2.cloned.1.call-start = ((), (), s32[]{:S(2)}) async-start(), calls=%async_computation.7 | async-start | bytes 4456448 | tf_op jit(solution)/shard_map/all_gather | solution.py:258
  12.6 75.3 %copy-start = (f32[256,4096]{1,0:T(8,128)}, f32[256,4096]{1,0:T(8,128)S(1)}, u32[]{:S(2)}) copy-start(f32[256,4096]{1,0:T(8,128)S(1)} %get-tuple-element.7.scores) | copy-start | bytes 12582916
  101.4 9.9 %all-to-all-start.6 = ((f32[16,2,128]{2,1,0:T(2,128)}), f32[16,2,128]{2,1,0:T(2,128)S(1)}, u32[]{:S(2)}, u32[]{:S(2)}) async-start(f32[16,2,128]{2,1,0:T(2,128)} %shard_map.47.token_potential), calls=%async_computation.6 | async-start | bytes 32768 | tf_op jit(solution)/shard_map/all_to_all | solution.py:256
Sparse Core Ops, SparseCore 0:
  10.4 63.1 all-gather.1

commit v6 on v3

--- a/solution.py
+++ b/solution.py
@@ -15,8 +15,9 @@
 rms_epsilon = 1e-06
 
 LANES = 128
-CHUNK = 512
-AHEAD = 3
+CHUNK = 1024
+DOT_CHUNK = 512
+AHEAD = 2
 MIB = 1 << 20
 
 score_scale = sharpness_factor * math.log2(math.e)
@@ -169,7 +170,8 @@
 
 
 def refresh_kernel(
-    scale, code_potential, potential, codebook, tokens, out, held, codes, column, sems, own_sem
+    scale, code_potential, potential, codebook, tokens,
+    out, held, codes, column, panel, sems, own_sem,
 ):
     own = own_code_copy(codebook, codes, own_sem)
     copies = chunk_copies(tokens, held, sems)
@@ -182,31 +184,38 @@
         column[pl.ds(h * LANES, LANES), :] = as_column(row) + scale
     own.wait()
 
-    def part(k):
-        return held[pl.ds(k * CHUNK, CHUNK), :]
-
     def chunk_scores(k):
         copies[k].wait()
         if k + AHEAD < len(copies):
             copies[k + AHEAD].start()
-        return lax.dot_general(
-            codes[...], part(k), (((1,), (1,)), ((), ())), preferred_element_type=jnp.float32
+        part = pl.ds(k * CHUNK, CHUNK)
+        panel[:, part] = (
+            lax.dot_general(
+                codes[...],
+                held[part, :],
+                (((1,), (1,)), ((), ())),
+                preferred_element_type=jnp.float32,
+            )
+            * score_scale
         )
 
     assigned = jnp.zeros(out.shape, jnp.float32)
-    scores = chunk_scores(0)
+    chunk_scores(0)
     for k in range(len(copies)):
-        ahead = chunk_scores(k + 1) if k + 1 < len(copies) else None
-        weights = []
-        for j in range(CHUNK // LANES):
-            at = k * CHUNK // LANES + j
-            row = potential[at // halves, pl.ds(at % halves, 1), :]
-            values = scores[:, j * LANES : (j + 1) * LANES] * score_scale + column[...] + row
-            weights.append(jnp.exp2(values).astype(held.dtype))
-        assigned += jnp.dot(
-            jnp.concatenate(weights, axis=1), part(k), preferred_element_type=jnp.float32
-        )
-        scores = ahead
+        if k + 1 < len(copies):
+            chunk_scores(k + 1)
+        for start in range(k * CHUNK, (k + 1) * CHUNK, DOT_CHUNK):
+            weights = []
+            for j in range(start // LANES, (start + DOT_CHUNK) // LANES):
+                row = potential[j // halves, pl.ds(j % halves, 1), :]
+                weights.append(
+                    jnp.exp2(panel[:, tile(j)] + column[...] + row).astype(held.dtype)
+                )
+            assigned += jnp.dot(
+                jnp.concatenate(weights, axis=1),
+                held[pl.ds(start, DOT_CHUNK), :],
+                preferred_element_type=jnp.float32,
+            )
     mixed = codes[...].astype(jnp.float32) + assigned
     out[...] = mixed * lax.rsqrt(
         jnp.mean(mixed * mixed, axis=1, keepdims=True) + rms_epsilon
@@ -255,8 +264,6 @@
     def exchange(copies, axis):
         return lax.all_to_all(copies, axis, 0, 0)
 
-    all_tokens = lax.all_gather(tokens, "tok", axis=0, tiled=True)
-
     scores, copies = call(
         scores_kernel,
         (pltpu.VMEM((tok_rows, code_rows), f32), to_tok),
@@ -271,6 +278,8 @@
         elements=elements,
         flops=2 * elements * depth,
     )(in_hbm(tokens), in_hbm(codebook))
+    copies, own_tokens = lax.optimization_barrier((copies, tokens))
+    all_tokens = lax.all_gather(own_tokens, "tok", axis=0, tiled=True)
     for step in range(ITERS):
         last = step == ITERS - 1
         potential = pltpu.VMEM((code_tiles, LANES), f32)
@@ -320,6 +329,7 @@
             pltpu.VMEM((total_tokens, depth), tokens.dtype),
             pltpu.VMEM((share, depth), codebook.dtype),
             pltpu.VMEM((share, LANES), f32),
+            pltpu.VMEM((share, total_tokens), f32),
             pltpu.SemaphoreType.DMA((total_tokens // CHUNK,)),
             pltpu.SemaphoreType.DMA,
         ],

time: 124 us -> 127 us (1.024)
  local copies, waits for them, and re-layouts: 0.01 us -> 4.32 us
    unnamed x2 -> x4, local copies, waits for them, and re-layouts: 0.01 us -> 4.32 us
  transfers between devices with their start and end apart: 2 -> 2, of which waited for: 1 -> 1; matrix products, arithmetic and copies ran while one was open for 0% -> 0% of each run, Pallas kernels for 14% -> 10%
where the time goes in v6:
time: 127 us; the launch traced here: 126 us
  blocking collectives  80.1 us (63%)
  Pallas kernels  21.6 us (17%)
  between operations  14.1 us (11%)
  local copies, waits for them, and re-layouts  4.32 us (3%)
  starting transfers between devices  3.53 us (3%)
  waiting for transfers between devices  2.4 us (2%)
    all_to_all x6, blocking collectives, exchange(): return lax.all_to_all(copies, axis, 0, 0)  80.1 us
    pallas_call x1, Pallas kernels, per_device(): call(functools.partial(refresh_kernel, math.log2(total_tokens)), jax.Shap...  5.23 us
    pallas_call x3, Pallas kernels, per_device(): call(functools.partial(rows_kernel, math.log2(total_codes)), (to_code, po...  5.18 us
    unnamed x4, local copies, waits for them, and re-layouts  4.32 us
    pallas_call x1, Pallas kernels, per_device(): call(functools.partial(targets_kernel, math.log2(total_tokens)), jax.Shap...  3.98 us
    pallas_call x1, Pallas kernels, per_device(): call(scores_kernel, (pltpu.VMEM((tok_rows, code_rows), f32), to_tok), [pl...  3.78 us
    all_to_all x1, starting transfers between devices, exchange(): return lax.all_to_all(copies, axis, 0, 0)  3.49 us
    pallas_call x2, Pallas kernels, per_device(): call(functools.partial(columns_kernel, math.log2(total_tokens)), to_tok,...  2.73 us
  transfers between devices with their start and end apart: 2, of which 1 were waited for; matrix products, arithmetic and copies ran while one was open for 0% of the time, Pallas kernels for 10%

profile of v6, /device:TPU:1, one launch (start us, length us, event | category | flops | bytes accessed | tf_op | source)
XLA Modules:
  0.0 126.0 jit_solution(12158064251337209145)
XLA Ops:
  7.2 0.0 all-gather.2.cloned.1.call-start
  7.2 3.8 %shard_map.41 = (f32[256,4096]{1,0:T(8,128)S(1)}, f32[16,32,128]{2,1,0:T(8,128)S(1)}) custom-call(bf16[256,512]{1,0:T(8,128)(2,1)} %tokens.1, bf16[4096,512]{1,0:T(8,128)(2,1)} %codebook.3), custom_call_target="tpu_custom_call" | custom-call | flops 1077936128 | bytes 4194304 | tf_op jit(solution)/shard_map/pallas_call | solution.py:267
  11.0 0.0 copy-start
  11.0 2.0 %copy-done = f32[256,4096]{1,0:T(8,128)} copy-done((f32[256,4096]{1,0:T(8,128)}, f32[256,4096]{1,0:T(8,128)S(1)}, u32[]{:S(2)}) %copy-start) | copy-done | bytes 4194328
  13.0 0.0 all-gather.2.cloned.1.call-update
  13.0 14.9 %all_to_all.35.received = f32[16,32,128]{2,1,0:T(8,128)S(1)} all-to-all(f32[16,32,128]{2,1,0:T(8,128)S(1)} %get-tuple-element.9), channel_id=1, replica_groups=mesh['tok'=16,'code'=16] {'tok'}, dimensions={0} | all-to-all | bytes 524288 | tf_op jit(solution)/shard_map/all_to_all | solution.py:265
  27.9 0.0 copy-start.1
  27.9 2.3 %copy-done.1 = f32[256,4096]{1,0:T(8,128)S(1)} copy-done((f32[256,4096]{1,0:T(8,128)S(1)}, f32[256,4096]{1,0:T(8,128)}, u32[]{:S(2)}) %copy-start.1) | copy-done | bytes 4194328
  30.3 1.7 %shard_map.42 = f32[16,2,128]{2,1,0:T(2,128)S(1)} custom-call(f32[16,32,128]{2,1,0:T(8,128)S(1)} %all_to_all.35.received, f32[256,4096]{1,0:T(8,128)S(1)} %copy-done.1), custom_call_target="tpu_custom_call" | custom-call | flops 4194304 | bytes 4194304 | tf_op jit(solution)/shard_map/pallas_call | solution.py:286
  32.0 17.5 %all_to_all.36.received = f32[16,2,128]{2,1,0:T(2,128)S(1)} all-to-all(f32[16,2,128]{2,1,0:T(2,128)S(1)} %shard_map.42), channel_id=1, replica_groups=mesh['tok'=16,'code'=16] {'code'}, dimensions={0} | all-to-all | bytes 32768 | tf_op jit(solution)/shard_map/all_to_all | solution.py:265
  49.6 1.4 %shard_map.43 = f32[16,32,128]{2,1,0:T(8,128)S(1)} custom-call(f32[16,2,128]{2,1,0:T(2,128)S(1)} %all_to_all.36.received, f32[256,4096]{1,0:T(8,128)S(1)} %copy-done.1), custom_call_target="tpu_custom_call" | custom-call | flops 4194304 | bytes 4194304 | tf_op jit(solution)/shard_map/pallas_call | solution.py:295
  50.9 13.7 %all_to_all.37.received = f32[16,32,128]{2,1,0:T(8,128)S(1)} all-to-all(f32[16,32,128]{2,1,0:T(8,128)S(1)} %shard_map.43), channel_id=1, replica_groups=mesh['tok'=16,'code'=16] {'tok'}, dimensions={0} | all-to-all | bytes 524288 | tf_op jit(solution)/shard_map/all_to_all | solution.py:265
  64.7 1.7 %shard_map.44 = f32[16,2,128]{2,1,0:T(2,128)S(1)} custom-call(f32[16,32,128]{2,1,0:T(8,128)S(1)} %all_to_all.37.received, f32[256,4096]{1,0:T(8,128)S(1)} %copy-done.1), custom_call_target="tpu_custom_call" | custom-call | flops 4194304 | bytes 4194304 | tf_op jit(solution)/shard_map/pallas_call | solution.py:286
  66.4 11.8 %all_to_all.38.received = f32[16,2,128]{2,1,0:T(2,128)S(1)} all-to-all(f32[16,2,128]{2,1,0:T(2,128)S(1)} %shard_map.44), channel_id=1, replica_groups=mesh['tok'=16,'code'=16] {'code'}, dimensions={0} | all-to-all | bytes 32768 | tf_op jit(solution)/shard_map/all_to_all | solution.py:265
  78.3 1.4 %shard_map.45 = f32[16,32,128]{2,1,0:T(8,128)S(1)} custom-call(f32[16,2,128]{2,1,0:T(2,128)S(1)} %all_to_all.38.received, f32[256,4096]{1,0:T(8,128)S(1)} %copy-done.1), custom_call_target="tpu_custom_call" | custom-call | flops 4194304 | bytes 4194304 | tf_op jit(solution)/shard_map/pallas_call | solution.py:295
  79.6 11.0 %all_to_all.39.received = f32[16,32,128]{2,1,0:T(8,128)S(1)} all-to-all(f32[16,32,128]{2,1,0:T(8,128)S(1)} %shard_map.45), channel_id=1, replica_groups=mesh['tok'=16,'code'=16] {'tok'}, dimensions={0} | all-to-all | bytes 524288 | tf_op jit(solution)/shard_map/all_to_all | solution.py:265
  90.6 1.7 %shard_map.46 = (f32[16,2,128]{2,1,0:T(2,128)S(1)}, f32[32,128]{1,0:T(8,128)S(1)}) custom-call(f32[16,32,128]{2,1,0:T(8,128)S(1)} %all_to_all.39.received, f32[256,4096]{1,0:T(8,128)S(1)} %copy-done.1), custom_call_target="tpu_custom_call" | custom-call | flops 4194304 | bytes 4194304 | tf_op jit(solution)/shard_map/pallas_call | solution.py:286
  92.3 11.1 %all_to_all.40.received = f32[16,2,128]{2,1,0:T(2,128)S(1)} all-to-all(f32[16,2,128]{2,1,0:T(2,128)S(1)} %get-tuple-element.11), channel_id=1, replica_groups=mesh['tok'=16,'code'=16] {'code'}, dimensions={0} | all-to-all | bytes 32768 | tf_op jit(solution)/shard_map/all_to_all | solution.py:265
  103.4 0.7 shard_map.47.token_potential
  104.1 3.5 %all-to-all-start.6 = ((f32[16,2,128]{2,1,0:T(2,128)}), f32[16,2,128]{2,1,0:T(2,128)S(1)}, u32[]{:S(2)}, u32[]{:S(2)}) async-start(f32[16,2,128]{2,1,0:T(2,128)} %shard_map.47.token_potential), calls=%async_computation.6 | async-start | bytes 32768 | tf_op jit(solution)/shard_map/all_to_all | solution.py:265
  107.6 4.0 %shard_map.48 = bf16[256,4096]{1,0:T(8,128)(2,1)} custom-call(f32[16,2,128]{2,1,0:T(2,128)} %shard_map.47.token_potential, f32[32,128]{1,0:T(8,128)S(1)} %get-tuple-element.12.code_potential, f32[256,4096]{1,0:T(8,128)} %copy-done), custom_call_target="tpu_custom_call" | custom-call | flops 4194304 | bytes 4194304 | tf_op jit(solution)/shard_map/pallas_call | solution.py:311
  111.5 2.4 %all-to-all-done.6.potential = f32[16,2,128]{2,1,0:T(2,128)S(1)} async-done(((f32[16,2,128]{2,1,0:T(2,128)}), f32[16,2,128]{2,1,0:T(2,128)S(1)}, u32[]{:S(2)}, u32[]{:S(2)}) %all-to-all-start.6) | async-done | bytes 16416 | tf_op jit(solution)/shard_map/all_to_all | solution.py:265
  113.9 0.0 all-gather.2.cloned.1.call-done.tokens
  113.9 5.2 %shard_map.49 = f32[256,512]{1,0:T(8,128)} custom-call(f32[32,128]{1,0:T(8,128)S(1)} %get-tuple-element.12.code_potential, f32[16,2,128]{2,1,0:T(2,128)S(1)} %all-to-all-done.6.potential, bf16[4096,512]{1,0:T(8,128)(2,1)} %codebook.3, bf16[4096,512]{1,0:T(8,128)(2,1)} %all-gather.2.cloned.1.call-done.tokens), custom_call_target="tpu_custom_call" | custom-call | flops 2151677952 | bytes 4194304 | tf_op jit(solution)/shard_map/pallas_call | solution.py:325
Async XLA Ops:
  7.2 106.8 %all-gather.2.cloned.1.call-start = ((), (), s32[]{:S(2)}) async-start(), calls=%async_computation.7 | async-start | bytes 4456448 | tf_op jit(solution)/shard_map/all_gather | solution.py:282
  11.0 2.0 %copy-start = (f32[256,4096]{1,0:T(8,128)}, f32[256,4096]{1,0:T(8,128)S(1)}, u32[]{:S(2)}) copy-start(f32[256,4096]{1,0:T(8,128)S(1)} %get-tuple-element.10.scores) | copy-start | bytes 12582916
  27.9 2.4 %copy-start.1 = (f32[256,4096]{1,0:T(8,128)S(1)}, f32[256,4096]{1,0:T(8,128)}, u32[]{:S(2)}) copy-start(f32[256,4096]{1,0:T(8,128)} %copy-done) | copy-start | bytes 12582916
  104.1 9.9 %all-to-all-start.6 = ((f32[16,2,128]{2,1,0:T(2,128)}), f32[16,2,128]{2,1,0:T(2,128)S(1)}, u32[]{:S(2)}, u32[]{:S(2)}) async-start(f32[16,2,128]{2,1,0:T(2,128)} %shard_map.47.token_potential), calls=%async_computation.6 | async-start | bytes 32768 | tf_op jit(solution)/shard_map/all_to_all | solution.py:265
Sparse Core Ops, SparseCore 0:
  13.1 63.1 all-gather.1

commit v7 on v6

--- a/solution.py
+++ b/solution.py
@@ -47,11 +47,6 @@
     most = jnp.max(top, axis=0, keepdims=True)
     total = jnp.sum(total * jnp.exp2(top - most), axis=0, keepdims=True)
     return most + jnp.log2(total)
-
-
-def send_copies(local, out):
-    for d in range(out.shape[0]):
-        out[d] = local[...]
 
 
 def send_copies(local, out):
@@ -128,13 +123,15 @@
             unroll=8,
         )
         partials.append((top, total))
+    lane = lax.broadcasted_iota(jnp.int32, (LANES, LANES), 1)
+    local = jnp.zeros((LANES, LANES), jnp.float32)
     for h, (top, total) in enumerate(partials):
-        top = top.T
-        most = jnp.max(top, axis=0, keepdims=True)
-        total = jnp.sum(total.T * jnp.exp2(top - most), axis=0, keepdims=True)
-        local = most + jnp.log2(total)
-        for d in range(out.shape[0]):
-            out[d, pl.ds(h, 1), :] = local
+        most = jnp.max(top, axis=1, keepdims=True)
+        total = jnp.sum(total * jnp.exp2(top - most), axis=1, keepdims=True)
+        local = jnp.where(lane == h, most + jnp.log2(total), local)
+    local = local.T[: out.shape[1], :]
+    for d in range(out.shape[0]):
+        out[d] = local
 
 
 def token_potential_kernel(shift, received, out):
@@ -264,6 +261,8 @@
     def exchange(copies, axis):
         return lax.all_to_all(copies, axis, 0, 0)
 
+    all_tokens = lax.all_gather(tokens, "tok", axis=0, tiled=True)
+
     scores, copies = call(
         scores_kernel,
         (pltpu.VMEM((tok_rows, code_rows), f32), to_tok),
@@ -278,8 +277,6 @@
         elements=elements,
         flops=2 * elements * depth,
     )(in_hbm(tokens), in_hbm(codebook))
-    copies, own_tokens = lax.optimization_barrier((copies, tokens))
-    all_tokens = lax.all_gather(own_tokens, "tok", axis=0, tiled=True)
     for step in range(ITERS):
         last = step == ITERS - 1
         potential = pltpu.VMEM((code_tiles, LANES), f32)

time: 127 us -> 123 us (0.969)
  local copies, waits for them, and re-layouts: 4.32 us -> 0.01 us
    unnamed x4 -> x2, local copies, waits for them, and re-layouts: 4.32 us -> 0.01 us
  transfers between devices with their start and end apart: 2 -> 2, of which waited for: 1 -> 1; matrix products, arithmetic and copies ran while one was open for 0% -> 0% of each run, Pallas kernels for 10% -> 14%
where the time goes in v7:
time: 123 us
  blocking collectives  80 us (65%)
  Pallas kernels  21.8 us (18%)
  between operations  14.1 us (11%)
  starting transfers between devices  3.53 us (3%)
  waiting for transfers between devices  3.06 us (2%)
    all_to_all x6, blocking collectives, exchange(): return lax.all_to_all(copies, axis, 0, 0)  80 us
    pallas_call x3, Pallas kernels, per_device(): call(functools.partial(rows_kernel, math.log2(total_codes)), (to_code, po...  5.44 us
    pallas_call x1, Pallas kernels, per_device(): call(functools.partial(refresh_kernel, math.log2(total_tokens)), jax.Shap...  5.23 us
    pallas_call x1, Pallas kernels, per_device(): call(functools.partial(targets_kernel, math.log2(total_tokens)), jax.Shap...  3.98 us
    pallas_call x1, Pallas kernels, per_device(): call(scores_kernel, (pltpu.VMEM((tok_rows, code_rows), f32), to_tok), [pl...  3.78 us
    all_to_all x1, starting transfers between devices, exchange(): return lax.all_to_all(copies, axis, 0, 0)  3.49 us
    pallas_call x2, Pallas kernels, per_device(): call(functools.partial(columns_kernel, math.log2(total_tokens)), to_tok,...  2.73 us
  transfers between devices with their start and end apart: 2, of which 1 were waited for; matrix products, arithmetic and copies ran while one was open for 0% of the time, Pallas kernels for 14%

profile of v7, /device:TPU:1, one launch (start us, length us, event | category | flops | bytes accessed | tf_op | source)
XLA Modules:
  0.0 122.6 jit_solution(11240472484073090277)
XLA Ops:
  7.2 0.0 all-gather.2.cloned.1.call-start
  7.2 0.7 all-gather.2.cloned.1.call-update
  7.9 3.8 %shard_map.41 = (f32[256,4096]{1,0:T(8,128)S(1)}, f32[16,32,128]{2,1,0:T(8,128)S(1)}) custom-call(bf16[256,512]{1,0:T(8,128)(2,1)} %tokens.1, bf16[4096,512]{1,0:T(8,128)(2,1)} %codebook.3), custom_call_target="tpu_custom_call" | custom-call | flops 1077936128 | bytes 4194304 | tf_op jit(solution)/shard_map/pallas_call | solution.py:266
  11.7 0.0 copy-start
  11.7 14.9 %all_to_all.35.received = f32[16,32,128]{2,1,0:T(8,128)S(1)} all-to-all(f32[16,32,128]{2,1,0:T(8,128)S(1)} %get-tuple-element.6), channel_id=1, replica_groups=mesh['tok'=16,'code'=16] {'tok'}, dimensions={0} | all-to-all | bytes 524288 | tf_op jit(solution)/shard_map/all_to_all | solution.py:262
  26.6 1.8 %shard_map.42 = f32[16,2,128]{2,1,0:T(2,128)S(1)} custom-call(f32[16,32,128]{2,1,0:T(8,128)S(1)} %all_to_all.35.received, f32[256,4096]{1,0:T(8,128)S(1)} %get-tuple-element.7.scores), custom_call_target="tpu_custom_call" | custom-call | flops 4194304 | bytes 4194304 | tf_op jit(solution)/shard_map/pallas_call | solution.py:283
  28.4 17.7 %all_to_all.36.received = f32[16,2,128]{2,1,0:T(2,128)S(1)} all-to-all(f32[16,2,128]{2,1,0:T(2,128)S(1)} %shard_map.42), channel_id=1, replica_groups=mesh['tok'=16,'code'=16] {'code'}, dimensions={0} | all-to-all | bytes 32768 | tf_op jit(solution)/shard_map/all_to_all | solution.py:262
  46.1 1.4 %shard_map.43 = f32[16,32,128]{2,1,0:T(8,128)S(1)} custom-call(f32[16,2,128]{2,1,0:T(2,128)S(1)} %all_to_all.36.received, f32[256,4096]{1,0:T(8,128)S(1)} %get-tuple-element.7.scores), custom_call_target="tpu_custom_call" | custom-call | flops 4194304 | bytes 4194304 | tf_op jit(solution)/shard_map/pallas_call | solution.py:292
  47.5 13.8 %all_to_all.37.received = f32[16,32,128]{2,1,0:T(8,128)S(1)} all-to-all(f32[16,32,128]{2,1,0:T(8,128)S(1)} %shard_map.43), channel_id=1, replica_groups=mesh['tok'=16,'code'=16] {'tok'}, dimensions={0} | all-to-all | bytes 524288 | tf_op jit(solution)/shard_map/all_to_all | solution.py:262
  61.3 1.8 %shard_map.44 = f32[16,2,128]{2,1,0:T(2,128)S(1)} custom-call(f32[16,32,128]{2,1,0:T(8,128)S(1)} %all_to_all.37.received, f32[256,4096]{1,0:T(8,128)S(1)} %get-tuple-element.7.scores), custom_call_target="tpu_custom_call" | custom-call | flops 4194304 | bytes 4194304 | tf_op jit(solution)/shard_map/pallas_call | solution.py:283
  63.2 11.6 %all_to_all.38.received = f32[16,2,128]{2,1,0:T(2,128)S(1)} all-to-all(f32[16,2,128]{2,1,0:T(2,128)S(1)} %shard_map.44), channel_id=1, replica_groups=mesh['tok'=16,'code'=16] {'code'}, dimensions={0} | all-to-all | bytes 32768 | tf_op jit(solution)/shard_map/all_to_all | solution.py:262
  74.7 1.4 %shard_map.45 = f32[16,32,128]{2,1,0:T(8,128)S(1)} custom-call(f32[16,2,128]{2,1,0:T(2,128)S(1)} %all_to_all.38.received, f32[256,4096]{1,0:T(8,128)S(1)} %get-tuple-element.7.scores), custom_call_target="tpu_custom_call" | custom-call | flops 4194304 | bytes 4194304 | tf_op jit(solution)/shard_map/pallas_call | solution.py:292
  76.1 11.0 %all_to_all.39.received = f32[16,32,128]{2,1,0:T(8,128)S(1)} all-to-all(f32[16,32,128]{2,1,0:T(8,128)S(1)} %shard_map.45), channel_id=1, replica_groups=mesh['tok'=16,'code'=16] {'tok'}, dimensions={0} | all-to-all | bytes 524288 | tf_op jit(solution)/shard_map/all_to_all | solution.py:262
  87.1 0.0 copy-done
  87.1 1.8 %shard_map.46 = (f32[16,2,128]{2,1,0:T(2,128)S(1)}, f32[32,128]{1,0:T(8,128)S(1)}) custom-call(f32[16,32,128]{2,1,0:T(8,128)S(1)} %all_to_all.39.received, f32[256,4096]{1,0:T(8,128)S(1)} %get-tuple-element.7.scores), custom_call_target="tpu_custom_call" | custom-call | flops 4194304 | bytes 4194304 | tf_op jit(solution)/shard_map/pallas_call | solution.py:283
  88.9 11.1 %all_to_all.40.received = f32[16,2,128]{2,1,0:T(2,128)S(1)} all-to-all(f32[16,2,128]{2,1,0:T(2,128)S(1)} %get-tuple-element.8), channel_id=1, replica_groups=mesh['tok'=16,'code'=16] {'code'}, dimensions={0} | all-to-all | bytes 32768 | tf_op jit(solution)/shard_map/all_to_all | solution.py:262
  99.9 0.7 shard_map.47.token_potential
  100.6 3.5 %all-to-all-start.6 = ((f32[16,2,128]{2,1,0:T(2,128)}), f32[16,2,128]{2,1,0:T(2,128)S(1)}, u32[]{:S(2)}, u32[]{:S(2)}) async-start(f32[16,2,128]{2,1,0:T(2,128)} %shard_map.47.token_potential), calls=%async_computation.6 | async-start | bytes 32768 | tf_op jit(solution)/shard_map/all_to_all | solution.py:262
  104.1 4.0 %shard_map.48 = bf16[256,4096]{1,0:T(8,128)(2,1)} custom-call(f32[16,2,128]{2,1,0:T(2,128)} %shard_map.47.token_potential, f32[32,128]{1,0:T(8,128)S(1)} %get-tuple-element.9.code_potential, f32[256,4096]{1,0:T(8,128)} %copy-done), custom_call_target="tpu_custom_call" | custom-call | flops 4194304 | bytes 4194304 | tf_op jit(solution)/shard_map/pallas_call | solution.py:308
  108.1 2.4 %all-to-all-done.6.potential = f32[16,2,128]{2,1,0:T(2,128)S(1)} async-done(((f32[16,2,128]{2,1,0:T(2,128)}), f32[16,2,128]{2,1,0:T(2,128)S(1)}, u32[]{:S(2)}, u32[]{:S(2)}) %all-to-all-start.6) | async-done | bytes 16416 | tf_op jit(solution)/shard_map/all_to_all | solution.py:262
  110.5 0.0 all-gather.2.cloned.1.call-done.tokens
  110.5 5.2 %shard_map.49 = f32[256,512]{1,0:T(8,128)} custom-call(f32[32,128]{1,0:T(8,128)S(1)} %get-tuple-element.9.code_potential, f32[16,2,128]{2,1,0:T(2,128)S(1)} %all-to-all-done.6.potential, bf16[4096,512]{1,0:T(8,128)(2,1)} %codebook.3, bf16[4096,512]{1,0:T(8,128)(2,1)} %all-gather.2.cloned.1.call-done.tokens), custom_call_target="tpu_custom_call" | custom-call | flops 2151677952 | bytes 4194304 | tf_op jit(solution)/shard_map/pallas_call | solution.py:322
Async XLA Ops:
  7.2 103.3 %all-gather.2.cloned.1.call-start = ((), (), s32[]{:S(2)}) async-start(), calls=%async_computation.7 | async-start | bytes 4456448 | tf_op jit(solution)/shard_map/all_gather | solution.py:264
  11.7 75.4 %copy-start = (f32[256,4096]{1,0:T(8,128)}, f32[256,4096]{1,0:T(8,128)S(1)}, u32[]{:S(2)}) copy-start(f32[256,4096]{1,0:T(8,128)S(1)} %get-tuple-element.7.scores) | copy-start | bytes 12582916
  100.6 9.9 %all-to-all-start.6 = ((f32[16,2,128]{2,1,0:T(2,128)}), f32[16,2,128]{2,1,0:T(2,128)S(1)}, u32[]{:S(2)}, u32[]{:S(2)}) async-start(f32[16,2,128]{2,1,0:T(2,128)} %shard_map.47.token_potential), calls=%async_computation.6 | async-start | bytes 32768 | tf_op jit(solution)/shard_map/all_to_all | solution.py:262
Sparse Core Ops, SparseCore 0:
  10.4 63.1 all-gather.1

commit v8 on v6

--- a/solution.py
+++ b/solution.py
@@ -15,7 +15,7 @@
 rms_epsilon = 1e-06
 
 LANES = 128
-CHUNK = 1024
+CHUNKS = 5
 DOT_CHUNK = 512
 AHEAD = 2
 MIB = 1 << 20
@@ -54,17 +54,21 @@
         out[d] = local[...]
 
 
-def send_copies(local, out):
-    for d in range(out.shape[0]):
-        out[d] = local[...]
+def chunks(size):
+    ends = [size // 8 * k for k in (0, 1, 3, 5, 7, 8)]
+    return [(start, end - start) for start, end in zip(ends, ends[1:])]
 
 
 def chunk_copies(source, held, sems, axis=0):
     copies = []
-    for k in range(source.shape[axis] // CHUNK):
-        part = (slice(None),) * axis + (pl.ds(k * CHUNK, CHUNK),)
+    for k, (start, length) in enumerate(chunks(source.shape[axis])):
+        part = (slice(None),) * axis + (pl.ds(start, length),)
         copies.append(pltpu.make_async_copy(source.at[part], held.at[part], sems.at[k]))
     return copies
+
+
+def tiles_of(start, length):
+    return range(start // LANES, (start + length) // LANES)
 
 
 def scores_kernel(tokens, codebook, scores, out, held, rows, local, sems, rows_sem):
@@ -74,22 +78,24 @@
     for copy in copies[:AHEAD]:
         copy.start()
     rows_copy.wait()
-    for k in range(len(copies) + 1):
-        if k < len(copies):
+    parts = chunks(codebook.shape[0])
+    for k in range(len(parts) + 1):
+        if k < len(parts):
             copies[k].wait()
-            if k + AHEAD < len(copies):
+            if k + AHEAD < len(parts):
                 copies[k + AHEAD].start()
-            scores[:, pl.ds(k * CHUNK, CHUNK)] = (
+            part = pl.ds(*parts[k])
+            scores[:, part] = (
                 lax.dot_general(
                     rows[...],
-                    held[pl.ds(k * CHUNK, CHUNK), :],
+                    held[part, :],
                     (((1,), (1,)), ((), ())),
                     preferred_element_type=jnp.float32,
                 )
                 * score_scale
             )
         if k > 0:
-            for j in range((k - 1) * CHUNK // LANES, k * CHUNK // LANES):
+            for j in tiles_of(*parts[k - 1]):
                 local[pl.ds(j, 1), :] = column_lse(scores, None, j)
     send_copies(local, out)
 
@@ -152,9 +158,9 @@
     for h in range(token_potential.shape[1]):
         column[pl.ds(h * LANES, LANES), :] = as_column(token_potential[0, pl.ds(h, 1), :]) + scale
     out_copies = chunk_copies(held, out, out_sems, 1)
-    for k in range(len(copies)):
+    for k, part in enumerate(chunks(scores.shape[1])):
         copies[k].wait()
-        for j in range(k * CHUNK // LANES, (k + 1) * CHUNK // LANES):
+        for j in tiles_of(*part):
             held[:, tile(j)] = jnp.exp2(
                 panel[:, tile(j)] + column[...] + code_potential[pl.ds(j, 1), :]
             ).astype(held.dtype)
@@ -184,11 +190,13 @@
         column[pl.ds(h * LANES, LANES), :] = as_column(row) + scale
     own.wait()
 
+    parts = chunks(tokens.shape[0])
+
     def chunk_scores(k):
         copies[k].wait()
         if k + AHEAD < len(copies):
             copies[k + AHEAD].start()
-        part = pl.ds(k * CHUNK, CHUNK)
+        part = pl.ds(*parts[k])
         panel[:, part] = (
             lax.dot_general(
                 codes[...],
@@ -201,12 +209,12 @@
 
     assigned = jnp.zeros(out.shape, jnp.float32)
     chunk_scores(0)
-    for k in range(len(copies)):
-        if k + 1 < len(copies):
+    for k, (first, length) in enumerate(parts):
+        if k + 1 < len(parts):
             chunk_scores(k + 1)
-        for start in range(k * CHUNK, (k + 1) * CHUNK, DOT_CHUNK):
+        for start in range(first, first + length, DOT_CHUNK):
             weights = []
-            for j in range(start // LANES, (start + DOT_CHUNK) // LANES):
+            for j in tiles_of(start, DOT_CHUNK):
                 row = potential[j // halves, pl.ds(j % halves, 1), :]
                 weights.append(
                     jnp.exp2(panel[:, tile(j)] + column[...] + row).astype(held.dtype)
@@ -264,6 +272,8 @@
     def exchange(copies, axis):
         return lax.all_to_all(copies, axis, 0, 0)
 
+    all_tokens = lax.all_gather(tokens, "tok", axis=0, tiled=True)
+
     scores, copies = call(
         scores_kernel,
         (pltpu.VMEM((tok_rows, code_rows), f32), to_tok),
@@ -271,15 +281,13 @@
             pltpu.VMEM((code_rows, depth), codebook.dtype),
             pltpu.VMEM((tok_rows, depth), tokens.dtype),
             pltpu.VMEM((code_tiles, LANES), f32),
-            pltpu.SemaphoreType.DMA((code_rows // CHUNK,)),
+            pltpu.SemaphoreType.DMA((CHUNKS,)),
             pltpu.SemaphoreType.DMA,
         ],
         specs=[hbm, hbm],
         elements=elements,
         flops=2 * elements * depth,
     )(in_hbm(tokens), in_hbm(codebook))
-    copies, own_tokens = lax.optimization_barrier((copies, tokens))
-    all_tokens = lax.all_gather(own_tokens, "tok", axis=0, tiled=True)
     for step in range(ITERS):
         last = step == ITERS - 1
         potential = pltpu.VMEM((code_tiles, LANES), f32)
@@ -307,7 +315,7 @@
         specs=[vmem],
     )(received)
     all_potential = exchange(copies, "tok")
-    code_sems = pltpu.SemaphoreType.DMA((code_rows // CHUNK,))
+    code_sems = pltpu.SemaphoreType.DMA((CHUNKS,))
     targets = call(
         functools.partial(targets_kernel, math.log2(total_tokens)),
         jax.ShapeDtypeStruct((tok_rows, code_rows), jnp.bfloat16),
@@ -330,7 +338,7 @@
             pltpu.VMEM((share, depth), codebook.dtype),
             pltpu.VMEM((share, LANES), f32),
             pltpu.VMEM((share, total_tokens), f32),
-            pltpu.SemaphoreType.DMA((total_tokens // CHUNK,)),
+            pltpu.SemaphoreType.DMA((CHUNKS,)),
             pltpu.SemaphoreType.DMA,
         ],
         specs=[vmem, vmem, hbm, hbm],

time: 127 us -> 124 us (0.976)
  local copies, waits for them, and re-layouts: 4.32 us -> 0.01 us
    unnamed x4 -> x2, local copies, waits for them, and re-layouts: 4.32 us -> 0.01 us
  transfers between devices with their start and end apart: 2 -> 2, of which waited for: 1 -> 1; matrix products, arithmetic and copies ran while one was open for 0% -> 0% of each run, Pallas kernels for 10% -> 14%
where the time goes in v8:
time: 124 us; the launch traced here: 123 us
  blocking collectives  80.1 us (65%)
  Pallas kernels  22.2 us (18%)
  between operations  14.1 us (11%)
  starting transfers between devices  3.53 us (3%)
  waiting for transfers between devices  3.14 us (3%)
    all_to_all x6, blocking collectives, exchange(): return lax.all_to_all(copies, axis, 0, 0)  80.1 us
    pallas_call x1, Pallas kernels, per_device(): call(functools.partial(refresh_kernel, math.log2(total_tokens)), jax.Shap...  5.54 us
    pallas_call x3, Pallas kernels, per_device(): call(functools.partial(rows_kernel, math.log2(total_codes)), (to_code, po...  5.19 us
    pallas_call x1, Pallas kernels, per_device(): call(scores_kernel, (pltpu.VMEM((tok_rows, code_rows), f32), to_tok), [pl...  4.16 us
    pallas_call x1, Pallas kernels, per_device(): call(functools.partial(targets_kernel, math.log2(total_tokens)), jax.Shap...  3.91 us
    all_to_all x1, starting transfers between devices, exchange(): return lax.all_to_all(copies, axis, 0, 0)  3.49 us
    pallas_call x2, Pallas kernels, per_device(): call(functools.partial(columns_kernel, math.log2(total_tokens)), to_tok,...  2.73 us
  transfers between devices with their start and end apart: 2, of which 1 were waited for; matrix products, arithmetic and copies ran while one was open for 0% of the time, Pallas kernels for 14%

profile of v8, /device:TPU:1, one launch (start us, length us, event | category | flops | bytes accessed | tf_op | source)
XLA Modules:
  0.0 123.0 jit_solution(12607314679950418025)
XLA Ops:
  7.2 0.0 all-gather.2.cloned.1.call-start
  7.2 0.7 all-gather.2.cloned.1.call-update
  7.9 4.2 %shard_map.41 = (f32[256,4096]{1,0:T(8,128)S(1)}, f32[16,32,128]{2,1,0:T(8,128)S(1)}) custom-call(bf16[256,512]{1,0:T(8,128)(2,1)} %tokens.1, bf16[4096,512]{1,0:T(8,128)(2,1)} %codebook.3), custom_call_target="tpu_custom_call" | custom-call | flops 1077936128 | bytes 4194304 | tf_op jit(solution)/shard_map/pallas_call | solution.py:277
  12.1 0.0 copy-start
  12.1 14.9 %all_to_all.35.received = f32[16,32,128]{2,1,0:T(8,128)S(1)} all-to-all(f32[16,32,128]{2,1,0:T(8,128)S(1)} %get-tuple-element.6), channel_id=1, replica_groups=mesh['tok'=16,'code'=16] {'tok'}, dimensions={0} | all-to-all | bytes 524288 | tf_op jit(solution)/shard_map/all_to_all | solution.py:273
  27.0 1.7 %shard_map.42 = f32[16,2,128]{2,1,0:T(2,128)S(1)} custom-call(f32[16,32,128]{2,1,0:T(8,128)S(1)} %all_to_all.35.received, f32[256,4096]{1,0:T(8,128)S(1)} %get-tuple-element.7.scores), custom_call_target="tpu_custom_call" | custom-call | flops 4194304 | bytes 4194304 | tf_op jit(solution)/shard_map/pallas_call | solution.py:294
  28.7 17.7 %all_to_all.36.received = f32[16,2,128]{2,1,0:T(2,128)S(1)} all-to-all(f32[16,2,128]{2,1,0:T(2,128)S(1)} %shard_map.42), channel_id=1, replica_groups=mesh['tok'=16,'code'=16] {'code'}, dimensions={0} | all-to-all | bytes 32768 | tf_op jit(solution)/shard_map/all_to_all | solution.py:273
  46.4 1.4 %shard_map.43 = f32[16,32,128]{2,1,0:T(8,128)S(1)} custom-call(f32[16,2,128]{2,1,0:T(2,128)S(1)} %all_to_all.36.received, f32[256,4096]{1,0:T(8,128)S(1)} %get-tuple-element.7.scores), custom_call_target="tpu_custom_call" | custom-call | flops 4194304 | bytes 4194304 | tf_op jit(solution)/shard_map/pallas_call | solution.py:303
  47.8 13.5 %all_to_all.37.received = f32[16,32,128]{2,1,0:T(8,128)S(1)} all-to-all(f32[16,32,128]{2,1,0:T(8,128)S(1)} %shard_map.43), channel_id=1, replica_groups=mesh['tok'=16,'code'=16] {'tok'}, dimensions={0} | all-to-all | bytes 524288 | tf_op jit(solution)/shard_map/all_to_all | solution.py:273
  61.3 1.7 %shard_map.44 = f32[16,2,128]{2,1,0:T(2,128)S(1)} custom-call(f32[16,32,128]{2,1,0:T(8,128)S(1)} %all_to_all.37.received, f32[256,4096]{1,0:T(8,128)S(1)} %get-tuple-element.7.scores), custom_call_target="tpu_custom_call" | custom-call | flops 4194304 | bytes 4194304 | tf_op jit(solution)/shard_map/pallas_call | solution.py:294
  63.1 11.9 %all_to_all.38.received = f32[16,2,128]{2,1,0:T(2,128)S(1)} all-to-all(f32[16,2,128]{2,1,0:T(2,128)S(1)} %shard_map.44), channel_id=1, replica_groups=mesh['tok'=16,'code'=16] {'code'}, dimensions={0} | all-to-all | bytes 32768 | tf_op jit(solution)/shard_map/all_to_all | solution.py:273
  75.0 1.4 %shard_map.45 = f32[16,32,128]{2,1,0:T(8,128)S(1)} custom-call(f32[16,2,128]{2,1,0:T(2,128)S(1)} %all_to_all.38.received, f32[256,4096]{1,0:T(8,128)S(1)} %get-tuple-element.7.scores), custom_call_target="tpu_custom_call" | custom-call | flops 4194304 | bytes 4194304 | tf_op jit(solution)/shard_map/pallas_call | solution.py:303
  76.3 11.0 %all_to_all.39.received = f32[16,32,128]{2,1,0:T(8,128)S(1)} all-to-all(f32[16,32,128]{2,1,0:T(8,128)S(1)} %shard_map.45), channel_id=1, replica_groups=mesh['tok'=16,'code'=16] {'tok'}, dimensions={0} | all-to-all | bytes 524288 | tf_op jit(solution)/shard_map/all_to_all | solution.py:273
  87.3 0.0 copy-done
  87.3 1.7 %shard_map.46 = (f32[16,2,128]{2,1,0:T(2,128)S(1)}, f32[32,128]{1,0:T(8,128)S(1)}) custom-call(f32[16,32,128]{2,1,0:T(8,128)S(1)} %all_to_all.39.received, f32[256,4096]{1,0:T(8,128)S(1)} %get-tuple-element.7.scores), custom_call_target="tpu_custom_call" | custom-call | flops 4194304 | bytes 4194304 | tf_op jit(solution)/shard_map/pallas_call | solution.py:294
  89.0 11.1 %all_to_all.40.received = f32[16,2,128]{2,1,0:T(2,128)S(1)} all-to-all(f32[16,2,128]{2,1,0:T(2,128)S(1)} %get-tuple-element.8), channel_id=1, replica_groups=mesh['tok'=16,'code'=16] {'code'}, dimensions={0} | all-to-all | bytes 32768 | tf_op jit(solution)/shard_map/all_to_all | solution.py:273
  100.1 0.7 shard_map.47.token_potential
  100.8 3.5 %all-to-all-start.6 = ((f32[16,2,128]{2,1,0:T(2,128)}), f32[16,2,128]{2,1,0:T(2,128)S(1)}, u32[]{:S(2)}, u32[]{:S(2)}) async-start(f32[16,2,128]{2,1,0:T(2,128)} %shard_map.47.token_potential), calls=%async_computation.6 | async-start | bytes 32768 | tf_op jit(solution)/shard_map/all_to_all | solution.py:273
  104.3 3.9 %shard_map.48 = bf16[256,4096]{1,0:T(8,128)(2,1)} custom-call(f32[16,2,128]{2,1,0:T(2,128)} %shard_map.47.token_potential, f32[32,128]{1,0:T(8,128)S(1)} %get-tuple-element.9.code_potential, f32[256,4096]{1,0:T(8,128)} %copy-done), custom_call_target="tpu_custom_call" | custom-call | flops 4194304 | bytes 4194304 | tf_op jit(solution)/shard_map/pallas_call | solution.py:319
  108.2 2.5 %all-to-all-done.6.potential = f32[16,2,128]{2,1,0:T(2,128)S(1)} async-done(((f32[16,2,128]{2,1,0:T(2,128)}), f32[16,2,128]{2,1,0:T(2,128)S(1)}, u32[]{:S(2)}, u32[]{:S(2)}) %all-to-all-start.6) | async-done | bytes 16416 | tf_op jit(solution)/shard_map/all_to_all | solution.py:273
  110.6 0.0 all-gather.2.cloned.1.call-done.tokens
  110.6 5.5 %shard_map.49 = f32[256,512]{1,0:T(8,128)} custom-call(f32[32,128]{1,0:T(8,128)S(1)} %get-tuple-element.9.code_potential, f32[16,2,128]{2,1,0:T(2,128)S(1)} %all-to-all-done.6.potential, bf16[4096,512]{1,0:T(8,128)(2,1)} %codebook.3, bf16[4096,512]{1,0:T(8,128)(2,1)} %all-gather.2.cloned.1.call-done.tokens), custom_call_target="tpu_custom_call" | custom-call | flops 2151677952 | bytes 4194304 | tf_op jit(solution)/shard_map/pallas_call | solution.py:333
Async XLA Ops:
  7.2 103.5 %all-gather.2.cloned.1.call-start = ((), (), s32[]{:S(2)}) async-start(), calls=%async_computation.7 | async-start | bytes 4456448 | tf_op jit(solution)/shard_map/all_gather | solution.py:275
  12.1 75.2 %copy-start = (f32[256,4096]{1,0:T(8,128)}, f32[256,4096]{1,0:T(8,128)S(1)}, u32[]{:S(2)}) copy-start(f32[256,4096]{1,0:T(8,128)S(1)} %get-tuple-element.7.scores) | copy-start | bytes 12582916
  100.8 9.9 %all-to-all-start.6 = ((f32[16,2,128]{2,1,0:T(2,128)}), f32[16,2,128]{2,1,0:T(2,128)S(1)}, u32[]{:S(2)}, u32[]{:S(2)}) async-start(f32[16,2,128]{2,1,0:T(2,128)} %shard_map.47.token_potential), calls=%async_computation.6 | async-start | bytes 32768 | tf_op jit(solution)/shard_map/all_to_all | solution.py:273
Sparse Core Ops, SparseCore 0:
  10.4 63.1 all-gather.1

commit v9 on v7

--- a/solution.py
+++ b/solution.py
@@ -102,36 +102,9 @@
     send_copies(local, out)
 
 
-def rows_kernel(shift, received, scores, out, potential):
-    potential[...] = -shift - lse2(received[...], 0)
-    tiles = potential.shape[0]
-    partials = []
-    for h in range(out.shape[1]):
-        rows = pl.ds(h * LANES, LANES)
-
-        def values(k):
-            return scores[rows, tile(k)] + potential[pl.ds(k, 1), :]
-
-        top = lax.fori_loop(
-            0, tiles, lambda k, top: jnp.maximum(top, values(k)), values(0), unroll=8
-        )
-        total = lax.fori_loop(
-            0,
-            tiles,
-            lambda k, total: total + jnp.exp2(values(k) - top),
-            jnp.zeros((LANES, LANES), jnp.float32),
-            unroll=8,
-        )
-        partials.append((top, total))
-    lane = lax.broadcasted_iota(jnp.int32, (LANES, LANES), 1)
-    local = jnp.zeros((LANES, LANES), jnp.float32)
-    for h, (top, total) in enumerate(partials):
-        most = jnp.max(top, axis=1, keepdims=True)
-        total = jnp.sum(total * jnp.exp2(top - most), axis=1, keepdims=True)
-        local = jnp.where(lane == h, most + jnp.log2(total), local)
-    local = local.T[: out.shape[1], :]
-    for d in range(out.shape[0]):
-        out[d] = local
+def row_partials(scores, potential, shape):
+    local = lse2(scores + potential.reshape(1, scores.shape[1]), 1)
+    return jnp.broadcast_to(local.reshape(shape[1:]), shape)
 
 
 def token_potential_kernel(shift, received, out):
@@ -255,7 +228,7 @@
     vmem = pl.BlockSpec(memory_space=pltpu.VMEM)
     hbm = pl.BlockSpec(memory_space=pltpu.HBM)
     to_tok = jax.ShapeDtypeStruct((tok_size, code_tiles, LANES), f32)
-    to_code = jax.ShapeDtypeStruct((code_size, row_tiles, LANES), f32)
+    to_code = (code_size, row_tiles, LANES)
     column = pltpu.VMEM((tok_rows, LANES), f32)
 
     def exchange(copies, axis):
@@ -280,13 +253,8 @@
     for step in range(ITERS):
         last = step == ITERS - 1
         potential = pltpu.VMEM((code_tiles, LANES), f32)
-        copies, *code_potential = call(
-            functools.partial(rows_kernel, math.log2(total_codes)),
-            (to_code, potential) if last else (to_code,),
-            [] if last else [potential],
-            specs=[vmem, vmem],
-            elements=elements,
-        )(exchange(copies, "tok"), in_vmem(scores))
+        code_potential = -math.log2(total_codes) - lse2(exchange(copies, "tok"), 0)
+        copies = row_partials(scores, code_potential, to_code)
         received = exchange(copies, "code")
         if not last:
             copies = call(
@@ -296,8 +264,6 @@
                 specs=[vmem, vmem],
                 elements=elements,
             )(received, in_vmem(scores))
-    (code_potential,) = code_potential
-
     copies = call(
         functools.partial(token_potential_kernel, math.log2(total_tokens)),
         jax.ShapeDtypeStruct((tok_size, row_tiles, LANES), f32),

time: 123 us -> 133 us (1.081)
  other arithmetic: 0 us -> 11.5 us
  Pallas kernels: 21.8 us -> 16.4 us
  local copies, waits for them, and re-layouts: 0.01 us -> 3.99 us
    reduce_max x0 -> x6, other arithmetic: none -> 8.32 us  [lse2(): top = jnp.max(values, axis=axis, keepdims=True)]
    pallas_call x3 -> x0, Pallas kernels: 5.44 us -> none  [per_device(): call(functools.partial(rows_kernel, math.log2(total_codes)), (to_code, po...]
    unnamed x2 -> x8, local copies, waits for them, and re-layouts: 0.01 us -> 3.96 us
    reduce_sum x0 -> x6, other arithmetic: none -> 3.11 us  [lse2(): total = jnp.sum(jnp.exp2(values - top), axis=axis)]
  transfers between devices with their start and end apart: 2 -> 2, of which waited for: 1 -> 1; matrix products, arithmetic and copies ran while one was open for 0% -> 9% of each run, Pallas kernels for 14% -> 8%
where the time goes in v9:
time: 133 us
  blocking collectives  80.2 us (60%)
  Pallas kernels  16.4 us (12%)
  between operations  14.2 us (11%)
  other arithmetic  11.5 us (9%)
  local copies, waits for them, and re-layouts  3.99 us (3%)
  starting transfers between devices  3.53 us (3%)
  waiting for transfers between devices  3.06 us (2%)
    all_to_all x6, blocking collectives, exchange(): return lax.all_to_all(copies, axis, 0, 0)  80.2 us
    reduce_max x6, other arithmetic, lse2(): top = jnp.max(values, axis=axis, keepdims=True)  8.32 us
    pallas_call x1, Pallas kernels, per_device(): call(functools.partial(refresh_kernel, math.log2(total_tokens)), jax.Shap...  5.23 us
    pallas_call x1, Pallas kernels, per_device(): call(functools.partial(targets_kernel, math.log2(total_tokens)), jax.Shap...  3.98 us
    unnamed x8, local copies, waits for them, and re-layouts  3.96 us
    pallas_call x1, Pallas kernels, per_device(): call(scores_kernel, (pltpu.VMEM((tok_rows, code_rows), f32), to_tok), [pl...  3.78 us
    all_to_all x1, starting transfers between devices, exchange(): return lax.all_to_all(copies, axis, 0, 0)  3.49 us
    reduce_sum x6, other arithmetic, lse2(): total = jnp.sum(jnp.exp2(values - top), axis=axis)  3.11 us
  transfers between devices with their start and end apart: 2, of which 1 were waited for; matrix products, arithmetic and copies ran while one was open for 9% of the time, Pallas kernels for 8%

profile of v9, /device:TPU:1, one launch (start us, length us, event | category | flops | bytes accessed | tf_op | source)
XLA Modules:
  0.0 132.8 jit_solution(7413945546788989613)
XLA Ops:
  7.2 0.0 all-gather.2.cloned.1.call-start
  7.2 0.7 all-gather.2.cloned.1.call-update
  7.9 3.8 %shard_map.41 = (f32[256,4096]{1,0:T(8,128)S(1)}, f32[16,32,128]{2,1,0:T(8,128)S(1)}) custom-call(bf16[256,512]{1,0:T(8,128)(2,1)} %tokens.1, bf16[4096,512]{1,0:T(8,128)(2,1)} %codebook.3), custom_call_target="tpu_custom_call" | custom-call | flops 1077936128 | bytes 4194304 | tf_op jit(solution)/shard_map/pallas_call | solution.py:239
  11.7 0.0 copy-start
  11.7 2.0 %copy-done = f32[256,4096]{1,0:T(8,128)} copy-done((f32[256,4096]{1,0:T(8,128)}, f32[256,4096]{1,0:T(8,128)S(1)}, u32[]{:S(2)}) %copy-start) | copy-done | bytes 4194328
  13.7 14.9 %all_to_all.35 = f32[16,32,128]{2,1,0:T(8,128)S(1)} all-to-all(f32[16,32,128]{2,1,0:T(8,128)S(1)} %get-tuple-element.5), channel_id=1, replica_groups=mesh['tok'=16,'code'=16] {'tok'}, dimensions={0} | all-to-all | bytes 524288 | tf_op jit(solution)/shard_map/all_to_all | solution.py:235
  28.6 0.0 copy-start.1
  28.6 0.1 exponential_reduce_fusion.5
  28.7 2.7 %add_reduce_fusion.2 = f32[256]{0:T(256)S(1)} fusion(f32[256,4096]{1,0:T(8,128)} %copy-done, f32[4096]{0:T(1024)S(1)} %subtract_bitcast_fusion.1), kind=kLoop, calls=%fused_computation.5 | loop fusion | flops 2096896 | bytes 4211712 | tf_op jit(solution)/shard_map/reduce_max | solution.py:27
  31.4 0.6 copy-done.1
  32.1 1.0 exponential_reduce_fusion.2
  33.1 17.8 %all_to_all.36.received = f32[16,2,128]{2,1,0:T(2,128)S(1)} all-to-all(f32[16,2,128]{2,1,0:T(2,128)S(1)} %broadcast_in_dim.6), channel_id=1, replica_groups=mesh['tok'=16,'code'=16] {'code'}, dimensions={0} | all-to-all | bytes 32768 | tf_op jit(solution)/shard_map/all_to_all | solution.py:235
  50.9 1.4 %shard_map.42 = f32[16,32,128]{2,1,0:T(8,128)S(1)} custom-call(f32[16,2,128]{2,1,0:T(2,128)S(1)} %all_to_all.36.received, f32[256,4096]{1,0:T(8,128)S(1)} %copy-done.1), custom_call_target="tpu_custom_call" | custom-call | flops 4194304 | bytes 4194304 | tf_op jit(solution)/shard_map/pallas_call | solution.py:260
  52.2 14.0 %all_to_all.37 = f32[16,32,128]{2,1,0:T(8,128)S(1)} all-to-all(f32[16,32,128]{2,1,0:T(8,128)S(1)} %shard_map.42), channel_id=1, replica_groups=mesh['tok'=16,'code'=16] {'tok'}, dimensions={0} | all-to-all | bytes 524288 | tf_op jit(solution)/shard_map/all_to_all | solution.py:235
  66.2 0.0 copy-start.2
  66.3 0.1 exponential_reduce_fusion.4
  66.3 2.8 %add_reduce_fusion.1 = f32[256]{0:T(256)S(1)} fusion(f32[256,4096]{1,0:T(8,128)} %copy-done, f32[4096]{0:T(1024)S(1)} %subtract_bitcast_fusion), kind=kLoop, calls=%fused_computation.4 | loop fusion | flops 2096896 | bytes 4211712 | tf_op jit(solution)/shard_map/reduce_max | solution.py:27
  69.1 0.7 copy-done.2
  69.9 1.0 exponential_reduce_fusion.1
  70.9 11.5 %all_to_all.38.received = f32[16,2,128]{2,1,0:T(2,128)S(1)} all-to-all(f32[16,2,128]{2,1,0:T(2,128)S(1)} %broadcast_in_dim.7), channel_id=1, replica_groups=mesh['tok'=16,'code'=16] {'code'}, dimensions={0} | all-to-all | bytes 32768 | tf_op jit(solution)/shard_map/all_to_all | solution.py:235
  82.3 1.4 %shard_map.43 = f32[16,32,128]{2,1,0:T(8,128)S(1)} custom-call(f32[16,2,128]{2,1,0:T(2,128)S(1)} %all_to_all.38.received, f32[256,4096]{1,0:T(8,128)S(1)} %copy-done.2), custom_call_target="tpu_custom_call" | custom-call | flops 4194304 | bytes 4194304 | tf_op jit(solution)/shard_map/pallas_call | solution.py:260
  83.7 10.9 %all_to_all.39 = f32[16,32,128]{2,1,0:T(8,128)S(1)} all-to-all(f32[16,32,128]{2,1,0:T(8,128)S(1)} %shard_map.43), channel_id=1, replica_groups=mesh['tok'=16,'code'=16] {'tok'}, dimensions={0} | all-to-all | bytes 524288 | tf_op jit(solution)/shard_map/all_to_all | solution.py:235
  94.6 0.1 exponential_reduce_fusion.3
  94.7 2.7 %add_reduce_fusion = f32[256]{0:T(256)S(1)} fusion(f32[256,4096]{1,0:T(8,128)} %copy-done, f32[4096]{0:T(1024)S(1)} %bitcast.11), kind=kLoop, calls=%fused_computation.3 | loop fusion | flops 2096896 | bytes 4211712 | tf_op jit(solution)/shard_map/reduce_max | solution.py:27
  97.4 0.6 copy-done.3
  98.1 1.0 exponential_reduce_fusion
  99.1 11.2 %all_to_all.40.received = f32[16,2,128]{2,1,0:T(2,128)S(1)} all-to-all(f32[16,2,128]{2,1,0:T(2,128)S(1)} %broadcast_in_dim.8), channel_id=1, replica_groups=mesh['tok'=16,'code'=16] {'code'}, dimensions={0} | all-to-all | bytes 32768 | tf_op jit(solution)/shard_map/all_to_all | solution.py:235
  110.2 0.7 shard_map.44.token_potential
  110.9 3.5 %all-to-all-start.6 = ((f32[16,2,128]{2,1,0:T(2,128)}), f32[16,2,128]{2,1,0:T(2,128)S(1)}, u32[]{:S(2)}, u32[]{:S(2)}) async-start(f32[16,2,128]{2,1,0:T(2,128)} %shard_map.44.token_potential), calls=%async_computation.6 | async-start | bytes 32768 | tf_op jit(solution)/shard_map/all_to_all | solution.py:235
  114.4 4.0 %shard_map.45 = bf16[256,4096]{1,0:T(8,128)(2,1)} custom-call(f32[16,2,128]{2,1,0:T(2,128)} %shard_map.44.token_potential, f32[32,128]{1,0:T(8,128)S(1)} %add_subtract_fusion.code_potential, f32[256,4096]{1,0:T(8,128)} %copy-done), custom_call_target="tpu_custom_call" | custom-call | flops 4194304 | bytes 4194304 | tf_op jit(solution)/shard_map/pallas_call | solution.py:274
  118.4 2.4 %all-to-all-done.6.potential = f32[16,2,128]{2,1,0:T(2,128)S(1)} async-done(((f32[16,2,128]{2,1,0:T(2,128)}), f32[16,2,128]{2,1,0:T(2,128)S(1)}, u32[]{:S(2)}, u32[]{:S(2)}) %all-to-all-start.6) | async-done | bytes 16416 | tf_op jit(solution)/shard_map/all_to_all | solution.py:235
  120.7 5.2 %shard_map.46 = f32[256,512]{1,0:T(8,128)} custom-call(f32[32,128]{1,0:T(8,128)S(1)} %add_subtract_fusion.code_potential, f32[16,2,128]{2,1,0:T(2,128)S(1)} %all-to-all-done.6.potential, bf16[4096,512]{1,0:T(8,128)(2,1)} %codebook.3, bf16[4096,512]{1,0:T(8,128)(2,1)} %all-gather.2.cloned.1.call-done.tokens), custom_call_target="tpu_custom_call" | custom-call | flops 2151677952 | bytes 4194304 | tf_op jit(solution)/shard_map/pallas_call | solution.py:288
  (14 shorter events, 0.2 us)
Async XLA Ops:
  7.2 113.6 %all-gather.2.cloned.1.call-start = ((), (), s32[]{:S(2)}) async-start(), calls=%async_computation.7 | async-start | bytes 4456448 | tf_op jit(solution)/shard_map/all_gather | solution.py:237
  11.7 2.0 %copy-start = (f32[256,4096]{1,0:T(8,128)}, f32[256,4096]{1,0:T(8,128)S(1)}, u32[]{:S(2)}) copy-start(f32[256,4096]{1,0:T(8,128)S(1)} %get-tuple-element.4.scores) | copy-start | bytes 12582916
  28.6 3.5 %copy-start.1 = (f32[256,4096]{1,0:T(8,128)S(1)}, f32[256,4096]{1,0:T(8,128)}, u32[]{:S(2)}) copy-start(f32[256,4096]{1,0:T(8,128)} %copy-done) | copy-start | bytes 12582916
  66.2 3.6 %copy-start.2 = (f32[256,4096]{1,0:T(8,128)S(1)}, f32[256,4096]{1,0:T(8,128)}, u32[]{:S(2)}) copy-start(f32[256,4096]{1,0:T(8,128)} %copy-done) | copy-start | bytes 12582916
  94.6 3.5 %copy-start.3 = (f32[256,4096]{1,0:T(8,128)S(1)}, f32[256,4096]{1,0:T(8,128)}, u32[]{:S(2)}) copy-start(f32[256,4096]{1,0:T(8,128)} %copy-done) | copy-start | bytes 12582916
  110.9 9.9 %all-to-all-start.6 = ((f32[16,2,128]{2,1,0:T(2,128)}), f32[16,2,128]{2,1,0:T(2,128)S(1)}, u32[]{:S(2)}, u32[]{:S(2)}) async-start(f32[16,2,128]{2,1,0:T(2,128)} %shard_map.44.token_potential), calls=%async_computation.6 | async-start | bytes 32768 | tf_op jit(solution)/shard_map/all_to_all | solution.py:235
Sparse Core Ops, SparseCore 0:
  10.4 63.1 all-gather.1

commit v10 on v6

--- a/solution.py
+++ b/solution.py
@@ -18,6 +18,7 @@
 CHUNK = 1024
 DOT_CHUNK = 512
 AHEAD = 2
+CODE = ("z", "core")
 MIB = 1 << 20
 
 score_scale = sharpness_factor * math.log2(math.e)
@@ -47,11 +48,6 @@
     most = jnp.max(top, axis=0, keepdims=True)
     total = jnp.sum(total * jnp.exp2(top - most), axis=0, keepdims=True)
     return most + jnp.log2(total)
-
-
-def send_copies(local, out):
-    for d in range(out.shape[0]):
-        out[d] = local[...]
 
 
 def send_copies(local, out):
@@ -246,7 +242,7 @@
 
 
 def per_device(tokens, codebook):
-    tok_size, code_size = lax.axis_size("tok"), lax.axis_size("code")
+    tok_size, code_size = lax.axis_size("tok"), lax.axis_size(CODE)
     tok_rows, depth = tokens.shape
     code_rows = codebook.shape[0]
     total_tokens = tok_rows * tok_size
@@ -263,6 +259,12 @@
 
     def exchange(copies, axis):
         return lax.all_to_all(copies, axis, 0, 0)
+
+    part_rows = tok_rows // lax.axis_size("core")
+    own_part = lax.dynamic_slice_in_dim(
+        tokens, lax.axis_index("core") * part_rows, part_rows, 0
+    )
+    all_tokens = lax.all_gather(own_part, ("tok", "core"), axis=0, tiled=True)
 
     scores, copies = call(
         scores_kernel,
@@ -278,8 +280,6 @@
         elements=elements,
         flops=2 * elements * depth,
     )(in_hbm(tokens), in_hbm(codebook))
-    copies, own_tokens = lax.optimization_barrier((copies, tokens))
-    all_tokens = lax.all_gather(own_tokens, "tok", axis=0, tiled=True)
     for step in range(ITERS):
         last = step == ITERS - 1
         potential = pltpu.VMEM((code_tiles, LANES), f32)
@@ -290,7 +290,7 @@
             specs=[vmem, vmem],
             elements=elements,
         )(exchange(copies, "tok"), in_vmem(scores))
-        received = exchange(copies, "code")
+        received = exchange(copies, CODE)
         if not last:
             copies = call(
                 functools.partial(columns_kernel, math.log2(total_tokens)),
@@ -341,10 +341,14 @@
 
 
 def solution(mesh):
+    tok_size, code_size = mesh.devices.shape
+    split = jax.sharding.Mesh(
+        mesh.devices.reshape(tok_size, code_size // 2, 2), ("tok",) + CODE
+    )
     return jax.shard_map(
         per_device,
-        mesh=mesh,
-        in_specs=(P("tok", None), P("code", None)),
-        out_specs=(P("tok", "code"), P(("code", "tok"), None)),
+        mesh=split,
+        in_specs=(P("tok", None), P(CODE, None)),
+        out_specs=(P("tok", CODE), P(CODE + ("tok",), None)),
         check_vma=False,
     )

time: 127 us -> 124 us (0.976)
  local copies, waits for them, and re-layouts: 4.32 us -> 1.58 us
    unnamed x4 -> x2, local copies, waits for them, and re-layouts: 4.32 us -> 0.01 us
    dynamic_slice x0 -> x1, local copies, waits for them, and re-layouts: none -> 1.57 us  [per_device(): lax.dynamic_slice_in_dim(tokens, lax.axis_index('core') * part_rows, part...]
  transfers between devices with their start and end apart: 2 -> 2, of which waited for: 1 -> 1; matrix products, arithmetic and copies ran while one was open for 0% -> 0% of each run, Pallas kernels for 10% -> 13%
where the time goes in v10:
time: 124 us; the launch traced here: 123 us
  blocking collectives  80.2 us (65%)
  Pallas kernels  21.5 us (17%)
  between operations  14.1 us (11%)
  starting transfers between devices  3.51 us (3%)
  waiting for transfers between devices  2.4 us (2%)
  local copies, waits for them, and re-layouts  1.58 us (1%)
    all_to_all x6, blocking collectives, exchange(): return lax.all_to_all(copies, axis, 0, 0)  80.2 us
    pallas_call x1, Pallas kernels, per_device(): call(functools.partial(refresh_kernel, math.log2(total_tokens)), jax.Shap...  5.23 us
    pallas_call x3, Pallas kernels, per_device(): call(functools.partial(rows_kernel, math.log2(total_codes)), (to_code, po...  5.19 us
    pallas_call x1, Pallas kernels, per_device(): call(functools.partial(targets_kernel, math.log2(total_tokens)), jax.Shap...  3.98 us
    pallas_call x1, Pallas kernels, per_device(): call(scores_kernel, (pltpu.VMEM((tok_rows, code_rows), f32), to_tok), [pl...  3.78 us
    all_to_all x1, starting transfers between devices, exchange(): return lax.all_to_all(copies, axis, 0, 0)  3.48 us
    pallas_call x2, Pallas kernels, per_device(): call(functools.partial(columns_kernel, math.log2(total_tokens)), to_tok,...  2.73 us
  transfers between devices with their start and end apart: 2, of which 1 were waited for; matrix products, arithmetic and copies ran while one was open for 0% of the time, Pallas kernels for 13%

profile of v10, /device:TPU:1, one launch (start us, length us, event | category | flops | bytes accessed | tf_op | source)
XLA Modules:
  0.0 123.4 jit_solution(10001567353292497890)
XLA Ops:
  7.2 0.0 all-gather.2.cloned.1.call-start
  7.2 1.6 %constant_dynamic-slice_fusion = bf16[128,512]{1,0:T(8,128)(2,1)} fusion(bf16[256,512]{1,0:T(8,128)(2,1)} %tokens.1, s32[]{:T(128)S(6)} %select_n.3), kind=kLoop, calls=%fused_computation | loop fusion | bytes 262148 | tf_op jit(solution)/shard_map/dynamic_slice | solution.py:264
  8.8 0.0 all-gather.2.cloned.1.call-update
  8.8 3.8 %shard_map.41 = (f32[256,4096]{1,0:T(8,128)S(1)}, f32[16,32,128]{2,1,0:T(8,128)S(1)}) custom-call(bf16[256,512]{1,0:T(8,128)(2,1)} %tokens.1, bf16[4096,512]{1,0:T(8,128)(2,1)} %codebook.3), custom_call_target="tpu_custom_call" | custom-call | flops 1077936128 | bytes 4194304 | tf_op jit(solution)/shard_map/pallas_call | solution.py:269
  12.6 0.0 copy-start
  12.6 14.9 %all_to_all.35.received = f32[16,32,128]{2,1,0:T(8,128)S(1)} all-to-all(f32[16,32,128]{2,1,0:T(8,128)S(1)} %get-tuple-element.6), channel_id=1, replica_groups=mesh['tok'=16,'z'=8,'core'=2] {'tok'}, dimensions={0} | all-to-all | bytes 524288 | tf_op jit(solution)/shard_map/all_to_all | solution.py:261
  27.5 1.7 %shard_map.42 = f32[16,2,128]{2,1,0:T(2,128)S(1)} custom-call(f32[16,32,128]{2,1,0:T(8,128)S(1)} %all_to_all.35.received, f32[256,4096]{1,0:T(8,128)S(1)} %get-tuple-element.7.scores), custom_call_target="tpu_custom_call" | custom-call | flops 4194304 | bytes 4194304 | tf_op jit(solution)/shard_map/pallas_call | solution.py:286
  29.3 17.7 %all_to_all.36.received = f32[16,2,128]{2,1,0:T(2,128)S(1)} all-to-all(f32[16,2,128]{2,1,0:T(2,128)S(1)} %shard_map.42), channel_id=1, replica_groups=mesh['tok'=16,'z'=8,'core'=2] {'z','core'}, dimensions={0} | all-to-all | bytes 32768 | tf_op jit(solution)/shard_map/all_to_all | solution.py:261
  47.0 1.4 %shard_map.43 = f32[16,32,128]{2,1,0:T(8,128)S(1)} custom-call(f32[16,2,128]{2,1,0:T(2,128)S(1)} %all_to_all.36.received, f32[256,4096]{1,0:T(8,128)S(1)} %get-tuple-element.7.scores), custom_call_target="tpu_custom_call" | custom-call | flops 4194304 | bytes 4194304 | tf_op jit(solution)/shard_map/pallas_call | solution.py:295
  48.4 13.7 %all_to_all.37.received = f32[16,32,128]{2,1,0:T(8,128)S(1)} all-to-all(f32[16,32,128]{2,1,0:T(8,128)S(1)} %shard_map.43), channel_id=1, replica_groups=mesh['tok'=16,'z'=8,'core'=2] {'tok'}, dimensions={0} | all-to-all | bytes 524288 | tf_op jit(solution)/shard_map/all_to_all | solution.py:261
  62.1 1.7 %shard_map.44 = f32[16,2,128]{2,1,0:T(2,128)S(1)} custom-call(f32[16,32,128]{2,1,0:T(8,128)S(1)} %all_to_all.37.received, f32[256,4096]{1,0:T(8,128)S(1)} %get-tuple-element.7.scores), custom_call_target="tpu_custom_call" | custom-call | flops 4194304 | bytes 4194304 | tf_op jit(solution)/shard_map/pallas_call | solution.py:286
  63.8 11.8 %all_to_all.38.received = f32[16,2,128]{2,1,0:T(2,128)S(1)} all-to-all(f32[16,2,128]{2,1,0:T(2,128)S(1)} %shard_map.44), channel_id=1, replica_groups=mesh['tok'=16,'z'=8,'core'=2] {'z','core'}, dimensions={0} | all-to-all | bytes 32768 | tf_op jit(solution)/shard_map/all_to_all | solution.py:261
  75.6 1.4 %shard_map.45 = f32[16,32,128]{2,1,0:T(8,128)S(1)} custom-call(f32[16,2,128]{2,1,0:T(2,128)S(1)} %all_to_all.38.received, f32[256,4096]{1,0:T(8,128)S(1)} %get-tuple-element.7.scores), custom_call_target="tpu_custom_call" | custom-call | flops 4194304 | bytes 4194304 | tf_op jit(solution)/shard_map/pallas_call | solution.py:295
  77.0 11.0 %all_to_all.39.received = f32[16,32,128]{2,1,0:T(8,128)S(1)} all-to-all(f32[16,32,128]{2,1,0:T(8,128)S(1)} %shard_map.45), channel_id=1, replica_groups=mesh['tok'=16,'z'=8,'core'=2] {'tok'}, dimensions={0} | all-to-all | bytes 524288 | tf_op jit(solution)/shard_map/all_to_all | solution.py:261
  88.0 0.0 copy-done
  88.0 1.7 %shard_map.46 = (f32[16,2,128]{2,1,0:T(2,128)S(1)}, f32[32,128]{1,0:T(8,128)S(1)}) custom-call(f32[16,32,128]{2,1,0:T(8,128)S(1)} %all_to_all.39.received, f32[256,4096]{1,0:T(8,128)S(1)} %get-tuple-element.7.scores), custom_call_target="tpu_custom_call" | custom-call | flops 4194304 | bytes 4194304 | tf_op jit(solution)/shard_map/pallas_call | solution.py:286
  89.7 11.0 %all_to_all.40.received = f32[16,2,128]{2,1,0:T(2,128)S(1)} all-to-all(f32[16,2,128]{2,1,0:T(2,128)S(1)} %get-tuple-element.8), channel_id=1, replica_groups=mesh['tok'=16,'z'=8,'core'=2] {'z','core'}, dimensions={0} | all-to-all | bytes 32768 | tf_op jit(solution)/shard_map/all_to_all | solution.py:261
  100.8 0.6 shard_map.47.token_potential
  101.4 3.5 %all-to-all-start.6 = ((f32[16,2,128]{2,1,0:T(2,128)}), f32[16,2,128]{2,1,0:T(2,128)S(1)}, u32[]{:S(2)}, u32[]{:S(2)}) async-start(f32[16,2,128]{2,1,0:T(2,128)} %shard_map.47.token_potential), calls=%async_computation.6 | async-start | bytes 32768 | tf_op jit(solution)/shard_map/all_to_all | solution.py:261
  104.9 4.0 %shard_map.48 = bf16[256,4096]{1,0:T(8,128)(2,1)} custom-call(f32[16,2,128]{2,1,0:T(2,128)} %shard_map.47.token_potential, f32[32,128]{1,0:T(8,128)S(1)} %get-tuple-element.9.code_potential, f32[256,4096]{1,0:T(8,128)} %copy-done), custom_call_target="tpu_custom_call" | custom-call | flops 4194304 | bytes 4194304 | tf_op jit(solution)/shard_map/pallas_call | solution.py:311
  108.9 2.4 %all-to-all-done.6.potential = f32[16,2,128]{2,1,0:T(2,128)S(1)} async-done(((f32[16,2,128]{2,1,0:T(2,128)}), f32[16,2,128]{2,1,0:T(2,128)S(1)}, u32[]{:S(2)}, u32[]{:S(2)}) %all-to-all-start.6) | async-done | bytes 16416 | tf_op jit(solution)/shard_map/all_to_all | solution.py:261
  111.3 0.0 all-gather.2.cloned.1.call-done.tokens
  111.3 5.2 %shard_map.49 = f32[256,512]{1,0:T(8,128)} custom-call(f32[32,128]{1,0:T(8,128)S(1)} %get-tuple-element.9.code_potential, f32[16,2,128]{2,1,0:T(2,128)S(1)} %all-to-all-done.6.potential, bf16[4096,512]{1,0:T(8,128)(2,1)} %codebook.3, bf16[4096,512]{1,0:T(8,128)(2,1)} %all-gather.2.cloned.1.call-done.tokens), custom_call_target="tpu_custom_call" | custom-call | flops 2151677952 | bytes 4194304 | tf_op jit(solution)/shard_map/pallas_call | solution.py:325
Async XLA Ops:
  7.2 104.1 %all-gather.2.cloned.1.call-start = ((), (), s32[]{:S(2)}) async-start(), calls=%async_computation.7 | async-start | bytes 4325376 | tf_op jit(solution)/shard_map/all_gather | solution.py:267
  12.6 75.4 %copy-start = (f32[256,4096]{1,0:T(8,128)}, f32[256,4096]{1,0:T(8,128)S(1)}, u32[]{:S(2)}) copy-start(f32[256,4096]{1,0:T(8,128)S(1)} %get-tuple-element.7.scores) | copy-start | bytes 12582916
  101.4 9.9 %all-to-all-start.6 = ((f32[16,2,128]{2,1,0:T(2,128)}), f32[16,2,128]{2,1,0:T(2,128)S(1)}, u32[]{:S(2)}, u32[]{:S(2)}) async-start(f32[16,2,128]{2,1,0:T(2,128)} %shard_map.47.token_potential), calls=%async_computation.6 | async-start | bytes 32768 | tf_op jit(solution)/shard_map/all_to_all | solution.py:261
Sparse Core Ops, SparseCore 0:
  11.1 57.8 all-gather.1

commit v11 on v6

--- a/solution.py
+++ b/solution.py
@@ -47,11 +47,6 @@
     most = jnp.max(top, axis=0, keepdims=True)
     total = jnp.sum(total * jnp.exp2(top - most), axis=0, keepdims=True)
     return most + jnp.log2(total)
-
-
-def send_copies(local, out):
-    for d in range(out.shape[0]):
-        out[d] = local[...]
 
 
 def send_copies(local, out):
@@ -264,6 +259,8 @@
     def exchange(copies, axis):
         return lax.all_to_all(copies, axis, 0, 0)
 
+    all_tokens = lax.all_gather(tokens, "tok", axis=0, tiled=True)
+
     scores, copies = call(
         scores_kernel,
         (pltpu.VMEM((tok_rows, code_rows), f32), to_tok),
@@ -278,8 +275,6 @@
         elements=elements,
         flops=2 * elements * depth,
     )(in_hbm(tokens), in_hbm(codebook))
-    copies, own_tokens = lax.optimization_barrier((copies, tokens))
-    all_tokens = lax.all_gather(own_tokens, "tok", axis=0, tiled=True)
     for step in range(ITERS):
         last = step == ITERS - 1
         potential = pltpu.VMEM((code_tiles, LANES), f32)

time: 127 us -> 123 us (0.969)
  local copies, waits for them, and re-layouts: 4.32 us -> 0.01 us
    unnamed x4 -> x2, local copies, waits for them, and re-layouts: 4.32 us -> 0.01 us
  transfers between devices with their start and end apart: 2 -> 2, of which waited for: 1 -> 1; matrix products, arithmetic and copies ran while one was open for 0% -> 0% of each run, Pallas kernels for 10% -> 13%
where the time goes in v11:
time: 123 us; the launch traced here: 122 us
  blocking collectives  80 us (65%)
  Pallas kernels  21.6 us (18%)
  between operations  14.1 us (11%)
  starting transfers between devices  3.53 us (3%)
  waiting for transfers between devices  3.06 us (2%)
    all_to_all x6, blocking collectives, exchange(): return lax.all_to_all(copies, axis, 0, 0)  80 us
    pallas_call x1, Pallas kernels, per_device(): call(functools.partial(refresh_kernel, math.log2(total_tokens)), jax.Shap...  5.23 us
    pallas_call x3, Pallas kernels, per_device(): call(functools.partial(rows_kernel, math.log2(total_codes)), (to_code, po...  5.19 us
    pallas_call x1, Pallas kernels, per_device(): call(functools.partial(targets_kernel, math.log2(total_tokens)), jax.Shap...  3.98 us
    pallas_call x1, Pallas kernels, per_device(): call(scores_kernel, (pltpu.VMEM((tok_rows, code_rows), f32), to_tok), [pl...  3.78 us
    all_to_all x1, starting transfers between devices, exchange(): return lax.all_to_all(copies, axis, 0, 0)  3.49 us
    pallas_call x2, Pallas kernels, per_device(): call(functools.partial(columns_kernel, math.log2(total_tokens)), to_tok,...  2.73 us
  transfers between devices with their start and end apart: 2, of which 1 were waited for; matrix products, arithmetic and copies ran while one was open for 0% of the time, Pallas kernels for 13%

profile of v11, /device:TPU:1, one launch (start us, length us, event | category | flops | bytes accessed | tf_op | source)
XLA Modules:
  0.0 122.3 jit_solution(16787296507799548347)
XLA Ops:
  7.2 0.0 all-gather.2.cloned.1.call-start
  7.2 0.7 all-gather.2.cloned.1.call-update
  7.9 3.8 %shard_map.41 = (f32[256,4096]{1,0:T(8,128)S(1)}, f32[16,32,128]{2,1,0:T(8,128)S(1)}) custom-call(bf16[256,512]{1,0:T(8,128)(2,1)} %tokens.1, bf16[4096,512]{1,0:T(8,128)(2,1)} %codebook.3), custom_call_target="tpu_custom_call" | custom-call | flops 1077936128 | bytes 4194304 | tf_op jit(solution)/shard_map/pallas_call | solution.py:264
  11.7 0.0 copy-start
  11.7 14.9 %all_to_all.35.received = f32[16,32,128]{2,1,0:T(8,128)S(1)} all-to-all(f32[16,32,128]{2,1,0:T(8,128)S(1)} %get-tuple-element.6), channel_id=1, replica_groups=mesh['tok'=16,'code'=16] {'tok'}, dimensions={0} | all-to-all | bytes 524288 | tf_op jit(solution)/shard_map/all_to_all | solution.py:260
  26.6 1.7 %shard_map.42 = f32[16,2,128]{2,1,0:T(2,128)S(1)} custom-call(f32[16,32,128]{2,1,0:T(8,128)S(1)} %all_to_all.35.received, f32[256,4096]{1,0:T(8,128)S(1)} %get-tuple-element.7.scores), custom_call_target="tpu_custom_call" | custom-call | flops 4194304 | bytes 4194304 | tf_op jit(solution)/shard_map/pallas_call | solution.py:281
  28.4 17.7 %all_to_all.36.received = f32[16,2,128]{2,1,0:T(2,128)S(1)} all-to-all(f32[16,2,128]{2,1,0:T(2,128)S(1)} %shard_map.42), channel_id=1, replica_groups=mesh['tok'=16,'code'=16] {'code'}, dimensions={0} | all-to-all | bytes 32768 | tf_op jit(solution)/shard_map/all_to_all | solution.py:260
  46.1 1.4 %shard_map.43 = f32[16,32,128]{2,1,0:T(8,128)S(1)} custom-call(f32[16,2,128]{2,1,0:T(2,128)S(1)} %all_to_all.36.received, f32[256,4096]{1,0:T(8,128)S(1)} %get-tuple-element.7.scores), custom_call_target="tpu_custom_call" | custom-call | flops 4194304 | bytes 4194304 | tf_op jit(solution)/shard_map/pallas_call | solution.py:290
  47.4 13.8 %all_to_all.37.received = f32[16,32,128]{2,1,0:T(8,128)S(1)} all-to-all(f32[16,32,128]{2,1,0:T(8,128)S(1)} %shard_map.43), channel_id=1, replica_groups=mesh['tok'=16,'code'=16] {'tok'}, dimensions={0} | all-to-all | bytes 524288 | tf_op jit(solution)/shard_map/all_to_all | solution.py:260
  61.3 1.7 %shard_map.44 = f32[16,2,128]{2,1,0:T(2,128)S(1)} custom-call(f32[16,32,128]{2,1,0:T(8,128)S(1)} %all_to_all.37.received, f32[256,4096]{1,0:T(8,128)S(1)} %get-tuple-element.7.scores), custom_call_target="tpu_custom_call" | custom-call | flops 4194304 | bytes 4194304 | tf_op jit(solution)/shard_map/pallas_call | solution.py:281
  63.0 11.5 %all_to_all.38.received = f32[16,2,128]{2,1,0:T(2,128)S(1)} all-to-all(f32[16,2,128]{2,1,0:T(2,128)S(1)} %shard_map.44), channel_id=1, replica_groups=mesh['tok'=16,'code'=16] {'code'}, dimensions={0} | all-to-all | bytes 32768 | tf_op jit(solution)/shard_map/all_to_all | solution.py:260
  74.6 1.4 %shard_map.45 = f32[16,32,128]{2,1,0:T(8,128)S(1)} custom-call(f32[16,2,128]{2,1,0:T(2,128)S(1)} %all_to_all.38.received, f32[256,4096]{1,0:T(8,128)S(1)} %get-tuple-element.7.scores), custom_call_target="tpu_custom_call" | custom-call | flops 4194304 | bytes 4194304 | tf_op jit(solution)/shard_map/pallas_call | solution.py:290
  75.9 10.9 %all_to_all.39.received = f32[16,32,128]{2,1,0:T(8,128)S(1)} all-to-all(f32[16,32,128]{2,1,0:T(8,128)S(1)} %shard_map.45), channel_id=1, replica_groups=mesh['tok'=16,'code'=16] {'tok'}, dimensions={0} | all-to-all | bytes 524288 | tf_op jit(solution)/shard_map/all_to_all | solution.py:260
  86.9 0.0 copy-done
  86.9 1.7 %shard_map.46 = (f32[16,2,128]{2,1,0:T(2,128)S(1)}, f32[32,128]{1,0:T(8,128)S(1)}) custom-call(f32[16,32,128]{2,1,0:T(8,128)S(1)} %all_to_all.39.received, f32[256,4096]{1,0:T(8,128)S(1)} %get-tuple-element.7.scores), custom_call_target="tpu_custom_call" | custom-call | flops 4194304 | bytes 4194304 | tf_op jit(solution)/shard_map/pallas_call | solution.py:281
  88.6 11.1 %all_to_all.40.received = f32[16,2,128]{2,1,0:T(2,128)S(1)} all-to-all(f32[16,2,128]{2,1,0:T(2,128)S(1)} %get-tuple-element.8), channel_id=1, replica_groups=mesh['tok'=16,'code'=16] {'code'}, dimensions={0} | all-to-all | bytes 32768 | tf_op jit(solution)/shard_map/all_to_all | solution.py:260
  99.7 0.7 shard_map.47.token_potential
  100.3 3.5 %all-to-all-start.6 = ((f32[16,2,128]{2,1,0:T(2,128)}), f32[16,2,128]{2,1,0:T(2,128)S(1)}, u32[]{:S(2)}, u32[]{:S(2)}) async-start(f32[16,2,128]{2,1,0:T(2,128)} %shard_map.47.token_potential), calls=%async_computation.6 | async-start | bytes 32768 | tf_op jit(solution)/shard_map/all_to_all | solution.py:260
  103.8 4.0 %shard_map.48 = bf16[256,4096]{1,0:T(8,128)(2,1)} custom-call(f32[16,2,128]{2,1,0:T(2,128)} %shard_map.47.token_potential, f32[32,128]{1,0:T(8,128)S(1)} %get-tuple-element.9.code_potential, f32[256,4096]{1,0:T(8,128)} %copy-done), custom_call_target="tpu_custom_call" | custom-call | flops 4194304 | bytes 4194304 | tf_op jit(solution)/shard_map/pallas_call | solution.py:306
  107.8 2.4 %all-to-all-done.6.potential = f32[16,2,128]{2,1,0:T(2,128)S(1)} async-done(((f32[16,2,128]{2,1,0:T(2,128)}), f32[16,2,128]{2,1,0:T(2,128)S(1)}, u32[]{:S(2)}, u32[]{:S(2)}) %all-to-all-start.6) | async-done | bytes 16416 | tf_op jit(solution)/shard_map/all_to_all | solution.py:260
  110.2 0.0 all-gather.2.cloned.1.call-done.tokens
  110.2 5.2 %shard_map.49 = f32[256,512]{1,0:T(8,128)} custom-call(f32[32,128]{1,0:T(8,128)S(1)} %get-tuple-element.9.code_potential, f32[16,2,128]{2,1,0:T(2,128)S(1)} %all-to-all-done.6.potential, bf16[4096,512]{1,0:T(8,128)(2,1)} %codebook.3, bf16[4096,512]{1,0:T(8,128)(2,1)} %all-gather.2.cloned.1.call-done.tokens), custom_call_target="tpu_custom_call" | custom-call | flops 2151677952 | bytes 4194304 | tf_op jit(solution)/shard_map/pallas_call | solution.py:320
Async XLA Ops:
  7.2 103.1 %all-gather.2.cloned.1.call-start = ((), (), s32[]{:S(2)}) async-start(), calls=%async_computation.7 | async-start | bytes 4456448 | tf_op jit(solution)/shard_map/all_gather | solution.py:262
  11.7 75.2 %copy-start = (f32[256,4096]{1,0:T(8,128)}, f32[256,4096]{1,0:T(8,128)S(1)}, u32[]{:S(2)}) copy-start(f32[256,4096]{1,0:T(8,128)S(1)} %get-tuple-element.7.scores) | copy-start | bytes 12582916
  100.3 9.9 %all-to-all-start.6 = ((f32[16,2,128]{2,1,0:T(2,128)}), f32[16,2,128]{2,1,0:T(2,128)S(1)}, u32[]{:S(2)}, u32[]{:S(2)}) async-start(f32[16,2,128]{2,1,0:T(2,128)} %shard_map.47.token_potential), calls=%async_computation.6 | async-start | bytes 32768 | tf_op jit(solution)/shard_map/all_to_all | solution.py:260
Sparse Core Ops, SparseCore 0:
  10.4 63.1 all-gather.1

commit v12 on v10

--- a/solution.py
+++ b/solution.py
@@ -18,7 +18,7 @@
 CHUNK = 1024
 DOT_CHUNK = 512
 AHEAD = 2
-CODE = ("z", "core")
+CODE = ("za", "zb", "core")
 MIB = 1 << 20
 
 score_scale = sharpness_factor * math.log2(math.e)
@@ -260,11 +260,13 @@
     def exchange(copies, axis):
         return lax.all_to_all(copies, axis, 0, 0)
 
-    part_rows = tok_rows // lax.axis_size("core")
+    sharing = ('za', 'core')
+    parts = lax.axis_size(sharing)
+    part_rows = tok_rows // parts
     own_part = lax.dynamic_slice_in_dim(
-        tokens, lax.axis_index("core") * part_rows, part_rows, 0
-    )
-    all_tokens = lax.all_gather(own_part, ("tok", "core"), axis=0, tiled=True)
+        tokens, lax.axis_index(sharing) * part_rows, part_rows, 0
+    )
+    all_tokens = lax.all_gather(own_part, ("tok",) + sharing, axis=0, tiled=True)
 
     scores, copies = call(
         scores_kernel,
@@ -343,7 +345,7 @@
 def solution(mesh):
     tok_size, code_size = mesh.devices.shape
     split = jax.sharding.Mesh(
-        mesh.devices.reshape(tok_size, code_size // 2, 2), ("tok",) + CODE
+        mesh.devices.reshape(tok_size, code_size // 4, 2, 2), ("tok",) + CODE
     )
     return jax.shard_map(
         per_device,

time: 124 us -> 122 us (0.984)
  blocking collectives: 80.2 us -> 78.3 us
    all_to_all x6, blocking collectives: 80.2 us -> 78.3 us  [exchange(): return lax.all_to_all(copies, axis, 0, 0)]
where the time goes in v12:
time: 122 us; the launch traced here: 121 us
  blocking collectives  78.3 us (64%)
  Pallas kernels  21.6 us (18%)
  between operations  14.1 us (12%)
  starting transfers between devices  3.51 us (3%)
  waiting for transfers between devices  2.4 us (2%)
  local copies, waits for them, and re-layouts  1.38 us (1%)
    all_to_all x6, blocking collectives, exchange(): return lax.all_to_all(copies, axis, 0, 0)  78.3 us
    pallas_call x1, Pallas kernels, per_device(): call(functools.partial(refresh_kernel, math.log2(total_tokens)), jax.Shap...  5.23 us
    pallas_call x3, Pallas kernels, per_device(): call(functools.partial(rows_kernel, math.log2(total_codes)), (to_code, po...  5.19 us
    pallas_call x1, Pallas kernels, per_device(): call(functools.partial(targets_kernel, math.log2(total_tokens)), jax.Shap...  3.98 us
    pallas_call x1, Pallas kernels, per_device(): call(scores_kernel, (pltpu.VMEM((tok_rows, code_rows), f32), to_tok), [pl...  3.78 us
    all_to_all x1, starting transfers between devices, exchange(): return lax.all_to_all(copies, axis, 0, 0)  3.48 us
    pallas_call x2, Pallas kernels, per_device(): call(functools.partial(columns_kernel, math.log2(total_tokens)), to_tok,...  2.73 us
  transfers between devices with their start and end apart: 2, of which 1 were waited for; matrix products, arithmetic and copies ran while one was open for 0% of the time, Pallas kernels for 13%

profile of v12, /device:TPU:1, one launch (start us, length us, event | category | flops | bytes accessed | tf_op | source)
XLA Modules:
  0.0 121.3 jit_solution(3212582567542044217)
XLA Ops:
  7.2 0.0 all-gather.2.cloned.1.call-start
  7.2 1.4 %constant_dynamic-slice_fusion = bf16[32,512]{1,0:T(8,128)(2,1)} fusion(bf16[256,512]{1,0:T(8,128)(2,1)} %tokens.1, s32[]{:T(128)S(6)} %select_n.3), kind=kLoop, calls=%fused_computation | loop fusion | bytes 65540 | tf_op jit(solution)/shard_map/dynamic_slice | solution.py:266
  8.6 0.0 all-gather.2.cloned.1.call-update
  8.6 3.8 %shard_map.41 = (f32[256,4096]{1,0:T(8,128)S(1)}, f32[16,32,128]{2,1,0:T(8,128)S(1)}) custom-call(bf16[256,512]{1,0:T(8,128)(2,1)} %tokens.1, bf16[4096,512]{1,0:T(8,128)(2,1)} %codebook.3), custom_call_target="tpu_custom_call" | custom-call | flops 1077936128 | bytes 4194304 | tf_op jit(solution)/shard_map/pallas_call | solution.py:271
  12.4 0.0 copy-start
  12.4 14.9 %all_to_all.35.received = f32[16,32,128]{2,1,0:T(8,128)S(1)} all-to-all(f32[16,32,128]{2,1,0:T(8,128)S(1)} %get-tuple-element.6), channel_id=1, replica_groups=mesh['tok'=16,'za'=4,'zb'=2,'core'=2] {'tok'}, dimensions={0} | all-to-all | bytes 524288 | tf_op jit(solution)/shard_map/all_to_all | solution.py:261
  27.3 1.7 %shard_map.42 = f32[16,2,128]{2,1,0:T(2,128)S(1)} custom-call(f32[16,32,128]{2,1,0:T(8,128)S(1)} %all_to_all.35.received, f32[256,4096]{1,0:T(8,128)S(1)} %get-tuple-element.7.scores), custom_call_target="tpu_custom_call" | custom-call | flops 4194304 | bytes 4194304 | tf_op jit(solution)/shard_map/pallas_call | solution.py:288
  29.1 17.7 %all_to_all.36.received = f32[16,2,128]{2,1,0:T(2,128)S(1)} all-to-all(f32[16,2,128]{2,1,0:T(2,128)S(1)} %shard_map.42), channel_id=1, replica_groups=mesh['tok'=16,'za'=4,'zb'=2,'core'=2] {'za','zb','core'}, dimensions={0} | all-to-all | bytes 32768 | tf_op jit(solution)/shard_map/all_to_all | solution.py:261
  46.8 1.4 %shard_map.43 = f32[16,32,128]{2,1,0:T(8,128)S(1)} custom-call(f32[16,2,128]{2,1,0:T(2,128)S(1)} %all_to_all.36.received, f32[256,4096]{1,0:T(8,128)S(1)} %get-tuple-element.7.scores), custom_call_target="tpu_custom_call" | custom-call | flops 4194304 | bytes 4194304 | tf_op jit(solution)/shard_map/pallas_call | solution.py:297
  48.2 11.3 %all_to_all.37.received = f32[16,32,128]{2,1,0:T(8,128)S(1)} all-to-all(f32[16,32,128]{2,1,0:T(8,128)S(1)} %shard_map.43), channel_id=1, replica_groups=mesh['tok'=16,'za'=4,'zb'=2,'core'=2] {'tok'}, dimensions={0} | all-to-all | bytes 524288 | tf_op jit(solution)/shard_map/all_to_all | solution.py:261
  59.4 1.7 %shard_map.44 = f32[16,2,128]{2,1,0:T(2,128)S(1)} custom-call(f32[16,32,128]{2,1,0:T(8,128)S(1)} %all_to_all.37.received, f32[256,4096]{1,0:T(8,128)S(1)} %get-tuple-element.7.scores), custom_call_target="tpu_custom_call" | custom-call | flops 4194304 | bytes 4194304 | tf_op jit(solution)/shard_map/pallas_call | solution.py:288
  61.2 11.2 %all_to_all.38.received = f32[16,2,128]{2,1,0:T(2,128)S(1)} all-to-all(f32[16,2,128]{2,1,0:T(2,128)S(1)} %shard_map.44), channel_id=1, replica_groups=mesh['tok'=16,'za'=4,'zb'=2,'core'=2] {'za','zb','core'}, dimensions={0} | all-to-all | bytes 32768 | tf_op jit(solution)/shard_map/all_to_all | solution.py:261
  72.4 1.4 %shard_map.45 = f32[16,32,128]{2,1,0:T(8,128)S(1)} custom-call(f32[16,2,128]{2,1,0:T(2,128)S(1)} %all_to_all.38.received, f32[256,4096]{1,0:T(8,128)S(1)} %get-tuple-element.7.scores), custom_call_target="tpu_custom_call" | custom-call | flops 4194304 | bytes 4194304 | tf_op jit(solution)/shard_map/pallas_call | solution.py:297
  73.8 11.6 %all_to_all.39.received = f32[16,32,128]{2,1,0:T(8,128)S(1)} all-to-all(f32[16,32,128]{2,1,0:T(8,128)S(1)} %shard_map.45), channel_id=1, replica_groups=mesh['tok'=16,'za'=4,'zb'=2,'core'=2] {'tok'}, dimensions={0} | all-to-all | bytes 524288 | tf_op jit(solution)/shard_map/all_to_all | solution.py:261
  85.4 0.0 copy-done
  85.4 1.7 %shard_map.46 = (f32[16,2,128]{2,1,0:T(2,128)S(1)}, f32[32,128]{1,0:T(8,128)S(1)}) custom-call(f32[16,32,128]{2,1,0:T(8,128)S(1)} %all_to_all.39.received, f32[256,4096]{1,0:T(8,128)S(1)} %get-tuple-element.7.scores), custom_call_target="tpu_custom_call" | custom-call | flops 4194304 | bytes 4194304 | tf_op jit(solution)/shard_map/pallas_call | solution.py:288
  87.1 11.6 %all_to_all.40.received = f32[16,2,128]{2,1,0:T(2,128)S(1)} all-to-all(f32[16,2,128]{2,1,0:T(2,128)S(1)} %get-tuple-element.8), channel_id=1, replica_groups=mesh['tok'=16,'za'=4,'zb'=2,'core'=2] {'za','zb','core'}, dimensions={0} | all-to-all | bytes 32768 | tf_op jit(solution)/shard_map/all_to_all | solution.py:261
  98.7 0.6 shard_map.47.token_potential
  99.3 3.5 %all-to-all-start.6 = ((f32[16,2,128]{2,1,0:T(2,128)}), f32[16,2,128]{2,1,0:T(2,128)S(1)}, u32[]{:S(2)}, u32[]{:S(2)}) async-start(f32[16,2,128]{2,1,0:T(2,128)} %shard_map.47.token_potential), calls=%async_computation.6 | async-start | bytes 32768 | tf_op jit(solution)/shard_map/all_to_all | solution.py:261
  102.8 4.0 %shard_map.48 = bf16[256,4096]{1,0:T(8,128)(2,1)} custom-call(f32[16,2,128]{2,1,0:T(2,128)} %shard_map.47.token_potential, f32[32,128]{1,0:T(8,128)S(1)} %get-tuple-element.9.code_potential, f32[256,4096]{1,0:T(8,128)} %copy-done), custom_call_target="tpu_custom_call" | custom-call | flops 4194304 | bytes 4194304 | tf_op jit(solution)/shard_map/pallas_call | solution.py:313
  106.8 2.4 %all-to-all-done.6.potential = f32[16,2,128]{2,1,0:T(2,128)S(1)} async-done(((f32[16,2,128]{2,1,0:T(2,128)}), f32[16,2,128]{2,1,0:T(2,128)S(1)}, u32[]{:S(2)}, u32[]{:S(2)}) %all-to-all-start.6) | async-done | bytes 16416 | tf_op jit(solution)/shard_map/all_to_all | solution.py:261
  109.2 0.0 all-gather.2.cloned.1.call-done.tokens
  109.2 5.2 %shard_map.49 = f32[256,512]{1,0:T(8,128)} custom-call(f32[32,128]{1,0:T(8,128)S(1)} %get-tuple-element.9.code_potential, f32[16,2,128]{2,1,0:T(2,128)S(1)} %all-to-all-done.6.potential, bf16[4096,512]{1,0:T(8,128)(2,1)} %codebook.3, bf16[4096,512]{1,0:T(8,128)(2,1)} %all-gather.2.cloned.1.call-done.tokens), custom_call_target="tpu_custom_call" | custom-call | flops 2151677952 | bytes 4194304 | tf_op jit(solution)/shard_map/pallas_call | solution.py:327
Async XLA Ops:
  7.2 102.0 %all-gather.2.cloned.1.call-start = ((), (), s32[]{:S(2)}) async-start(), calls=%async_computation.7 | async-start | bytes 4227072 | tf_op jit(solution)/shard_map/all_gather | solution.py:269
  12.4 73.0 %copy-start = (f32[256,4096]{1,0:T(8,128)}, f32[256,4096]{1,0:T(8,128)S(1)}, u32[]{:S(2)}) copy-start(f32[256,4096]{1,0:T(8,128)S(1)} %get-tuple-element.7.scores) | copy-start | bytes 12582916
  99.3 9.9 %all-to-all-start.6 = ((f32[16,2,128]{2,1,0:T(2,128)}), f32[16,2,128]{2,1,0:T(2,128)S(1)}, u32[]{:S(2)}, u32[]{:S(2)}) async-start(f32[16,2,128]{2,1,0:T(2,128)} %shard_map.47.token_potential), calls=%async_computation.6 | async-start | bytes 32768 | tf_op jit(solution)/shard_map/all_to_all | solution.py:261
Sparse Core Ops, SparseCore 0:
  12.2 83.7 all-gather.1

commit v13 on v12

--- a/solution.py
+++ b/solution.py
@@ -159,6 +159,14 @@
         copy.wait()
 
 
+def part_kernel(sharing, tokens, out, sem):
+    rows = out.shape[0]
+    start = pl.multiple_of(lax.axis_index(sharing) * rows, rows)
+    copy = pltpu.make_async_copy(tokens.at[pl.ds(start, rows)], out, sem)
+    copy.start()
+    copy.wait()
+
+
 def own_code_copy(codebook, codes, sem):
     share = codes.shape[0]
     start = pl.multiple_of(lax.axis_index("tok") * share, share)
@@ -263,9 +271,13 @@
     sharing = ('za', 'core')
     parts = lax.axis_size(sharing)
     part_rows = tok_rows // parts
-    own_part = lax.dynamic_slice_in_dim(
-        tokens, lax.axis_index(sharing) * part_rows, part_rows, 0
-    )
+    own_part = call(
+        functools.partial(part_kernel, sharing),
+        pltpu.HBM((part_rows, depth), tokens.dtype),
+        [pltpu.SemaphoreType.DMA],
+        specs=[hbm],
+        out_specs=hbm,
+    )(in_hbm(tokens))
     all_tokens = lax.all_gather(own_part, ("tok",) + sharing, axis=0, tiled=True)
 
     scores, copies = call(

time: 122 us -> 123 us (level)
  Pallas kernels: 21.6 us -> 23.7 us
  local copies, waits for them, and re-layouts: 1.38 us -> 0.01 us
    pallas_call x0 -> x1, Pallas kernels: none -> 2.11 us  [per_device(): call(functools.partial(part_kernel, sharing), pltpu.HBM((part_rows, depth...]
    dynamic_slice x1 -> x0, local copies, waits for them, and re-layouts: 1.38 us -> none  [per_device(): lax.dynamic_slice_in_dim(tokens, lax.axis_index(sharing) * part_rows, par...]
where the time goes in v13:
time: 123 us; the launch traced here: 122 us
  blocking collectives  78.6 us (64%)
  Pallas kernels  23.7 us (19%)
  between operations  14.1 us (11%)
  starting transfers between devices  3.51 us (3%)
  waiting for transfers between devices  2.4 us (2%)
    all_to_all x6, blocking collectives, exchange(): return lax.all_to_all(copies, axis, 0, 0)  78.6 us
    pallas_call x1, Pallas kernels, per_device(): call(functools.partial(refresh_kernel, math.log2(total_tokens)), jax.Shap...  5.23 us
    pallas_call x3, Pallas kernels, per_device(): call(functools.partial(rows_kernel, math.log2(total_codes)), (to_code, po...  5.19 us
    pallas_call x1, Pallas kernels, per_device(): call(functools.partial(targets_kernel, math.log2(total_tokens)), jax.Shap...  3.98 us
    pallas_call x1, Pallas kernels, per_device(): call(scores_kernel, (pltpu.VMEM((tok_rows, code_rows), f32), to_tok), [pl...  3.78 us
    all_to_all x1, starting transfers between devices, exchange(): return lax.all_to_all(copies, axis, 0, 0)  3.48 us
    pallas_call x2, Pallas kernels, per_device(): call(functools.partial(columns_kernel, math.log2(total_tokens)), to_tok,...  2.73 us
  transfers between devices with their start and end apart: 2, of which 1 were waited for; matrix products, arithmetic and copies ran while one was open for 0% of the time, Pallas kernels for 13%

profile of v13, /device:TPU:1, one launch (start us, length us, event | category | flops | bytes accessed | tf_op | source)
XLA Modules:
  0.0 122.3 jit_solution(12795133713164462744)
XLA Ops:
  7.2 0.0 all-gather.2.cloned.1.call-start
  7.2 2.1 %shard_map.49 = bf16[32,512]{1,0:T(8,128)(2,1)} custom-call(bf16[256,512]{1,0:T(8,128)(2,1)} %tokens.3), custom_call_target="tpu_custom_call" | custom-call | tf_op jit(solution)/shard_map/pallas_call | solution.py:274
  9.3 0.0 all-gather.2.cloned.1.call-update
  9.4 3.8 %shard_map.41 = (f32[256,4096]{1,0:T(8,128)S(1)}, f32[16,32,128]{2,1,0:T(8,128)S(1)}) custom-call(bf16[256,512]{1,0:T(8,128)(2,1)} %tokens.3, bf16[4096,512]{1,0:T(8,128)(2,1)} %codebook.3), custom_call_target="tpu_custom_call" | custom-call | flops 1077936128 | bytes 4194304 | tf_op jit(solution)/shard_map/pallas_call | solution.py:283
  13.1 0.0 copy-start
  13.2 14.9 %all_to_all.35.received = f32[16,32,128]{2,1,0:T(8,128)S(1)} all-to-all(f32[16,32,128]{2,1,0:T(8,128)S(1)} %get-tuple-element.6), channel_id=1, replica_groups=mesh['tok'=16,'za'=4,'zb'=2,'core'=2] {'tok'}, dimensions={0} | all-to-all | bytes 524288 | tf_op jit(solution)/shard_map/all_to_all | solution.py:269
  28.1 1.7 %shard_map.42 = f32[16,2,128]{2,1,0:T(2,128)S(1)} custom-call(f32[16,32,128]{2,1,0:T(8,128)S(1)} %all_to_all.35.received, f32[256,4096]{1,0:T(8,128)S(1)} %get-tuple-element.7.scores), custom_call_target="tpu_custom_call" | custom-call | flops 4194304 | bytes 4194304 | tf_op jit(solution)/shard_map/pallas_call | solution.py:300
  29.8 17.7 %all_to_all.36.received = f32[16,2,128]{2,1,0:T(2,128)S(1)} all-to-all(f32[16,2,128]{2,1,0:T(2,128)S(1)} %shard_map.42), channel_id=1, replica_groups=mesh['tok'=16,'za'=4,'zb'=2,'core'=2] {'za','zb','core'}, dimensions={0} | all-to-all | bytes 32768 | tf_op jit(solution)/shard_map/all_to_all | solution.py:269
  47.5 1.4 %shard_map.43 = f32[16,32,128]{2,1,0:T(8,128)S(1)} custom-call(f32[16,2,128]{2,1,0:T(2,128)S(1)} %all_to_all.36.received, f32[256,4096]{1,0:T(8,128)S(1)} %get-tuple-element.7.scores), custom_call_target="tpu_custom_call" | custom-call | flops 4194304 | bytes 4194304 | tf_op jit(solution)/shard_map/pallas_call | solution.py:309
  48.9 11.5 %all_to_all.37.received = f32[16,32,128]{2,1,0:T(8,128)S(1)} all-to-all(f32[16,32,128]{2,1,0:T(8,128)S(1)} %shard_map.43), channel_id=1, replica_groups=mesh['tok'=16,'za'=4,'zb'=2,'core'=2] {'tok'}, dimensions={0} | all-to-all | bytes 524288 | tf_op jit(solution)/shard_map/all_to_all | solution.py:269
  60.5 1.7 %shard_map.44 = f32[16,2,128]{2,1,0:T(2,128)S(1)} custom-call(f32[16,32,128]{2,1,0:T(8,128)S(1)} %all_to_all.37.received, f32[256,4096]{1,0:T(8,128)S(1)} %get-tuple-element.7.scores), custom_call_target="tpu_custom_call" | custom-call | flops 4194304 | bytes 4194304 | tf_op jit(solution)/shard_map/pallas_call | solution.py:300
  62.2 10.9 %all_to_all.38.received = f32[16,2,128]{2,1,0:T(2,128)S(1)} all-to-all(f32[16,2,128]{2,1,0:T(2,128)S(1)} %shard_map.44), channel_id=1, replica_groups=mesh['tok'=16,'za'=4,'zb'=2,'core'=2] {'za','zb','core'}, dimensions={0} | all-to-all | bytes 32768 | tf_op jit(solution)/shard_map/all_to_all | solution.py:269
  73.1 1.4 %shard_map.45 = f32[16,32,128]{2,1,0:T(8,128)S(1)} custom-call(f32[16,2,128]{2,1,0:T(2,128)S(1)} %all_to_all.38.received, f32[256,4096]{1,0:T(8,128)S(1)} %get-tuple-element.7.scores), custom_call_target="tpu_custom_call" | custom-call | flops 4194304 | bytes 4194304 | tf_op jit(solution)/shard_map/pallas_call | solution.py:309
  74.5 10.7 %all_to_all.39.received = f32[16,32,128]{2,1,0:T(8,128)S(1)} all-to-all(f32[16,32,128]{2,1,0:T(8,128)S(1)} %shard_map.45), channel_id=1, replica_groups=mesh['tok'=16,'za'=4,'zb'=2,'core'=2] {'tok'}, dimensions={0} | all-to-all | bytes 524288 | tf_op jit(solution)/shard_map/all_to_all | solution.py:269
  85.2 0.0 copy-done
  85.2 1.7 %shard_map.46 = (f32[16,2,128]{2,1,0:T(2,128)S(1)}, f32[32,128]{1,0:T(8,128)S(1)}) custom-call(f32[16,32,128]{2,1,0:T(8,128)S(1)} %all_to_all.39.received, f32[256,4096]{1,0:T(8,128)S(1)} %get-tuple-element.7.scores), custom_call_target="tpu_custom_call" | custom-call | flops 4194304 | bytes 4194304 | tf_op jit(solution)/shard_map/pallas_call | solution.py:300
  87.0 12.7 %all_to_all.40.received = f32[16,2,128]{2,1,0:T(2,128)S(1)} all-to-all(f32[16,2,128]{2,1,0:T(2,128)S(1)} %get-tuple-element.8), channel_id=1, replica_groups=mesh['tok'=16,'za'=4,'zb'=2,'core'=2] {'za','zb','core'}, dimensions={0} | all-to-all | bytes 32768 | tf_op jit(solution)/shard_map/all_to_all | solution.py:269
  99.7 0.6 shard_map.47.token_potential
  100.3 3.5 %all-to-all-start.6 = ((f32[16,2,128]{2,1,0:T(2,128)}), f32[16,2,128]{2,1,0:T(2,128)S(1)}, u32[]{:S(2)}, u32[]{:S(2)}) async-start(f32[16,2,128]{2,1,0:T(2,128)} %shard_map.47.token_potential), calls=%async_computation.6 | async-start | bytes 32768 | tf_op jit(solution)/shard_map/all_to_all | solution.py:269
  103.8 4.0 %shard_map.48 = bf16[256,4096]{1,0:T(8,128)(2,1)} custom-call(f32[16,2,128]{2,1,0:T(2,128)} %shard_map.47.token_potential, f32[32,128]{1,0:T(8,128)S(1)} %get-tuple-element.9.code_potential, f32[256,4096]{1,0:T(8,128)} %copy-done), custom_call_target="tpu_custom_call" | custom-call | flops 4194304 | bytes 4194304 | tf_op jit(solution)/shard_map/pallas_call | solution.py:325
  107.8 2.4 %all-to-all-done.6.potential = f32[16,2,128]{2,1,0:T(2,128)S(1)} async-done(((f32[16,2,128]{2,1,0:T(2,128)}), f32[16,2,128]{2,1,0:T(2,128)S(1)}, u32[]{:S(2)}, u32[]{:S(2)}) %all-to-all-start.6) | async-done | bytes 16416 | tf_op jit(solution)/shard_map/all_to_all | solution.py:269
  110.2 0.0 all-gather.2.cloned.1.call-done.tokens
  110.2 5.2 %shard_map.50 = f32[256,512]{1,0:T(8,128)} custom-call(f32[32,128]{1,0:T(8,128)S(1)} %get-tuple-element.9.code_potential, f32[16,2,128]{2,1,0:T(2,128)S(1)} %all-to-all-done.6.potential, bf16[4096,512]{1,0:T(8,128)(2,1)} %codebook.3, bf16[4096,512]{1,0:T(8,128)(2,1)} %all-gather.2.cloned.1.call-done.tokens), custom_call_target="tpu_custom_call" | custom-call | flops 2151677952 | bytes 4194304 | tf_op jit(solution)/shard_map/pallas_call | solution.py:339
Async XLA Ops:
  7.2 103.0 %all-gather.2.cloned.1.call-start = ((), (), s32[]{:S(2)}) async-start(), calls=%async_computation.7 | async-start | bytes 4227072 | tf_op jit(solution)/shard_map/all_gather | solution.py:281
  13.1 72.1 %copy-start = (f32[256,4096]{1,0:T(8,128)}, f32[256,4096]{1,0:T(8,128)S(1)}, u32[]{:S(2)}) copy-start(f32[256,4096]{1,0:T(8,128)S(1)} %get-tuple-element.7.scores) | copy-start | bytes 12582916
  100.3 9.9 %all-to-all-start.6 = ((f32[16,2,128]{2,1,0:T(2,128)}), f32[16,2,128]{2,1,0:T(2,128)S(1)}, u32[]{:S(2)}, u32[]{:S(2)}) async-start(f32[16,2,128]{2,1,0:T(2,128)} %shard_map.47.token_potential), calls=%async_computation.6 | async-start | bytes 32768 | tf_op jit(solution)/shard_map/all_to_all | solution.py:269
Sparse Core Ops, SparseCore 0:
  12.2 83.8 all-gather.1
